TPU v7x, 32 devices: a whole 2x2x4 slice. The times are simulated.
32 devices in a mesh: dp: 8 (over z, x), seq: 4 (over y, core).
Axes of the slice: x: 2, y: 2, z: 4, core: 2. Of those that a mesh axis runs over, the one named last changes fastest.
Arguments:
- inputs: bfloat16 [2, 4096, 2048], P(None, ('dp', 'seq')), may hold values from -6 to 6
- segments: int32 [2, 4096], P(None, 'dp'), may hold values from 0 to 31, never falling along the last dimension, each value on 1 to 512 neighbouring positions
- cotangent: bfloat16 [2, 4096, 2048], P(None, ('dp', 'seq')), may hold values from -6 to 6
- attn_gain: bfloat16 [2048], P(('dp', 'seq')), may hold values from 0.5 to 1.5
- w_query: bfloat16 [2048, 2048], P('dp', 'seq'), may hold values from -0.125 to 0.125
- w_key: bfloat16 [2048, 256], P('dp', 'seq'), may hold values from -0.125 to 0.125
- w_value: bfloat16 [2048, 256], P('dp', 'seq'), may hold values from -0.125 to 0.125
- w_out: bfloat16 [2048, 2048], P('dp', 'seq'), may hold values from -0.5 to 0.5
- mlp_gain: bfloat16 [2048], P(('dp', 'seq')), may hold values from 0.5 to 1.5
- w_gate: bfloat16 [2048, 5632], P('dp', 'seq'), may hold values from -0.125 to 0.125
- w_up: bfloat16 [2048, 5632], P('dp', 'seq'), may hold values from -0.125 to 0.125
- w_down: bfloat16 [2048, 5632], P('dp', 'seq'), may hold values from -0.078125 to 0.078125
Outputs:
- outputs: bfloat16 [2, 4096, 2048], P(None, ('dp', 'seq'))
- input_grad: float32 [2, 4096, 2048], P(None, ('dp', 'seq'))
- attn_gain_grad: float32 [2048], P(('dp', 'seq'))
- query_grad: float32 [2048, 2048], P('dp', 'seq')
- key_grad: float32 [2048, 256], P('dp', 'seq')
- value_grad: float32 [2048, 256], P('dp', 'seq')
- out_grad: float32 [2048, 2048], P('dp', 'seq')
- mlp_gain_grad: float32 [2048], P(('dp', 'seq'))
- gate_grad: float32 [2048, 5632], P('dp', 'seq')
- up_grad: float32 [2048, 5632], P('dp', 'seq')
- down_grad: float32 [2048, 5632], P('dp', 'seq')
Inputs may be any that keep to these rules, and one draw needn't show every extreme that they name: `segments`: segment numbers never fall along a micro-batch's tokens; a document holds 1 to 512 tokens, and one holds exactly 512.
All inputs are finite; a program needn't handle non-finite values.
Results may differ from a plain program's by a relative error of at most 0.02.
Values may be sent and summed in bfloat16 or wider, within the bound.
A program may use at most 768 MiB of HBM per device.

v0:
```python
import jax
import jax.numpy as jnp
from jax import lax
from jax.sharding import PartitionSpec as P

D = 2048
H = 32
KVH = 4
HD = 64


EPS = 1e-05
THETA = 10000.0
NEGATIVE = -1e30


def rope_tables(positions):
    half_dim = HD // 2
    frequency = THETA ** (-(jnp.arange(half_dim).astype(jnp.float32) * (2.0 / HD)))
    angles = positions.astype(jnp.float32)[:, None] * frequency[None, :]
    return (jnp.cos(angles), jnp.sin(angles))


def rotate(values, cosine, sine_table):
    half_dim = values.shape[-1] // 2
    c = cosine[:, None, :]
    s = sine_table[:, None, :]
    first_half = values[..., :half_dim]
    second = values[..., half_dim:]
    return jnp.concatenate([first_half * c - second * s, second * c + first_half * s], axis=-1)


def unrotate(gradient, cosine, sine_table):
    half_dim = gradient.shape[-1] // 2
    c = cosine[:, None, :]
    s = sine_table[:, None, :]
    first_half = gradient[..., :half_dim]
    second = gradient[..., half_dim:]
    return jnp.concatenate([first_half * c + second * s, second * c - first_half * s], axis=-1)


def rope_heads(values, head_count, cosine, sine_table):
    row_count = values.shape[0]
    turned = rotate(values.reshape(row_count, head_count, HD), cosine, sine_table)
    return turned.astype(jnp.bfloat16).reshape(row_count, head_count * HD)


def unrope_heads(gradient, head_count, cosine, sine_table):
    row_count = gradient.shape[0]
    turned = unrotate(gradient.reshape(row_count, head_count, HD), cosine, sine_table)
    return turned.astype(jnp.bfloat16).reshape(row_count, head_count * HD)


def normalize(hidden, gain_vec):
    inverse = lax.rsqrt(jnp.mean(hidden * hidden, axis=-1, keepdims=True) + EPS)
    return (hidden * inverse * gain_vec, inverse)


def normalize_back(hidden, inverse, gain_vec, gradient):
    unit_rows = hidden * inverse
    gain_grad = jnp.sum(gradient * unit_rows, axis=0)
    weighted = gradient * gain_vec
    return (
        inverse * (weighted - unit_rows * jnp.mean(weighted * unit_rows, axis=-1, keepdims=True)),
        gain_grad,
    )


def project(left_side, right_side):
    return jnp.dot(left_side, right_side, preferred_element_type=jnp.float32)


def project_back(left_side, right_side):
    return lax.dot_general(
        left_side, right_side, (((1,), (1,)), ((), ())), preferred_element_type=jnp.float32
    )


def outer_sum(left_side, right_side):
    return lax.dot_general(
        left_side, right_side, (((0,), (0,)), ((), ())), preferred_element_type=jnp.float32
    )


def split_heads(queries, keys_all, values_all):
    kv_count = keys_all.shape[1] // HD
    groups = H // KVH
    query_g = queries.reshape(queries.shape[0], kv_count, groups, HD)
    keys_g = keys_all.reshape(keys_all.shape[0], kv_count, HD)
    values_g = values_all.reshape(values_all.shape[0], kv_count, HD)
    return (query_g, keys_g, values_g)


def masked_scores(query_g, keys_g, allowed):
    scores = jnp.einsum(
        "qkgd,pkd->kgqp", query_g, keys_g, preferred_element_type=jnp.float32
    ) * HD ** (-0.5)
    return jnp.where(allowed[None, None], scores, NEGATIVE)


def attend(queries, keys_all, values_all, allowed):
    query_g, keys_g, values_g = split_heads(queries, keys_all, values_all)
    scores = masked_scores(query_g, keys_g, allowed)
    maximum = jnp.max(scores, axis=-1, keepdims=True)
    weights = jnp.where(allowed[None, None], jnp.exp(scores - maximum), 0.0)
    denominator = jnp.sum(weights, axis=-1, keepdims=True)
    log_total = maximum + jnp.log(denominator)
    probability = (weights / denominator).astype(jnp.bfloat16)
    attended = jnp.einsum(
        "kgqp,pkd->qkgd", probability, values_g, preferred_element_type=jnp.float32
    )
    return (attended.astype(jnp.bfloat16).reshape(queries.shape[0], -1), log_total)


def attend_back(queries, keys_all, values_all, allowed, log_total, d_attended):
    query_g, keys_g, values_g = split_heads(queries, keys_all, values_all)
    d_out_g = d_attended.reshape(query_g.shape)
    scores = masked_scores(query_g, keys_g, allowed)
    prob_full = jnp.where(allowed[None, None], jnp.exp(scores - log_total), 0.0)
    d_values = jnp.einsum(
        "kgqp,qkgd->pkd",
        prob_full.astype(jnp.bfloat16),
        d_out_g,
        preferred_element_type=jnp.float32,
    )
    d_prob = jnp.einsum("qkgd,pkd->kgqp", d_out_g, values_g, preferred_element_type=jnp.float32)
    row_sum = jnp.sum(prob_full * d_prob, axis=-1, keepdims=True)
    d_scores = (prob_full * (d_prob - row_sum) * HD ** (-0.5)).astype(jnp.bfloat16)
    d_query = jnp.einsum("kgqp,pkd->qkgd", d_scores, keys_g, preferred_element_type=jnp.float32)
    d_keys = jnp.einsum("kgqp,qkgd->pkd", d_scores, query_g, preferred_element_type=jnp.float32)
    key_rows = keys_all.shape[0]
    return (
        d_query.reshape(queries.shape[0], -1),
        d_keys.reshape(key_rows, -1),
        d_values.reshape(key_rows, -1),
    )


def swiglu(normed_m, weight_gate, weight_up):
    gate_pre = project(normed_m, weight_gate)
    up_proj = project(normed_m, weight_up)
    sigmoid_g = jax.nn.sigmoid(gate_pre)
    active = gate_pre * sigmoid_g
    return (gate_pre, up_proj, sigmoid_g, active, (active * up_proj).astype(jnp.bfloat16))


def swiglu_back(d_product, gate_pre, up_proj, sigmoid_g, active):
    d_gate = (d_product * up_proj * sigmoid_g * (1.0 + gate_pre * (1.0 - sigmoid_g))).astype(
        jnp.bfloat16
    )
    d_up = (d_product * active).astype(jnp.bfloat16)
    return (d_gate, d_up)


def per_device(
    inputs,
    segments,
    cotangent,
    attn_gain,
    w_query,
    w_key,
    w_value,
    w_out,
    mlp_gain,
    w_gate,
    w_up,
    w_down,
):
    local_rows = inputs.shape[1]
    seq_count = lax.axis_size("seq")
    seq_length = local_rows * seq_count
    offset = lax.axis_index("seq") * local_rows
    all_pos = jnp.arange(seq_length, dtype=jnp.int32)
    gains = (
        lax.all_gather(attn_gain, ("dp", "seq"), axis=0, tiled=True),
        lax.all_gather(mlp_gain, ("dp", "seq"), axis=0, tiled=True),
    )
    gain_a = gains[0].astype(jnp.float32)
    gain_m = gains[1].astype(jnp.float32)
    zero_gains = (jnp.zeros((D,), jnp.float32), jnp.zeros((D,), jnp.float32))
    column_parts = (
        lax.all_gather(w_query, "seq", axis=1, tiled=True),
        lax.all_gather(w_key, "seq", axis=1, tiled=True),
        lax.all_gather(w_value, "seq", axis=1, tiled=True),
        lax.all_gather(w_out, "seq", axis=1, tiled=True),
        lax.all_gather(w_gate, "seq", axis=1, tiled=True),
        lax.all_gather(w_up, "seq", axis=1, tiled=True),
        lax.all_gather(w_down, "seq", axis=1, tiled=True),
    )
    own_pos = offset + jnp.arange(local_rows, dtype=jnp.int32)
    cosine, sine_table = rope_tables(own_pos)
    causal = all_pos[None, :] <= own_pos[:, None]

    def attention_weights():
        return (
            lax.all_gather(column_parts[0], "dp", axis=0, tiled=True),
            lax.all_gather(column_parts[1], "dp", axis=0, tiled=True),
            lax.all_gather(column_parts[2], "dp", axis=0, tiled=True),
            lax.all_gather(column_parts[3], "dp", axis=0, tiled=True),
        )

    def mlp_weights():
        return (
            lax.all_gather(column_parts[4], "dp", axis=0, tiled=True),
            lax.all_gather(column_parts[5], "dp", axis=0, tiled=True),
            lax.all_gather(column_parts[6], "dp", axis=0, tiled=True),
        )

    def micro_step(carried, micro_batch):
        tokens, segment, upstream = micro_batch
        own_segment = lax.dynamic_slice_in_dim(segment, offset, local_rows, 0)
        allowed = causal & (own_segment[:, None] == segment[None, :])
        full_query, full_key, full_value, full_out = attention_weights()
        hidden = tokens.astype(jnp.float32)
        normed, inverse_a = normalize(hidden, gain_a)
        normed_a = normed.astype(jnp.bfloat16)
        queries = rope_heads(project(normed_a, full_query), H, cosine, sine_table)
        keys_rot = rope_heads(project(normed_a, full_key), KVH, cosine, sine_table)
        values = project(normed_a, full_value).astype(jnp.bfloat16)
        keys_all, values_all = (
            lax.all_gather(keys_rot, "seq", axis=0, tiled=True),
            lax.all_gather(values, "seq", axis=0, tiled=True),
        )
        attended, log_total = attend(queries, keys_all, values_all, allowed)
        residual = hidden + project_back(attended, full_out)
        full_gate, full_up, full_down = mlp_weights()
        normed, inverse_m = normalize(residual, gain_m)
        normed_m = normed.astype(jnp.bfloat16)
        gate_pre, up_proj, sigmoid_g, active, product = swiglu(normed_m, full_gate, full_up)
        output = (residual + project_back(product, full_down)).astype(jnp.bfloat16)
        full_gate, full_up, full_down = mlp_weights()
        d_product = project(upstream, full_down)
        d_gate, d_up = swiglu_back(d_product, gate_pre, up_proj, sigmoid_g, active)
        d_normed_m = project_back(d_gate, full_gate) + project_back(d_up, full_up)
        d_norm_m, g_gain_m = normalize_back(residual, inverse_m, gain_m, d_normed_m)
        d_residual = upstream.astype(jnp.float32) + d_norm_m
        d_res_b = d_residual.astype(jnp.bfloat16)
        full_query, full_key, full_value, full_out = attention_weights()
        d_attended = project(d_res_b, full_out).astype(jnp.bfloat16)
        d_query, d_keys, d_values = attend_back(
            queries, keys_all, values_all, allowed, log_total, d_attended
        )
        own_keys, own_values = (
            lax.psum_scatter(d_keys, "seq", scatter_dimension=0, tiled=True),
            lax.psum_scatter(d_values, "seq", scatter_dimension=0, tiled=True),
        )
        d_query_b = unrope_heads(d_query, H, cosine, sine_table)
        d_keys_b = unrope_heads(own_keys, KVH, cosine, sine_table)
        d_values_b = own_values.astype(jnp.bfloat16)
        d_normed_a = (
            project_back(d_query_b, full_query)
            + project_back(d_keys_b, full_key)
            + project_back(d_values_b, full_value)
        )
        d_norm_a, g_gain_a = normalize_back(hidden, inverse_a, gain_a, d_normed_a)
        updates = (
            g_gain_a,
            g_gain_m,
            outer_sum(normed_a, d_query_b),
            outer_sum(normed_a, d_keys_b),
            outer_sum(normed_a, d_values_b),
            outer_sum(d_res_b, attended),
            outer_sum(normed_m, d_gate),
            outer_sum(normed_m, d_up),
            outer_sum(upstream, product),
        )
        return (tuple((a + b for a, b in zip(carried, updates))), (output, d_residual + d_norm_a))

    initial = zero_gains + tuple(
        (jnp.zeros((D, matrix.shape[1]), jnp.float32) for matrix in column_parts)
    )
    totals, (outputs, d_inputs) = lax.scan(micro_step, initial, (inputs, segments, cotangent))
    row_owned = (
        lax.psum_scatter(
            totals[2].astype(jnp.bfloat16), "dp", scatter_dimension=0, tiled=True
        ).astype(jnp.float32),
        lax.psum_scatter(
            totals[3].astype(jnp.bfloat16), "dp", scatter_dimension=0, tiled=True
        ).astype(jnp.float32),
        lax.psum_scatter(
            totals[4].astype(jnp.bfloat16), "dp", scatter_dimension=0, tiled=True
        ).astype(jnp.float32),
        lax.psum_scatter(
            totals[5].astype(jnp.bfloat16), "dp", scatter_dimension=0, tiled=True
        ).astype(jnp.float32),
        lax.psum_scatter(
            totals[6].astype(jnp.bfloat16), "dp", scatter_dimension=0, tiled=True
        ).astype(jnp.float32),
        lax.psum_scatter(
            totals[7].astype(jnp.bfloat16), "dp", scatter_dimension=0, tiled=True
        ).astype(jnp.float32),
        lax.psum_scatter(
            totals[8].astype(jnp.bfloat16), "dp", scatter_dimension=0, tiled=True
        ).astype(jnp.float32),
    )
    shards = (
        lax.psum_scatter(
            row_owned[0].astype(jnp.bfloat16), "seq", scatter_dimension=1, tiled=True
        ).astype(jnp.float32),
        lax.psum_scatter(
            row_owned[1].astype(jnp.bfloat16), "seq", scatter_dimension=1, tiled=True
        ).astype(jnp.float32),
        lax.psum_scatter(
            row_owned[2].astype(jnp.bfloat16), "seq", scatter_dimension=1, tiled=True
        ).astype(jnp.float32),
        lax.psum_scatter(
            row_owned[3].astype(jnp.bfloat16), "seq", scatter_dimension=1, tiled=True
        ).astype(jnp.float32),
        lax.psum_scatter(
            row_owned[4].astype(jnp.bfloat16), "seq", scatter_dimension=1, tiled=True
        ).astype(jnp.float32),
        lax.psum_scatter(
            row_owned[5].astype(jnp.bfloat16), "seq", scatter_dimension=1, tiled=True
        ).astype(jnp.float32),
        lax.psum_scatter(
            row_owned[6].astype(jnp.bfloat16), "seq", scatter_dimension=1, tiled=True
        ).astype(jnp.float32),
    )
    gain_sums = (
        lax.psum_scatter(totals[0], ("dp", "seq"), scatter_dimension=0, tiled=True),
        lax.psum_scatter(totals[1], ("dp", "seq"), scatter_dimension=0, tiled=True),
    )
    return (
        outputs,
        d_inputs,
        gain_sums[0],
        shards[0],
        shards[1],
        shards[2],
        shards[3],
        gain_sums[1],
        shards[4],
        shards[5],
        shards[6],
    )


def solution(mesh):
    return jax.shard_map(
        per_device,
        mesh=mesh,
        in_specs=(
            P(None, ("dp", "seq"), None),
            P(None, "dp"),
            P(None, ("dp", "seq"), None),
            P(("dp", "seq")),
            P("dp", "seq"),
            P("dp", "seq"),
            P("dp", "seq"),
            P("dp", "seq"),
            P(("dp", "seq")),
            P("dp", "seq"),
            P("dp", "seq"),
            P("dp", "seq"),
        ),
        out_specs=(
            P(None, ("dp", "seq"), None),
            P(None, ("dp", "seq"), None),
            P(("dp", "seq")),
            P("dp", "seq"),
            P("dp", "seq"),
            P("dp", "seq"),
            P("dp", "seq"),
            P(("dp", "seq")),
            P("dp", "seq"),
            P("dp", "seq"),
            P("dp", "seq"),
        ),
        check_vma=False,
    )
```

profile of v0, /device:TPU:0, one launch (start us, length us, event | category | flops | bytes accessed | tf_op | source)
XLA Modules:
  0.0 5698.4 jit_solution(14192381825803001176)
XLA Ops:
  13.5 42.1 all-reduce.5
  78.3 28.5 all-gather.19.cloned.1.call-done
  106.8 28.5 all-gather.21.cloned.1.call-done
  135.3 3769.8 %while.36 = (s32[]{:T(128)}, f32[2048]{0:T(1024)}, f32[2048]{0:T(1024)}, f32[2048,2048]{1,0:T(8,128)}, f32[2048,256]{1,0:T(8,128)}, /*index=5*/f32[2048,256]{1,0...) while((s32[]{:T(128)}, f32[2048]{0:T(1024)}, ...), condition=%wide.region_12.13_spmd.clone.clone.clone, body=%wide.region_0.12_spmd.clone.clone.clone.sunk | while | flops 35651170304 | bytes 1108662272 | solution.py:272
  141.9 36.5 all-gather.25.cloned.1.call-done
  185.9 33.0 all-gather.23.cloned.1.call-done
  226.6 118.9 %all-gather.29.cloned.1.call-done = bf16[2048,2048]{0,1:T(8,128)(2,1)} async-done(((bf16[256,2048]{0,1:T(8,128)(2,1)}), bf16[2048,2048]{0,1:T(8,128)(2,1)}) %all-gather.29.cloned.1.call-update) | async-done | bytes 8388624 | tf_op jit(solution)/shard_map/while/body/eval_jaxpr/all_gather | solution.py:196
  360.3 110.7 %all-gather.27.cloned.1.call-done = bf16[2048,2048]{1,0:T(8,128)(2,1)} async-done(((bf16[256,2048]{1,0:T(8,128)(2,1)}), bf16[2048,2048]{1,0:T(8,128)(2,1)}) %all-gather.27.cloned.1.call-update) | async-done | bytes 8388624 | tf_op jit(solution)/shard_map/while/body/eval_jaxpr/all_gather | solution.py:199
  479.1 432.7 %all-gather.33.cloned.1.call-done = bf16[2048,5632]{1,0:T(8,128)(2,1)} async-done(((bf16[256,5632]{1,0:T(8,128)(2,1)}), bf16[2048,5632]{1,0:T(8,128)(2,1)}) %all-gather.33.cloned.1.call-update) | async-done | bytes 23068688 | tf_op jit(solution)/shard_map/while/body/eval_jaxpr/all_gather | solution.py:206
  924.2 430.3 %all-gather.31.cloned.1.call-done = bf16[2048,5632]{1,0:T(8,128)(2,1)} async-done(((bf16[256,5632]{1,0:T(8,128)(2,1)}), bf16[2048,5632]{1,0:T(8,128)(2,1)}) %all-gather.31.cloned.1.call-update) | async-done | bytes 23068688 | tf_op jit(solution)/shard_map/while/body/eval_jaxpr/all_gather | solution.py:204
  1366.9 430.2 %all-gather.35.cloned.1.call-done = bf16[2048,5632]{1,0:T(8,128)(2,1)} async-done(((bf16[256,5632]{1,0:T(8,128)(2,1)}), bf16[2048,5632]{1,0:T(8,128)(2,1)}) %all-gather.35.cloned.1.call-update) | async-done | bytes 23068688 | tf_op jit(solution)/shard_map/while/body/eval_jaxpr/all_gather | solution.py:205
  1999.6 36.7 all-gather.25.cloned.1.call-done
  2043.9 32.9 all-gather.23.cloned.1.call-done
  2084.4 118.8 %all-gather.29.cloned.1.call-done = bf16[2048,2048]{0,1:T(8,128)(2,1)} async-done(((bf16[256,2048]{0,1:T(8,128)(2,1)}), bf16[2048,2048]{0,1:T(8,128)(2,1)}) %all-gather.29.cloned.1.call-update) | async-done | bytes 8388624 | tf_op jit(solution)/shard_map/while/body/eval_jaxpr/all_gather | solution.py:196
  2217.6 110.9 %all-gather.27.cloned.1.call-done = bf16[2048,2048]{1,0:T(8,128)(2,1)} async-done(((bf16[256,2048]{1,0:T(8,128)(2,1)}), bf16[2048,2048]{1,0:T(8,128)(2,1)}) %all-gather.27.cloned.1.call-update) | async-done | bytes 8388624 | tf_op jit(solution)/shard_map/while/body/eval_jaxpr/all_gather | solution.py:199
  2336.6 432.8 %all-gather.33.cloned.1.call-done = bf16[2048,5632]{1,0:T(8,128)(2,1)} async-done(((bf16[256,5632]{1,0:T(8,128)(2,1)}), bf16[2048,5632]{1,0:T(8,128)(2,1)}) %all-gather.33.cloned.1.call-update) | async-done | bytes 23068688 | tf_op jit(solution)/shard_map/while/body/eval_jaxpr/all_gather | solution.py:206
  2781.8 430.2 %all-gather.31.cloned.1.call-done = bf16[2048,5632]{1,0:T(8,128)(2,1)} async-done(((bf16[256,5632]{1,0:T(8,128)(2,1)}), bf16[2048,5632]{1,0:T(8,128)(2,1)}) %all-gather.31.cloned.1.call-update) | async-done | bytes 23068688 | tf_op jit(solution)/shard_map/while/body/eval_jaxpr/all_gather | solution.py:204
  3224.3 430.4 %all-gather.35.cloned.1.call-done = bf16[2048,5632]{1,0:T(8,128)(2,1)} async-done(((bf16[256,5632]{1,0:T(8,128)(2,1)}), bf16[2048,5632]{1,0:T(8,128)(2,1)}) %all-gather.35.cloned.1.call-update) | async-done | bytes 23068688 | tf_op jit(solution)/shard_map/while/body/eval_jaxpr/all_gather | solution.py:205
  3749.7 30.5 select_add_fusion.18
  3780.2 29.4 select_add_fusion.19
  3823.7 30.4 select_add_fusion.20
  4004.4 36.1 reduce-scatter.31.cloned.1.call-done
  4040.6 151.5 %reduce-scatter.23.cloned.1.call-done = bf16[256,2048]{1,0:T(8,128)(2,1)} async-done(((bf16[2048,2048]{1,0:T(8,128)(2,1)}), bf16[256,2048]{1,0:T(8,128)(2,1)}) %reduce-scatter.23.cloned.1.call-update) | async-done | bytes 1048592 | tf_op jit(solution)/shard_map/reduce_scatter | solution.py:274
  4192.2 151.9 %reduce-scatter.35.cloned.1.call-done = bf16[256,2048]{1,0:T(8,128)(2,1)} async-done(((bf16[2048,2048]{1,0:T(8,128)(2,1)}), bf16[256,2048]{1,0:T(8,128)(2,1)}) %reduce-scatter.35.cloned.1.call-update) | async-done | bytes 1048592 | tf_op jit(solution)/shard_map/reduce_scatter | solution.py:283
  4344.2 376.4 %reduce-scatter.39.cloned.1.call-done = bf16[256,5632]{1,0:T(8,128)(2,1)} async-done(((bf16[2048,5632]{1,0:T(8,128)(2,1)}), bf16[256,5632]{1,0:T(8,128)(2,1)}) %reduce-scatter.39.cloned.1.call-update) | async-done | bytes 2883600 | tf_op jit(solution)/shard_map/reduce_scatter | solution.py:286
  4725.2 371.9 %reduce-scatter.41.cloned.1.call-done = bf16[256,5632]{1,0:T(8,128)(2,1)} async-done(((bf16[2048,5632]{1,0:T(8,128)(2,1)}), bf16[256,5632]{1,0:T(8,128)(2,1)}) %reduce-scatter.41.cloned.1.call-update) | async-done | bytes 2883600 | tf_op jit(solution)/shard_map/reduce_scatter | solution.py:289
  5101.8 371.9 %reduce-scatter.43.cloned.1.call-done = bf16[256,5632]{1,0:T(8,128)(2,1)} async-done(((bf16[2048,5632]{1,0:T(8,128)(2,1)}), bf16[256,5632]{1,0:T(8,128)(2,1)}) %reduce-scatter.43.cloned.1.call-update) | async-done | bytes 2883600 | tf_op jit(solution)/shard_map/reduce_scatter | solution.py:292
  5478.3 39.6 all-reduce.4
  5546.2 25.8 reduce-scatter.37.cloned.1.call-done
  5573.9 37.1 reduce-scatter.45.cloned.1.call-done
  5613.6 36.3 reduce-scatter.47.cloned.1.call-done
  5652.5 36.1 reduce-scatter.49.cloned.1.call-done
  (411 shorter events, 668.1 us)
Async XLA Ops:
  10.5 96.3 %all-gather.19.cloned.1.call-start = ((), (), s32[]{:S(2)}) async-start(), calls=%async_computation.19 | async-start | bytes 3604480 | tf_op jit(solution)/shard_map/all_gather | solution.py:187
  11.1 124.2 %all-gather.21.cloned.1.call-start = ((), (), s32[]{:S(2)}) async-start(), calls=%async_computation.20 | async-start | bytes 3604480 | tf_op jit(solution)/shard_map/all_gather | solution.py:186
  135.8 83.1 %all-gather.23.cloned.1.call-start = ((), (), s32[]{:S(2)}) async-start(), calls=%async_computation.35 | async-start | bytes 1179648 | tf_op jit(solution)/shard_map/while/body/eval_jaxpr/all_gather | solution.py:197
  136.6 208.9 %all-gather.29.cloned.1.call-start = ((), (), s32[]{:S(2)}) async-start(), calls=%async_computation.38 | async-start | bytes 9437184 | tf_op jit(solution)/shard_map/while/body/eval_jaxpr/all_gather | solution.py:196
  137.3 333.7 %all-gather.27.cloned.1.call-start = ((), (), s32[]{:S(2)}) async-start(), calls=%async_computation.37 | async-start | bytes 9437184 | tf_op jit(solution)/shard_map/while/body/eval_jaxpr/all_gather | solution.py:199
  138.1 773.7 %all-gather.33.cloned.1.call-start = ((), (), s32[]{:S(2)}) async-start(), calls=%async_computation.40 | async-start | bytes 25952256 | tf_op jit(solution)/shard_map/while/body/eval_jaxpr/all_gather | solution.py:206
  138.7 1215.8 %all-gather.31.cloned.1.call-start = ((), (), s32[]{:S(2)}) async-start(), calls=%async_computation.39 | async-start | bytes 25952256 | tf_op jit(solution)/shard_map/while/body/eval_jaxpr/all_gather | solution.py:204
  139.4 1657.7 %all-gather.35.cloned.1.call-start = ((), (), s32[]{:S(2)}) async-start(), calls=%async_computation.41 | async-start | bytes 25952256 | tf_op jit(solution)/shard_map/while/body/eval_jaxpr/all_gather | solution.py:205
  140.0 1841.6 %reduce-scatter.51.cloned.1.call-start = ((), (), s32[]{:S(2)}) async-start(), calls=%async_computation.42 | async-start | bytes 655360 | tf_op jit(solution)/shard_map/while/body/eval_jaxpr/reduce_scatter | solution.py:244
  1889.5 94.9 %reduce-scatter.53.cloned.1.call-start = ((), (), s32[]{:S(2)}) async-start(), calls=%async_computation.43 | async-start | bytes 655360 | tf_op jit(solution)/shard_map/while/body/eval_jaxpr/reduce_scatter | solution.py:245
  1993.8 82.9 %all-gather.23.cloned.1.call-start = ((), (), s32[]{:S(2)}) async-start(), calls=%async_computation.35 | async-start | bytes 1179648 | tf_op jit(solution)/shard_map/while/body/eval_jaxpr/all_gather | solution.py:197
  1994.4 208.7 %all-gather.29.cloned.1.call-start = ((), (), s32[]{:S(2)}) async-start(), calls=%async_computation.38 | async-start | bytes 9437184 | tf_op jit(solution)/shard_map/while/body/eval_jaxpr/all_gather | solution.py:196
  1995.0 333.5 %all-gather.27.cloned.1.call-start = ((), (), s32[]{:S(2)}) async-start(), calls=%async_computation.37 | async-start | bytes 9437184 | tf_op jit(solution)/shard_map/while/body/eval_jaxpr/all_gather | solution.py:199
  1995.6 773.8 %all-gather.33.cloned.1.call-start = ((), (), s32[]{:S(2)}) async-start(), calls=%async_computation.40 | async-start | bytes 25952256 | tf_op jit(solution)/shard_map/while/body/eval_jaxpr/all_gather | solution.py:206
  1996.3 1215.7 %all-gather.31.cloned.1.call-start = ((), (), s32[]{:S(2)}) async-start(), calls=%async_computation.39 | async-start | bytes 25952256 | tf_op jit(solution)/shard_map/while/body/eval_jaxpr/all_gather | solution.py:204
  1996.9 1657.8 %all-gather.35.cloned.1.call-start = ((), (), s32[]{:S(2)}) async-start(), calls=%async_computation.41 | async-start | bytes 25952256 | tf_op jit(solution)/shard_map/while/body/eval_jaxpr/all_gather | solution.py:205
  1997.7 1890.2 %reduce-scatter.51.cloned.1.call-start = ((), (), s32[]{:S(2)}) async-start(), calls=%async_computation.42 | async-start | bytes 655360 | tf_op jit(solution)/shard_map/while/body/eval_jaxpr/reduce_scatter | solution.py:244
  3747.4 143.3 %reduce-scatter.53.cloned.1.call-start = ((), (), s32[]{:S(2)}) async-start(), calls=%async_computation.43 | async-start | bytes 655360 | tf_op jit(solution)/shard_map/while/body/eval_jaxpr/reduce_scatter | solution.py:245
  3905.0 98.7 %reduce-scatter.27.cloned.1.call-start = ((), (), s32[]{:S(2)}) async-start(), calls=%async_computation.23 | async-start | bytes 1179648 | tf_op jit(solution)/shard_map/reduce_scatter | solution.py:277
  3907.7 132.9 %reduce-scatter.31.cloned.1.call-start = ((), (), s32[]{:S(2)}) async-start(), calls=%async_computation.25 | async-start | bytes 1179648 | tf_op jit(solution)/shard_map/reduce_scatter | solution.py:280
  3910.3 281.8 %reduce-scatter.23.cloned.1.call-start = ((), (), s32[]{:S(2)}) async-start(), calls=%async_computation.21 | async-start | bytes 9437184 | tf_op jit(solution)/shard_map/reduce_scatter | solution.py:274
  3919.5 424.6 %reduce-scatter.35.cloned.1.call-start = ((), (), s32[]{:S(2)}) async-start(), calls=%async_computation.27 | async-start | bytes 9437184 | tf_op jit(solution)/shard_map/reduce_scatter | solution.py:283
  3928.7 791.8 %reduce-scatter.39.cloned.1.call-start = ((), (), s32[]{:S(2)}) async-start(), calls=%async_computation.29 | async-start | bytes 25952256 | tf_op jit(solution)/shard_map/reduce_scatter | solution.py:286
  3953.7 1143.4 %reduce-scatter.41.cloned.1.call-start = ((), (), s32[]{:S(2)}) async-start(), calls=%async_computation.30 | async-start | bytes 25952256 | tf_op jit(solution)/shard_map/reduce_scatter | solution.py:289
  3978.7 1495.0 %reduce-scatter.43.cloned.1.call-start = ((), (), s32[]{:S(2)}) async-start(), calls=%async_computation.31 | async-start | bytes 25952256 | tf_op jit(solution)/shard_map/reduce_scatter | solution.py:292
  4003.7 1515.4 %reduce-scatter.29.cloned.1.call-start = ((), (), s32[]{:S(2)}) async-start(), calls=%async_computation.24 | async-start | bytes 163840 | tf_op jit(solution)/shard_map/reduce_scatter | solution.py:300
  4004.4 1516.1 %reduce-scatter.33.cloned.1.call-start = ((), (), s32[]{:S(2)}) async-start(), calls=%async_computation.26 | async-start | bytes 163840 | tf_op jit(solution)/shard_map/reduce_scatter | solution.py:303
  4040.6 1503.8 %reduce-scatter.25.cloned.1.call-start = ((), (), s32[]{:S(2)}) async-start(), calls=%async_computation.22 | async-start | bytes 1310720 | tf_op jit(solution)/shard_map/reduce_scatter | solution.py:297
  4192.2 1379.9 %reduce-scatter.37.cloned.1.call-start = ((), (), s32[]{:S(2)}) async-start(), calls=%async_computation.28 | async-start | bytes 1310720 | tf_op jit(solution)/shard_map/reduce_scatter | solution.py:306
  4344.1 1266.8 %reduce-scatter.45.cloned.1.call-start = ((), (), s32[]{:S(2)}) async-start(), calls=%async_computation.32 | async-start | bytes 3604480
  4725.2 924.7 %reduce-scatter.47.cloned.1.call-start = ((), (), s32[]{:S(2)}) async-start(), calls=%async_computation.33 | async-start | bytes 3604480
  5101.7 586.9 %reduce-scatter.49.cloned.1.call-start = ((), (), s32[]{:S(2)}) async-start(), calls=%async_computation.34 | async-start | bytes 3604480
  (93 other events, 13451.9 us)
Sparse Core Ops, SparseCore 0:
  49.8 28.4 all-gather.16
  79.7 27.0 all-gather.18
  108.2 27.0 all-gather.20
  138.1 40.2 all-gather.24
  180.6 38.2 all-gather.22
  221.2 124.2 all-gather.28
  347.9 123.1 all-gather.26
  472.4 439.3 all-gather.32
  913.4 441.0 all-gather.30
  1356.0 441.0 all-gather.34
  1889.7 21.6 reduce-scatter.50
  1934.8 21.6 reduce-scatter.52
  1996.1 40.1 all-gather.24
  2038.4 38.2 all-gather.22
  2078.8 124.2 all-gather.28
  2205.3 123.1 all-gather.26
  2330.1 439.2 all-gather.32
  2770.9 441.0 all-gather.30
  3213.6 441.0 all-gather.34
  3747.5 21.6 reduce-scatter.50
  3909.5 63.7 reduce-scatter.26
  3977.7 62.8 reduce-scatter.30
  4044.0 148.0 reduce-scatter.22
  4196.0 147.9 reduce-scatter.34
  4348.0 372.5 reduce-scatter.38
  4724.4 372.7 reduce-scatter.40
  5100.9 372.7 reduce-scatter.42
  5519.5 24.8 reduce-scatter.24
  5547.1 24.8 reduce-scatter.36
  5574.6 36.3 reduce-scatter.44
  5613.5 36.3 reduce-scatter.46
  5652.2 36.3 reduce-scatter.48
  (5 shorter events, 96.2 us)
where the time goes:
time: 5700 us
  waiting for transfers between devices  4880 us (86%)
  matrix products  513 us (9%)
  other arithmetic  128 us (2%)
  blocking collectives  120 us (2%)
    all_gather x2, waiting for transfers between devices, mlp_weights(): lax.all_gather(column_parts[6], 'dp', axis=0, tiled=True)  866 us
    all_gather x2, waiting for transfers between devices, mlp_weights(): lax.all_gather(column_parts[5], 'dp', axis=0, tiled=True)  861 us
    all_gather x2, waiting for transfers between devices, mlp_weights(): lax.all_gather(column_parts[4], 'dp', axis=0, tiled=True)  861 us
    reduce_scatter x1, waiting for transfers between devices, per_device(): lax.psum_scatter(totals[6].astype(jnp.bfloat16), 'dp', scatter_dimension=...  376 us
    reduce_scatter x1, waiting for transfers between devices, per_device(): lax.psum_scatter(totals[7].astype(jnp.bfloat16), 'dp', scatter_dimension=...  372 us
    reduce_scatter x1, waiting for transfers between devices, per_device(): lax.psum_scatter(totals[8].astype(jnp.bfloat16), 'dp', scatter_dimension=...  372 us
    all_gather x2, waiting for transfers between devices, attention_weights(): lax.all_gather(column_parts[0], 'dp', axis=0, tiled=True)  238 us
    all_gather x2, waiting for transfers between devices, attention_weights(): lax.all_gather(column_parts[3], 'dp', axis=0, tiled=True)  222 us
  transfers between devices with their start and end apart: 37, of which 28 were waited for; matrix products, arithmetic and copies ran while one was open for 8% of the time, Pallas kernels for 0%

commit v1 on v0

v1 whole, which is shorter than its diff:
```python
import jax
import jax.numpy as jnp
from jax import lax
from jax.sharding import PartitionSpec as P

HD = 64
EPS = 1e-05
THETA = 10000.0
NEGATIVE = -1e30
BF = jnp.bfloat16
F32 = jnp.float32


def rope_tables(positions):
    half_dim = HD // 2
    frequency = THETA ** (-(jnp.arange(half_dim).astype(F32) * (2.0 / HD)))
    angles = positions.astype(F32)[:, None] * frequency[None, :]
    return (jnp.cos(angles), jnp.sin(angles))


def rotate(values, cosine, sine_table):
    half_dim = values.shape[-1] // 2
    c = cosine[:, None, :]
    s = sine_table[:, None, :]
    a = values[..., :half_dim]
    b = values[..., half_dim:]
    return jnp.concatenate([a * c - b * s, b * c + a * s], axis=-1)


def unrotate(gradient, cosine, sine_table):
    return rotate(gradient, cosine, -sine_table)


def normalize(hidden, gain_vec):
    inverse = lax.rsqrt(jnp.mean(hidden * hidden, axis=-1, keepdims=True) + EPS)
    return (hidden * inverse * gain_vec, inverse)


def normalize_back(hidden, inverse, gain_vec, gradient):
    unit_rows = hidden * inverse
    gain_grad = jnp.sum(gradient * unit_rows, axis=0)
    weighted = gradient * gain_vec
    return (
        inverse * (weighted - unit_rows * jnp.mean(weighted * unit_rows, axis=-1, keepdims=True)),
        gain_grad,
    )


def project(a, b):
    return jnp.dot(a, b, preferred_element_type=F32)


def project_back(a, b):
    return lax.dot_general(a, b, (((1,), (1,)), ((), ())), preferred_element_type=F32)


def outer_sum(a, b):
    return lax.dot_general(a, b, (((0,), (0,)), ((), ())), preferred_element_type=F32)


def per_device(
    inputs, segments, cotangent, attn_gain, w_query, w_key, w_value, w_out, mlp_gain, w_gate, w_up, w_down,
):
    micro, rows, d = inputs.shape
    seq = lax.axis_size("seq")
    length = rows * seq
    full = micro * length

    def gather_rows(x):
        return lax.all_gather(x.reshape(micro, rows, -1), "seq", axis=1, tiled=True).reshape(full, -1)

    def scatter_rows(x):
        x = x.astype(BF).reshape(micro, length, -1)
        return lax.psum_scatter(x, "seq", scatter_dimension=1, tiled=True).reshape(micro * rows, -1).astype(F32)

    def gather_w(w):
        return lax.all_gather(w, "dp", axis=0, tiled=True)

    def scatter_w(g):
        return lax.psum_scatter(g.astype(BF), "dp", scatter_dimension=0, tiled=True).astype(F32)

    gain_a = lax.all_gather(attn_gain, ("dp", "seq"), axis=0, tiled=True).astype(F32)
    gain_m = lax.all_gather(mlp_gain, ("dp", "seq"), axis=0, tiled=True).astype(F32)
    wq, wk, wv, wo = gather_w(w_query), gather_w(w_key), gather_w(w_value), gather_w(w_out)
    wg, wu, wd = gather_w(w_gate), gather_w(w_up), gather_w(w_down)
    heads = wq.shape[1] // HD
    kv_heads = wk.shape[1] // HD
    groups = heads // kv_heads

    pos = jnp.arange(length, dtype=jnp.int32)
    cosine, sine = rope_tables(pos)
    cos_f, sin_f = jnp.tile(cosine, (micro, 1)), jnp.tile(sine, (micro, 1))
    allowed = (pos[None, :] <= pos[:, None])[None] & (segments[:, :, None] == segments[:, None, :])
    allowed = allowed[:, None, None]

    hidden = inputs.reshape(micro * rows, d).astype(F32)
    upstream = cotangent.reshape(micro * rows, d)
    normed, inverse_a = normalize(hidden, gain_a)
    na = gather_rows(normed.astype(BF))
    up_full = gather_rows(upstream)

    def rope(x, n, s):
        return rotate(x.reshape(full, n, HD), cos_f, s).astype(BF).reshape(full, n * HD)

    q = rope(project(na, wq), heads, sin_f)
    k = rope(project(na, wk), kv_heads, sin_f)
    v = project(na, wv).astype(BF)
    qg = q.reshape(micro, length, kv_heads, groups, HD)
    kg = k.reshape(micro, length, kv_heads, HD)
    vg = v.reshape(micro, length, kv_heads, HD)
    scores = jnp.einsum("mqkgd,mpkd->mkgqp", qg, kg, preferred_element_type=F32) * HD ** (-0.5)
    scores = jnp.where(allowed, scores, NEGATIVE)
    maximum = jnp.max(scores, axis=-1, keepdims=True)
    weights = jnp.where(allowed, jnp.exp(scores - maximum), 0.0)
    denominator = jnp.sum(weights, axis=-1, keepdims=True)
    prob = weights / denominator
    prob_b = prob.astype(BF)
    attended = jnp.einsum("mkgqp,mpkd->mqkgd", prob_b, vg, preferred_element_type=F32)
    attended = attended.astype(BF).reshape(full, heads * HD)
    residual = hidden + scatter_rows(project_back(attended, wo))
    normed, inverse_m = normalize(residual, gain_m)
    nm = gather_rows(normed.astype(BF))
    gate_pre = project(nm, wg)
    up_proj = project(nm, wu)
    sigmoid_g = jax.nn.sigmoid(gate_pre)
    active = gate_pre * sigmoid_g
    product = (active * up_proj).astype(BF)
    output = (residual + scatter_rows(project_back(product, wd))).astype(BF)
    g_down = scatter_w(outer_sum(up_full, product))
    d_product = project(up_full, wd)
    d_gate = (d_product * up_proj * sigmoid_g * (1.0 + gate_pre * (1.0 - sigmoid_g))).astype(BF)
    d_up = (d_product * active).astype(BF)
    g_gate = scatter_w(outer_sum(nm, d_gate))
    g_up = scatter_w(outer_sum(nm, d_up))
    d_nm = scatter_rows(project_back(d_gate, wg) + project_back(d_up, wu))
    d_norm_m, g_gain_m = normalize_back(residual, inverse_m, gain_m, d_nm)
    d_residual = upstream.astype(F32) + d_norm_m
    dr = gather_rows(d_residual.astype(BF))
    g_out = scatter_w(outer_sum(dr, attended))
    d_att = project(dr, wo).astype(BF)
    dg = d_att.reshape(micro, length, kv_heads, groups, HD)
    d_values = jnp.einsum("mkgqp,mqkgd->mpkd", prob_b, dg, preferred_element_type=F32)
    d_prob = jnp.einsum("mqkgd,mpkd->mkgqp", dg, vg, preferred_element_type=F32)
    row_sum = jnp.sum(prob * d_prob, axis=-1, keepdims=True)
    d_scores = (prob * (d_prob - row_sum) * HD ** (-0.5)).astype(BF)
    d_query = jnp.einsum("mkgqp,mpkd->mqkgd", d_scores, kg, preferred_element_type=F32)
    d_keys = jnp.einsum("mkgqp,mqkgd->mpkd", d_scores, qg, preferred_element_type=F32)
    dq = rope(d_query, heads, -sin_f)
    dk = rope(d_keys, kv_heads, -sin_f)
    dv = d_values.astype(BF).reshape(full, kv_heads * HD)
    g_query = scatter_w(outer_sum(na, dq))
    g_key = scatter_w(outer_sum(na, dk))
    g_value = scatter_w(outer_sum(na, dv))
    d_na = scatter_rows(project_back(dq, wq) + project_back(dk, wk) + project_back(dv, wv))
    d_norm_a, g_gain_a = normalize_back(hidden, inverse_a, gain_a, d_na)
    d_input = d_residual + d_norm_a
    gain_grads = lax.psum_scatter(
        jnp.stack([g_gain_a, g_gain_m]), ("dp", "seq"), scatter_dimension=1, tiled=True
    )
    return (
        output.reshape(micro, rows, d),
        d_input.reshape(micro, rows, d),
        gain_grads[0],
        g_query,
        g_key,
        g_value,
        g_out,
        gain_grads[1],
        g_gate,
        g_up,
        g_down,
    )


def solution(mesh):
    tok, wt, gn = P(None, ("dp", "seq"), None), P("dp", "seq"), P(("dp", "seq"))
    return jax.shard_map(
        per_device,
        mesh=mesh,
        in_specs=(tok, P(None, "dp"), tok, gn, wt, wt, wt, wt, gn, wt, wt, wt),
        out_specs=(tok, tok, gn, wt, wt, wt, wt, gn, wt, wt, wt),
        check_vma=False,
    )
```

time: 5700 us -> 1540 us (0.27)
  waiting for transfers between devices: 4880 us -> 1130 us
  matrix products: 513 us -> 193 us
  other arithmetic: 128 us -> 50.2 us
    all_gather x19 -> x9, waiting for transfers between devices: 3250 us -> 324 us  [the longest x5 267 us: gather_w(): return lax.all_gather(w, 'dp', axis=0, tiled=True)]
    reduce_scatter x15 -> x11, waiting for transfers between devices: 1510 us -> 667 us  [the longest x7 491 us: scatter_w(): lax.psum_scatter(g.astype(BF), 'dp', scatter_dimension=0, tiled=True)]
    dot_general x54 -> x27, matrix products: 513 us -> 193 us  [the longest x7 57.4 us: project(): return jnp.dot(a, b, preferred_element_type=F32)]
    convert_element_type x20 -> x13, other arithmetic: 106 us -> 19.4 us  [the longest x6 11 us: scatter_w(): lax.psum_scatter(g.astype(BF), 'dp', scatter_dimension=0, tiled=True)]
  transfers between devices with their start and end apart: 37 -> 21, of which waited for: 28 -> 17; matrix products, arithmetic and copies ran while one was open for 8% -> 14% of each run, Pallas kernels for 0% -> 0%
where the time goes in v1:
time: 1540 us; the launch traced here: 1530 us
  waiting for transfers between devices  1130 us (73%)
  matrix products  193 us (13%)
  blocking collectives  104 us (7%)
  other arithmetic  50.2 us (3%)
  local copies, waits for them, and re-layouts  39.3 us (3%)
  between operations  15.6 us (1%)
    reduce_scatter x7, waiting for transfers between devices, scatter_w(): lax.psum_scatter(g.astype(BF), 'dp', scatter_dimension=0, tiled=True)  491 us
    all_gather x5, waiting for transfers between devices, gather_w(): return lax.all_gather(w, 'dp', axis=0, tiled=True)  267 us
    reduce_scatter x4, waiting for transfers between devices, scatter_rows(): lax.psum_scatter(x, 'seq', scatter_dimension=1, tiled=True)  175 us
    unnamed x22, waiting for transfers between devices  136 us
    all_gather x2, blocking collectives, gather_w(): return lax.all_gather(w, 'dp', axis=0, tiled=True)  61.8 us
    all_gather x4, waiting for transfers between devices, gather_rows(): lax.all_gather(x.reshape(micro, rows, -1), 'seq', axis=1, tiled=True)  57.5 us
    dot_general x7, matrix products, project(): return jnp.dot(a, b, preferred_element_type=F32)  57.4 us
    dot_general x7, matrix products, outer_sum(): lax.dot_general(a, b, (((0,), (0,)), ((), ())), preferred_element_type=F32)  47.5 us
  transfers between devices with their start and end apart: 21, of which 17 were waited for; matrix products, arithmetic and copies ran while one was open for 14% of the time, Pallas kernels for 0%

profile of v1, /device:TPU:0, one launch (start us, length us, event | category | flops | bytes accessed | tf_op | source)
XLA Modules:
  0.0 1530.6 jit_solution(7457518318486003662)
XLA Ops:
  9.7 42.6 %all-reduce.2 = (bf16[2048]{0:T(1024)(128)(2,1)S(1)}, bf16[2048]{0:T(1024)(128)(2,1)S(1)}) all-reduce(bf16[2048]{0:T(1024)(128)(2,1)S(1)} %dynamic-update-slice, bf16[2048]{0:T(1024)(128)(2,1)S(1)} %dynamic-update-slice.1), channel_id=1, replica_groups=mesh['dp'=8,'seq'=4] {'dp','seq'}, use_global_device_ids=true, to_apply=%add | all-reduce | flops 4096 | bytes 16384
  59.3 30.7 %all_gather.42 = bf16[2048,64]{0,1:T(8,128)(2,1)S(1)} all-gather(bf16[256,64]{0,1:T(8,128)(2,1)S(1)} %copy-done.48), channel_id=1, replica_groups=mesh['dp'=8,'seq'=4] {'dp'}, dimensions={0}, use_global_device_ids=true | all-gather | bytes 294912 | tf_op jit(solution)/shard_map/all_gather | solution.py:77
  90.0 31.1 %all_gather.41 = bf16[2048,64]{0,1:T(8,128)(2,1)S(1)} all-gather(bf16[256,64]{0,1:T(8,128)(2,1)S(1)} %copy-done.49), channel_id=1, replica_groups=mesh['dp'=8,'seq'=4] {'dp'}, dimensions={0}, use_global_device_ids=true | all-gather | bytes 294912 | tf_op jit(solution)/shard_map/all_gather | solution.py:77
  163.1 44.7 %reduce-scatter.15.cloned.1.call-done = bf16[2,128,2048]{2,1,0:T(8,128)(2,1)} async-done(((bf16[2,512,2048]{2,1,0:T(8,128)(2,1)}), bf16[2,128,2048]{2,1,0:T(8,128)(2,1)}) %reduce-scatter.15.cloned.1.call-update) | async-done | bytes 1048592 | tf_op jit(solution)/shard_map/reduce_scatter | solution.py:74
  214.4 88.4 %all-gather.20.cloned.1.call-done = bf16[2048,1408]{1,0:T(8,128)(2,1)} async-done(((bf16[256,1408]{1,0:T(8,128)(2,1)}), bf16[2048,1408]{1,0:T(8,128)(2,1)}) %all-gather.20.cloned.1.call-update) | async-done | bytes 5767184 | tf_op jit(solution)/shard_map/all_gather | solution.py:77
  302.7 34.8 %all-gather.16.cloned.1.call-done = bf16[2,512,2048]{2,1,0:T(8,128)(2,1)} async-done(((bf16[2,128,2048]{2,1,0:T(8,128)(2,1)}), bf16[2,512,2048]{2,1,0:T(8,128)(2,1)}) %all-gather.16.cloned.1.call-update) | async-done | bytes 4194320 | tf_op jit(solution)/shard_map/all_gather | solution.py:70
  337.5 11.7 fusion.65
  349.2 83.4 %all-gather.18.cloned.1.call-done = bf16[2048,1408]{1,0:T(8,128)(2,1)} async-done(((bf16[256,1408]{1,0:T(8,128)(2,1)}), bf16[2048,1408]{1,0:T(8,128)(2,1)}) %all-gather.18.cloned.1.call-update) | async-done | bytes 5767184 | tf_op jit(solution)/shard_map/all_gather | solution.py:77
  432.6 11.7 fusion.64
  444.3 22.7 %all-gather.24.cloned.1.call-done = bf16[2,512,2048]{2,1,0:T(8,128)(2,1)} async-done(((bf16[2,128,2048]{2,1,0:T(8,128)(2,1)}), bf16[2,512,2048]{2,1,0:T(8,128)(2,1)}) %all-gather.24.cloned.1.call-update) | async-done | bytes 4194320 | tf_op jit(solution)/shard_map/all_gather | solution.py:70
  466.9 95.1 %all-gather.22.cloned.1.call-done = bf16[2048,1408]{1,0:T(8,128)(2,1)} async-done(((bf16[256,1408]{1,0:T(8,128)(2,1)}), bf16[2048,1408]{1,0:T(8,128)(2,1)}) %all-gather.22.cloned.1.call-update) | async-done | bytes 5767184 | tf_op jit(solution)/shard_map/all_gather | solution.py:77
  562.0 16.1 %multiply_convert_fusion = (bf16[1024,1408]{1,0:T(8,128)(2,1)}, bf16[1024,1408]{1,0:T(8,128)(2,1)S(1)}, bf16[1024,1408]{1,0:T(8,128)(2,1)}) fusion(f32[1024,1408]{1,0:T(8,128)} %fusion.64, f32[1024,1408]{1,0:T(8,128)} %fusion.65, bf16[1024,2048]{1,0:T(8,128)(2,1)} %bitcast.247, bf16[2048,1408]{1,0:T(8,128)(2,1)} %all-gather.22.cloned.1.call-done), kind=kOutput, calls=%fused_computation.23 | convolution fusion | flops 5927206912 | bytes 30146560 | tf_op jit(solution)/shard_map/dot_general | solution.py:50
  578.2 6.7 fusion.66
  584.9 11.2 add_convert_fusion.1
  596.2 42.8 %reduce-scatter.19.cloned.1.call-done = bf16[2,128,2048]{2,1,0:T(8,128)(2,1)} async-done(((bf16[2,512,2048]{2,1,0:T(8,128)(2,1)}), bf16[2,128,2048]{2,1,0:T(8,128)(2,1)}) %reduce-scatter.19.cloned.1.call-update) | async-done | bytes 1048592 | tf_op jit(solution)/shard_map/reduce_scatter | solution.py:74
  645.5 10.5 fusion.12
  657.8 10.9 convolution_convert_fusion.1
  670.5 10.9 convolution_convert_fusion.2
  694.0 9.1 fusion.45
  703.4 15.7 %fusion = (f32[2,8,512]{2,1,0:T(8,128)S(1)}, f32[2,512,512,8]{2,1,3,0:T(8,128)}) fusion(f32[2,8,512]{2,1,0:T(8,128)S(1)} %copy-done.42, f32[2,8,512]{2,1,0:T(8,128)S(1)} %copy-done.37, f32[2,512,512,8]{2,1,3,0:T(8,128)} %copy-done, pred[2,512,512]{1,2,0:T(8,128)(4,1)S(1)} %copy-done.10, bf16[2,512,8,64]{1,3,2,0:T(8,128)(2,1)S(1)} %copy-done.26, ...), kind=kOutput, calls=%fused_computation.3 | convolution fusion | flops 566222848 | bytes 35356672 | tf_op jit(solution)/shard_map/mqkgd,mpkd->mkgqp/dot_general | solution.py:143
  719.1 12.2 fusion.7
  731.3 6.2 convolution_bitcast_fusion.2
  777.2 11.0 convolution_convert_fusion.3
  796.4 111.0 %reduce-scatter.33.cloned.1.call-done = bf16[256,1408]{1,0:T(8,128)(2,1)} async-done(((bf16[2048,1408]{1,0:T(8,128)(2,1)}), bf16[256,1408]{1,0:T(8,128)(2,1)}) %reduce-scatter.33.cloned.1.call-update) | async-done | bytes 720912 | tf_op jit(solution)/shard_map/reduce_scatter | solution.py:80
  909.7 111.0 %reduce-scatter.31.cloned.1.call-done = bf16[256,1408]{1,0:T(8,128)(2,1)} async-done(((bf16[2048,1408]{1,0:T(8,128)(2,1)}), bf16[256,1408]{1,0:T(8,128)(2,1)}) %reduce-scatter.31.cloned.1.call-update) | async-done | bytes 720912 | tf_op jit(solution)/shard_map/reduce_scatter | solution.py:80
  1023.0 62.9 %reduce-scatter.27.cloned.1.call-done = bf16[256,64]{0,1:T(8,128)(2,1)} async-done(((bf16[2048,64]{0,1:T(8,128)(2,1)}), bf16[256,64]{0,1:T(8,128)(2,1)}) %reduce-scatter.27.cloned.1.call-update) | async-done | bytes 32784 | tf_op jit(solution)/shard_map/reduce_scatter | solution.py:80
  1087.3 63.1 %reduce-scatter.25.cloned.1.call-done = bf16[256,64]{0,1:T(8,128)(2,1)} async-done(((bf16[2048,64]{0,1:T(8,128)(2,1)}), bf16[256,64]{0,1:T(8,128)(2,1)}) %reduce-scatter.25.cloned.1.call-update) | async-done | bytes 32784 | tf_op jit(solution)/shard_map/reduce_scatter | solution.py:80
  1151.8 68.8 %reduce-scatter.29.cloned.1.call-done = bf16[256,512]{1,0:T(8,128)(2,1)} async-done(((bf16[2048,512]{1,0:T(8,128)(2,1)}), bf16[256,512]{1,0:T(8,128)(2,1)}) %reduce-scatter.29.cloned.1.call-update) | async-done | bytes 262160 | tf_op jit(solution)/shard_map/reduce_scatter | solution.py:80
  1222.4 68.9 %reduce-scatter.23.cloned.1.call-done = bf16[256,512]{1,0:T(8,128)(2,1)} async-done(((bf16[2048,512]{1,0:T(8,128)(2,1)}), bf16[256,512]{1,0:T(8,128)(2,1)}) %reduce-scatter.23.cloned.1.call-update) | async-done | bytes 262160 | tf_op jit(solution)/shard_map/reduce_scatter | solution.py:80
  1293.1 44.3 %reduce-scatter.21.cloned.1.call-done = bf16[2,128,2048]{2,1,0:T(8,128)(2,1)} async-done(((bf16[2,512,2048]{2,1,0:T(8,128)(2,1)}), bf16[2,128,2048]{2,1,0:T(8,128)(2,1)}) %reduce-scatter.21.cloned.1.call-update) | async-done | bytes 1048592 | tf_op jit(solution)/shard_map/reduce_scatter | solution.py:74
  1340.8 43.7 %reduce-scatter.17.cloned.1.call-done = bf16[2,128,2048]{2,1,0:T(8,128)(2,1)} async-done(((bf16[2,512,2048]{2,1,0:T(8,128)(2,1)}), bf16[2,128,2048]{2,1,0:T(8,128)(2,1)}) %reduce-scatter.17.cloned.1.call-update) | async-done | bytes 1048592 | tf_op jit(solution)/shard_map/reduce_scatter | solution.py:74
  1389.7 131.8 %reduce-scatter.37.cloned.1.call-done = f32[64,2]{1,0:T(8,128)} async-done(((f32[2048,2]{1,0:T(8,128)}), f32[64,2]{1,0:T(8,128)}) %reduce-scatter.37.cloned.1.call-update) | async-done | bytes 528
  (264 shorter events, 149.5 us)
Async XLA Ops:
  7.2 114.4 %all-gather.12.cloned.1.call-start = ((), (), s32[]{:S(2)}) async-start(), calls=%async_computation.13 | async-start | bytes 2359296 | tf_op jit(solution)/shard_map/all_gather | solution.py:77
  7.9 116.8 %all-gather.10.cloned.1.call-start = ((), (), s32[]{:S(2)}) async-start(), calls=%async_computation.12 | async-start | bytes 5242880 | tf_op jit(solution)/shard_map/all_gather | solution.py:70
  56.9 98.5 %all-gather.14.cloned.1.call-start = ((), (), s32[]{:S(2)}) async-start(), calls=%async_computation.14 | async-start | bytes 2359296 | tf_op jit(solution)/shard_map/all_gather | solution.py:77
  57.7 150.1 %reduce-scatter.15.cloned.1.call-start = ((), (), s32[]{:S(2)}) async-start(), calls=%async_computation.15 | async-start | bytes 5242880 | tf_op jit(solution)/shard_map/reduce_scatter | solution.py:74
  162.4 140.3 %all-gather.20.cloned.1.call-start = ((), (), s32[]{:S(2)}) async-start(), calls=%async_computation.18 | async-start | bytes 6488064 | tf_op jit(solution)/shard_map/all_gather | solution.py:77
  163.0 174.5 %all-gather.16.cloned.1.call-start = ((), (), s32[]{:S(2)}) async-start(), calls=%async_computation.16 | async-start | bytes 5242880 | tf_op jit(solution)/shard_map/all_gather | solution.py:70
  163.1 478.6 %copy-start.38 = (f32[2048]{0:T(1024)}, f32[2048]{0:T(1024)S(1)}, u32[]{:S(2)}) copy-start(f32[2048]{0:T(1024)S(1)} %convert_element_type.278) | copy-start | bytes 24580
  209.5 432.2 %copy-start.50 = (f32[2,128]{1,0:T(2,128)}, f32[2,128]{1,0:T(2,128)S(1)}, u32[]{:S(2)}) copy-start(f32[2,128]{1,0:T(2,128)S(1)} %add_rsqrt_fusion) | copy-start | bytes 3076
  212.1 220.5 %all-gather.18.cloned.1.call-start = ((), (), s32[]{:S(2)}) async-start(), calls=%async_computation.17 | async-start | bytes 6488064 | tf_op jit(solution)/shard_map/all_gather | solution.py:77
  212.8 254.1 %all-gather.24.cloned.1.call-start = ((), (), s32[]{:S(2)}) async-start(), calls=%async_computation.21 | async-start | bytes 5242880 | tf_op jit(solution)/shard_map/all_gather | solution.py:70
  213.6 348.5 %all-gather.22.cloned.1.call-start = ((), (), s32[]{:S(2)}) async-start(), calls=%async_computation.19 | async-start | bytes 6488064 | tf_op jit(solution)/shard_map/all_gather | solution.py:77
  214.3 424.7 %reduce-scatter.19.cloned.1.call-start = ((), (), s32[]{:S(2)}) async-start(), calls=%async_computation.22 | async-start | bytes 5242880 | tf_op jit(solution)/shard_map/reduce_scatter | solution.py:74
  596.1 85.3 %all-gather.26.cloned.1.call-start = ((), (), s32[]{:S(2)}) async-start(), calls=%async_computation.23 | async-start | bytes 5242880 | tf_op jit(solution)/shard_map/all_gather | solution.py:70
  645.4 148.5 %reduce-scatter.35.cloned.1.call-start = ((), (), s32[]{:S(2)}) async-start(), calls=%async_computation.31 | async-start | bytes 6488064 | tf_op jit(solution)/shard_map/reduce_scatter | solution.py:80
  656.0 251.4 %reduce-scatter.33.cloned.1.call-start = ((), (), s32[]{:S(2)}) async-start(), calls=%async_computation.30 | async-start | bytes 6488064 | tf_op jit(solution)/shard_map/reduce_scatter | solution.py:80
  668.7 352.0 %reduce-scatter.31.cloned.1.call-start = ((), (), s32[]{:S(2)}) async-start(), calls=%async_computation.29 | async-start | bytes 6488064 | tf_op jit(solution)/shard_map/reduce_scatter | solution.py:80
  681.4 404.5 %reduce-scatter.27.cloned.1.call-start = ((), (), s32[]{:S(2)}) async-start(), calls=%async_computation.27 | async-start | bytes 294912 | tf_op jit(solution)/shard_map/reduce_scatter | solution.py:80
  739.2 411.2 %reduce-scatter.25.cloned.1.call-start = ((), (), s32[]{:S(2)}) async-start(), calls=%async_computation.26 | async-start | bytes 294912 | tf_op jit(solution)/shard_map/reduce_scatter | solution.py:80
  743.3 477.2 %reduce-scatter.29.cloned.1.call-start = ((), (), s32[]{:S(2)}) async-start(), calls=%async_computation.28 | async-start | bytes 2359296 | tf_op jit(solution)/shard_map/reduce_scatter | solution.py:80
  749.6 541.7 %reduce-scatter.23.cloned.1.call-start = ((), (), s32[]{:S(2)}) async-start(), calls=%async_computation.25 | async-start | bytes 2359296 | tf_op jit(solution)/shard_map/reduce_scatter | solution.py:80
  766.8 570.5 %reduce-scatter.21.cloned.1.call-start = ((), (), s32[]{:S(2)}) async-start(), calls=%async_computation.24 | async-start | bytes 5242880 | tf_op jit(solution)/shard_map/reduce_scatter | solution.py:74
  775.4 609.0 %reduce-scatter.17.cloned.1.call-start = ((), (), s32[]{:S(2)}) async-start(), calls=%async_computation.20 | async-start | bytes 5242880 | tf_op jit(solution)/shard_map/reduce_scatter | solution.py:74
  788.2 549.1 %copy-start.4 = (bf16[2,128,2048]{2,1,0:T(8,128)(2,1)S(1)}, bf16[2,128,2048]{2,1,0:T(8,128)(2,1)}, u32[]{:S(2)}) copy-start(bf16[2,128,2048]{2,1,0:T(8,128)(2,1)} %param.12) | copy-start | bytes 3145732
  788.3 549.1 %copy-start.46 = (f32[2048]{0:T(1024)S(1)}, f32[2048]{0:T(1024)}, u32[]{:S(2)}) copy-start(f32[2048]{0:T(1024)} %copy-done.45) | copy-start | bytes 24580
  788.3 549.1 %copy-start.53 = (f32[2,128]{1,0:T(2,128)S(1)}, f32[2,128]{1,0:T(2,128)}, u32[]{:S(2)}) copy-start(f32[2,128]{1,0:T(2,128)} %copy-done.52) | copy-start | bytes 3076
  788.3 733.2 %reduce-scatter.37.cloned.1.call-start = ((), (), s32[]{:S(2)}) async-start(), calls=%async_computation.32 | async-start | bytes 1081344
  796.4 542.9 %copy-start.47 = (f32[2048]{0:T(1024)S(1)}, f32[2048]{0:T(1024)}, u32[]{:S(2)}) copy-start(f32[2048]{0:T(1024)} %get-tuple-element.44) | copy-start | bytes 24580
  909.7 474.8 %copy-start.6 = (bf16[2,128,2048]{2,1,0:T(8,128)(2,1)S(1)}, bf16[2,128,2048]{2,1,0:T(8,128)(2,1)}, u32[]{:S(2)}) copy-start(bf16[2,128,2048]{2,1,0:T(8,128)(2,1)} %reduce-scatter.15.cloned.1.call-done) | copy-start | bytes 3145732
  909.7 474.8 %copy-start.8 = (bf16[2,128,2048]{2,1,0:T(8,128)(2,1)S(1)}, bf16[2,128,2048]{2,1,0:T(8,128)(2,1)}, u32[]{:S(2)}) copy-start(bf16[2,128,2048]{2,1,0:T(8,128)(2,1)} %param.14) | copy-start | bytes 3145732
  909.7 474.8 %copy-start.39 = (f32[2048]{0:T(1024)S(1)}, f32[2048]{0:T(1024)}, u32[]{:S(2)}) copy-start(f32[2048]{0:T(1024)} %copy-done.38) | copy-start | bytes 24580
  909.7 474.8 %copy-start.51 = (f32[2,128]{1,0:T(2,128)S(1)}, f32[2,128]{1,0:T(2,128)}, u32[]{:S(2)}) copy-start(f32[2,128]{1,0:T(2,128)} %copy-done.50) | copy-start | bytes 3076
  909.7 474.8 %copy-start.56 = (f32[2,128]{1,0:T(2,128)S(1)}, f32[2,128]{1,0:T(2,128)}, u32[]{:S(2)}) copy-start(f32[2,128]{1,0:T(2,128)} %copy-done.55) | copy-start | bytes 3076
  (57 other events, 973.4 us)
Sparse Core Ops, SparseCore 0:
  10.2 53.2 all-gather.11
  65.6 32.9 all-gather.9
  100.7 48.8 all-gather.13
  162.5 45.2 reduce-scatter.14
  210.1 92.6 all-gather.19
  304.8 32.6 all-gather.15
  339.9 92.6 all-gather.17
  434.2 32.6 all-gather.23
  469.4 92.6 all-gather.21
  596.3 42.6 reduce-scatter.18
  645.6 34.4 all-gather.25
  683.6 110.2 reduce-scatter.34
  797.5 109.7 reduce-scatter.32
  910.9 109.7 reduce-scatter.30
  1024.4 61.4 reduce-scatter.26
  1089.7 60.7 reduce-scatter.24
  1153.8 66.7 reduce-scatter.28
  1224.5 66.7 reduce-scatter.22
  1293.8 43.5 reduce-scatter.20
  1339.9 44.4 reduce-scatter.16
  1386.7 134.7 reduce-scatter.36

commit v2 on v1

v2 whole, which is shorter than its diff:
```python
import jax
import jax.numpy as jnp
from jax import lax
from jax.experimental import pallas as pl
from jax.experimental.pallas import tpu as pltpu
from jax.sharding import PartitionSpec as P

HD = 64
EPS = 1e-05
THETA = 10000.0
NEGATIVE = -1e30
BF = jnp.bfloat16
F32 = jnp.float32


def rope_tables(positions):
    half_dim = HD // 2
    frequency = THETA ** (-(jnp.arange(half_dim).astype(F32) * (2.0 / HD)))
    angles = positions.astype(F32)[:, None] * frequency[None, :]
    return (jnp.cos(angles), jnp.sin(angles))


def rotate(values, cosine, sine_table):
    half_dim = values.shape[-1] // 2
    c = cosine[:, None, :]
    s = sine_table[:, None, :]
    a = values[..., :half_dim]
    b = values[..., half_dim:]
    return jnp.concatenate([a * c - b * s, b * c + a * s], axis=-1)


def unrotate(gradient, cosine, sine_table):
    return rotate(gradient, cosine, -sine_table)


def normalize(hidden, gain_vec):
    inverse = lax.rsqrt(jnp.mean(hidden * hidden, axis=-1, keepdims=True) + EPS)
    return (hidden * inverse * gain_vec, inverse)


def normalize_back(hidden, inverse, gain_vec, gradient):
    unit_rows = hidden * inverse
    gain_grad = jnp.sum(gradient * unit_rows, axis=0)
    weighted = gradient * gain_vec
    return (
        inverse * (weighted - unit_rows * jnp.mean(weighted * unit_rows, axis=-1, keepdims=True)),
        gain_grad,
    )


def project(a, b):
    return jnp.dot(a, b, preferred_element_type=F32)


def project_back(a, b):
    return lax.dot_general(a, b, (((1,), (1,)), ((), ())), preferred_element_type=F32)


def outer_sum(a, b):
    return lax.dot_general(a, b, (((0,), (0,)), ((), ())), preferred_element_type=F32)


MESH_ID = pl.DeviceIdType.MESH
HBM = pl.BlockSpec(memory_space=pl.ANY)


def gather_kernel(x_ref, c_ref, *refs):
    count = (len(refs) - 5) // 2
    shards, refs = refs[:count], refs[count:]
    x_full, c_full, refs = refs[0], refs[1], refs[2:]
    fulls, (send, recv, local) = refs[:count], refs[count:]
    rows = x_ref.shape[1]
    dp, sq = lax.axis_index("dp"), lax.axis_index("seq")
    across = [(lax.rem(dp + 2 * r, 8), sq) for r in range(4)]
    x_peer = (dp + 1 - 2 * lax.rem(dp, 2), sq)
    core_peer = (dp, sq + 1 - 2 * lax.rem(sq, 2))
    y_peer = (dp, lax.rem(sq + 2, 4))
    peers = across[1:] + [x_peer, core_peer, y_peer]
    barrier = pltpu.get_barrier_semaphore()
    for peer in peers:
        pl.semaphore_signal(barrier, inc=1, device_id=peer, device_id_type=MESH_ID)
    pl.semaphore_wait(barrier, len(peers))
    remote, own = [], []

    def put(src, dst, peer):
        i = len(remote)
        copy = pltpu.make_async_remote_copy(
            src_ref=src,
            dst_ref=dst,
            send_sem=send.at[i],
            recv_sem=recv.at[i],
            device_id=peer,
            device_id_type=MESH_ID,
        )
        copy.start()
        remote.append([copy, False])
        return i

    def arrived(i):
        remote[i][0].wait_recv()
        remote[i][1] = True

    def keep(src, dst):
        copy = pltpu.make_async_copy(src, dst, local.at[len(own)])
        copy.start()
        own.append(copy)

    def part(full, k):
        return full.at[:, pl.ds(k * rows, rows)]

    def seq_start(src, full):
        i = put(src, part(full, 1), y_peer)
        put(src, part(full, 2), core_peer)
        keep(src, part(full, 0))
        return i

    def seq_forward(full, i):
        arrived(i)
        put(part(full, 1), part(full, 3), core_peer)

    def z_start(i):
        keep(shards[i], fulls[i].at[0, 0])
        copies = [put(shards[i], fulls[i].at[0, r], across[4 - r]) for r in (1, 2, 3)]
        put(shards[i], fulls[i].at[1, 0], x_peer)
        return copies

    def x_forward(i, copies):
        for r in (1, 3, 2):
            arrived(copies[r - 1])
            put(fulls[i].at[0, r], fulls[i].at[1, r], x_peer)

    xs = seq_start(x_ref, x_full)
    zs = [z_start(0), z_start(1)]
    seq_forward(x_full, xs)
    x_forward(0, zs[0])
    cs = seq_start(c_ref, c_full)
    zs.append(z_start(2))
    x_forward(1, zs[1])
    zs.append(z_start(3))
    seq_forward(c_full, cs)
    x_forward(2, zs[2])
    zs.append(z_start(4))
    x_forward(3, zs[3])
    x_forward(4, zs[4])
    for copy, seen in remote:
        copy.wait_send()
        if not seen:
            copy.wait_recv()
    for copy in own:
        copy.wait()


def gather_all(x, c, shards):
    micro, rows, d = x.shape
    tokens = jax.ShapeDtypeStruct((micro, 4 * rows, d), x.dtype)
    fulls = [jax.ShapeDtypeStruct((2, 4) + w.shape, w.dtype) for w in shards]
    outs = pl.pallas_call(
        gather_kernel,
        out_shape=[tokens, tokens] + fulls,
        in_specs=[HBM] * (2 + len(shards)),
        out_specs=[HBM] * (2 + len(shards)),
        scratch_shapes=[pltpu.SemaphoreType.DMA((48,)), pltpu.SemaphoreType.DMA((48,)), pltpu.SemaphoreType.DMA((8,))],
        compiler_params=pltpu.CompilerParams(collective_id=0, has_side_effects=True),
    )(x, c, *shards)
    return outs[0], outs[1], [w.reshape(-1, w.shape[-1]) for w in outs[2:]]


class Mesh2D:
    n = 8

    def shift_x(self, a):
        return lax.ppermute(a, "dp", [(i, i ^ 1) for i in range(8)])

    def shift_z(self, a, r):
        return lax.ppermute(a, "dp", [(i, (i + 2 * r) % 8) for i in range(8)])

    def gather(self, x, c, shards):
        return gather_all(x, c, shards)

    def gather_gains(self, g):
        g = jnp.zeros((2, 4, g.shape[1]), F32).at[:, lax.axis_index("seq")].set(g).reshape(2, -1)
        g = g + shift_core(g)
        g = g + shift_y(g)
        g = jnp.concatenate([g, self.shift_x(g)], axis=0)
        g = jnp.stack([g] + [self.shift_z(g, -r) for r in (1, 2, 3)])
        return jnp.transpose(g.reshape(4, 2, 2, -1), (2, 1, 0, 3)).reshape(2, -1)

    def scatter_gain(self, g):
        g = g.reshape(2, -1)
        g = (g[0] + self.shift_x(g[1])).reshape(4, -1)
        g = g[0] + self.shift_z(g[1], 1) + self.shift_z(g[2], 2) + self.shift_z(g[3], 3)
        g = g + shift_core(g)
        g = g + shift_y(g)
        size = g.shape[0] // 4
        return lax.dynamic_slice_in_dim(g, lax.axis_index("seq") * size, size, 0)

    def scatter(self, left, right):
        half = left.shape[1] // 2
        far = outer_sum(left[:, half:], right).astype(BF)
        got = self.shift_x(far)
        near = (outer_sum(left[:, :half], right) + got.astype(F32)).astype(BF)
        blocks = near.reshape(4, half // 4, -1)
        total = blocks[0].astype(F32)
        for r in (1, 2, 3):
            total = total + self.shift_z(blocks[r], r).astype(F32)
        return total

    def to_relative(self, a):
        dp = lax.axis_index("dp")
        z, x = dp // 2, dp % 2
        lead = a.shape[:-1]
        a = a.reshape(lead + (4, 2, -1))
        a = jnp.where(x == 0, a, jnp.flip(a, -2))
        a = lax.dynamic_slice_in_dim(jnp.concatenate([a, a], -3), z, 4, len(lead))
        return jnp.swapaxes(a, -2, -3).reshape(lead + (-1,))

    def from_relative(self, a):
        dp = lax.axis_index("dp")
        z, x = dp // 2, dp % 2
        lead = a.shape[:-1]
        a = jnp.swapaxes(a.reshape(lead + (2, 4, -1)), -2, -3)
        a = jnp.where(x == 0, a, jnp.flip(a, -2))
        a = lax.dynamic_slice_in_dim(jnp.concatenate([a, a], -3), 4 - z, 4, len(lead))
        return a.reshape(lead + (-1,))


class AnyMesh:
    def gather(self, x, c, shards):
        fulls = [lax.all_gather(w, "dp", axis=0, tiled=True) for w in shards]
        return gather_rows(x), gather_rows(c), fulls

    def gather_gains(self, g):
        return lax.all_gather(g, ("dp", "seq"), axis=1, tiled=True)

    def scatter_gain(self, g):
        return lax.psum_scatter(g, ("dp", "seq"), scatter_dimension=0, tiled=True)

    def scatter(self, left, right):
        return lax.psum_scatter(
            outer_sum(left, right).astype(BF), "dp", scatter_dimension=0, tiled=True
        ).astype(F32)

    def to_relative(self, a):
        return a

    def from_relative(self, a):
        return a


def shift_core(a):
    return lax.ppermute(a, "seq", [(i, i ^ 1) for i in range(4)])


def shift_y(a):
    return lax.ppermute(a, "seq", [(i, i ^ 2) for i in range(4)])


def gather_rows(a):
    across = shift_y(a)
    return jnp.concatenate([a, across, shift_core(a), shift_core(across)], axis=-2)


def scatter_rows(make):
    got = shift_core(make(1).astype(BF))
    near = make(0) + got.astype(F32)
    rows = near.shape[1] // 2
    got = shift_y(near[:, rows:].astype(BF))
    return near[:, :rows] + got.astype(F32)


def per_device(
    inputs, segments, cotangent, attn_gain, w_query, w_key, w_value, w_out, mlp_gain, w_gate, w_up, w_down,
):
    micro, rows, d = inputs.shape
    seq = lax.axis_size("seq")
    length = rows * seq
    full = micro * length
    half = length // 2
    grid = Mesh2D() if lax.axis_size("dp") == 8 else AnyMesh()

    nq, nk = w_query.shape[1], w_key.shape[1]
    heads, kv_heads = nq // HD, nk // HD
    groups = heads // kv_heads
    w_qkv = jnp.concatenate([w_query, w_key, w_value], axis=1)

    inputs = grid.to_relative(inputs)
    cotangent = grid.to_relative(cotangent)
    gains = grid.gather_gains(jnp.stack([attn_gain, mlp_gain]).astype(F32))
    gain_a, gain_m = gains[0], gains[1]

    shards = [w_qkv, w_out, w_gate, w_up, w_down]
    x_full, up_full, (wqkv, wo, wg, wu, wd) = grid.gather(inputs, cotangent, shards)

    me = lax.axis_index("seq")
    order = [me, me ^ 2, me ^ 1, me ^ 3]
    pos = jnp.concatenate([j * rows + jnp.arange(rows, dtype=jnp.int32) for j in order])
    segs = jnp.concatenate([lax.dynamic_slice_in_dim(segments, j * rows, rows, 1) for j in order], axis=1)
    cosine, sine = rope_tables(pos)
    cos_f, sin_f = jnp.tile(cosine, (micro, 1)), jnp.tile(sine, (micro, 1))
    allowed = (pos[None, :] <= pos[:, None])[None] & (segs[:, :, None] == segs[:, None, :])
    allowed = allowed[:, None, None]

    def pieces(make):
        return lambda i: make(slice(i * half, (i + 1) * half)).reshape(micro, half, d)

    def rows_of(a, s):
        return a.reshape(micro, length, -1)[:, s].reshape(micro * half, -1)

    hidden_full = x_full.reshape(full, d).astype(F32)
    normed, inverse_f = normalize(hidden_full, gain_a)
    na = normed.astype(BF)
    hidden = inputs.astype(F32)
    upstream = cotangent.astype(F32)
    up_full = up_full.reshape(full, d)

    def rope(x, n, s):
        return rotate(x.reshape(full, n, HD), cos_f, s).astype(BF).reshape(full, n * HD)

    qkv = project(na, wqkv)
    q = rope(qkv[:, :nq], heads, sin_f)
    k = rope(qkv[:, nq : nq + nk], kv_heads, sin_f)
    v = qkv[:, nq + nk :].astype(BF)
    qg = q.reshape(micro, length, kv_heads, groups, HD)
    kg = k.reshape(micro, length, kv_heads, HD)
    vg = v.reshape(micro, length, kv_heads, HD)
    scores = jnp.einsum("mqkgd,mpkd->mkgqp", qg, kg, preferred_element_type=F32) * HD ** (-0.5)
    scores = jnp.where(allowed, scores, NEGATIVE)
    maximum = jnp.max(scores, axis=-1, keepdims=True)
    weights = jnp.where(allowed, jnp.exp(scores - maximum), 0.0)
    denominator = jnp.sum(weights, axis=-1, keepdims=True)
    prob = weights / denominator
    prob_b = prob.astype(BF)
    attended = jnp.einsum("mkgqp,mpkd->mqkgd", prob_b, vg, preferred_element_type=F32)
    attended = attended.astype(BF).reshape(full, heads * HD)
    residual = hidden + scatter_rows(pieces(lambda s: project_back(rows_of(attended, s), wo)))
    normed, inverse_m = normalize(residual, gain_m)
    nm = gather_rows(normed.astype(BF)).reshape(full, d)
    gate_pre = project(nm, wg)
    up_proj = project(nm, wu)
    sigmoid_g = jax.nn.sigmoid(gate_pre)
    active = gate_pre * sigmoid_g
    product = (active * up_proj).astype(BF)
    g_down = grid.scatter(up_full, product)
    d_product = project(up_full, wd)
    d_gate = (d_product * up_proj * sigmoid_g * (1.0 + gate_pre * (1.0 - sigmoid_g))).astype(BF)
    d_up = (d_product * active).astype(BF)
    d_nm = scatter_rows(
        pieces(lambda s: project_back(rows_of(d_gate, s), wg) + project_back(rows_of(d_up, s), wu))
    )
    g_gate = grid.scatter(nm, d_gate)
    g_up = grid.scatter(nm, d_up)
    output = (residual + scatter_rows(pieces(lambda s: project_back(rows_of(product, s), wd)))).astype(BF)
    flat = lambda a: a.reshape(micro * rows, -1)
    d_norm_m, g_gain_m = normalize_back(flat(residual), flat(inverse_m), gain_m, flat(d_nm))
    d_residual = upstream + d_norm_m.reshape(micro, rows, d)
    dr = gather_rows(d_residual.astype(BF)).reshape(full, d)
    d_att = project(dr, wo).astype(BF)
    dg = d_att.reshape(micro, length, kv_heads, groups, HD)
    d_values = jnp.einsum("mkgqp,mqkgd->mpkd", prob_b, dg, preferred_element_type=F32)
    d_prob = jnp.einsum("mqkgd,mpkd->mkgqp", dg, vg, preferred_element_type=F32)
    row_sum = jnp.sum(prob * d_prob, axis=-1, keepdims=True)
    d_scores = (prob * (d_prob - row_sum) * HD ** (-0.5)).astype(BF)
    d_query = jnp.einsum("mkgqp,mpkd->mqkgd", d_scores, kg, preferred_element_type=F32)
    d_keys = jnp.einsum("mkgqp,mqkgd->mpkd", d_scores, qg, preferred_element_type=F32)
    dq = rope(d_query, heads, -sin_f)
    dk = rope(d_keys, kv_heads, -sin_f)
    dv = d_values.astype(BF).reshape(full, kv_heads * HD)
    dqkv = jnp.concatenate([dq, dk, dv], axis=1)
    g_out = grid.scatter(dr, attended)
    d_na = scatter_rows(pieces(lambda s: project_back(rows_of(dqkv, s), wqkv)))
    g_qkv = grid.scatter(na, dqkv)
    inverse_a = inverse_f.reshape(micro, length, 1)[:, :rows]
    d_norm_a, g_gain_a = normalize_back(flat(hidden), flat(inverse_a), gain_a, flat(d_na))
    d_input = d_residual + d_norm_a.reshape(micro, rows, d)
    return (
        grid.from_relative(output),
        grid.from_relative(d_input),
        grid.scatter_gain(g_gain_a),
        g_qkv[:, :nq],
        g_qkv[:, nq : nq + nk],
        g_qkv[:, nq + nk :],
        g_out,
        grid.scatter_gain(g_gain_m),
        g_gate,
        g_up,
        g_down,
    )


def solution(mesh):
    tok, wt, gn = P(None, ("dp", "seq"), None), P("dp", "seq"), P(("dp", "seq"))
    return jax.shard_map(
        per_device,
        mesh=mesh,
        in_specs=(tok, P(None, "dp"), tok, gn, wt, wt, wt, wt, gn, wt, wt, wt),
        out_specs=(tok, tok, gn, wt, wt, wt, wt, gn, wt, wt, wt),
        check_vma=False,
    )
```

time: 1540 us -> 987 us (0.64)
  waiting for transfers between devices: 1130 us -> 283 us
  Pallas kernels: 0 us -> 273 us
  starting transfers between devices: 1.24 us -> 136 us
  blocking collectives: 104 us -> 0 us
  matrix products: 193 us -> 155 us
  other arithmetic: 50.2 us -> 71.2 us
  local copies, waits for them, and re-layouts: 39.3 us -> 57.2 us
    reduce_scatter x11 -> x0, waiting for transfers between devices: 667 us -> none  [the longest x7 491 us: scatter_w(): lax.psum_scatter(g.astype(BF), 'dp', scatter_dimension=0, tiled=True)]
    all_gather x9 -> x0, waiting for transfers between devices: 324 us -> none  [the longest x5 267 us: gather_w(): return lax.all_gather(w, 'dp', axis=0, tiled=True)]
    ppermute x0 -> x52, waiting for transfers between devices: none -> 283 us  [the longest x8 125 us: shift_x(): return lax.ppermute(a, 'dp', [(i, i ^ 1) for i in range(8)])]
    pallas_call x0 -> x1, Pallas kernels: none -> 273 us  [gather_all(): pl.pallas_call(gather_kernel, out_shape=[tokens, tokens] + fulls, in_spec...]
    unnamed x22 -> x0, waiting for transfers between devices: 136 us -> none
    ppermute x0 -> x52, starting transfers between devices: none -> 136 us  [the longest x24 118 us: shift_z(): return lax.ppermute(a, 'dp', [(i, (i + 2 * r) % 8) for i in range(8)])]
    all_gather x2 -> x0, blocking collectives: 61.8 us -> none  [gather_w(): return lax.all_gather(w, 'dp', axis=0, tiled=True)]
    unnamed x1 -> x0, blocking collectives: 42.6 us -> none
  transfers between devices with their start and end apart: 21 -> 52, of which waited for: 17 -> 20; matrix products, arithmetic and copies ran while one was open for 14% -> 22% of each run, Pallas kernels for 0% -> 28%
where the time goes in v2:
time: 987 us; the launch traced here: 979 us
  waiting for transfers between devices  283 us (29%)
  Pallas kernels  273 us (28%)
  matrix products  155 us (16%)
  starting transfers between devices  136 us (14%)
  other arithmetic  71.2 us (7%)
  local copies, waits for them, and re-layouts  57.2 us (6%)
    pallas_call x1, Pallas kernels, gather_all(): pl.pallas_call(gather_kernel, out_shape=[tokens, tokens] + fulls, in_spec...  273 us
    ppermute x8, waiting for transfers between devices, shift_x(): return lax.ppermute(a, 'dp', [(i, i ^ 1) for i in range(8)])  125 us
    ppermute x24, starting transfers between devices, shift_z(): return lax.ppermute(a, 'dp', [(i, (i + 2 * r) % 8) for i in range(8)])  118 us
    ppermute x24, waiting for transfers between devices, shift_z(): return lax.ppermute(a, 'dp', [(i, (i + 2 * r) % 8) for i in range(8)])  79.5 us
    ppermute x9, waiting for transfers between devices, shift_y(): return lax.ppermute(a, 'seq', [(i, i ^ 2) for i in range(4)])  73.5 us
    dot_general x10, matrix products, project_back(): lax.dot_general(a, b, (((1,), (1,)), ((), ())), preferred_element_type=F32)  48.3 us
    dot_general x10, matrix products, outer_sum(): lax.dot_general(a, b, (((0,), (0,)), ((), ())), preferred_element_type=F32)  39.6 us
    dot_general x5, matrix products, project(): return jnp.dot(a, b, preferred_element_type=F32)  35.6 us
  transfers between devices with their start and end apart: 52, of which 20 were waited for; matrix products, arithmetic and copies ran while one was open for 22% of the time, Pallas kernels for 28%

profile of v2, /device:TPU:0, one launch (start us, length us, event | category | flops | bytes accessed | tf_op | source)
XLA Modules:
  0.0 979.3 jit_solution(17727011734005890018)
XLA Ops:
  18.8 273.3 %shard_map.203 = (bf16[2,512,2048]{2,1,0:T(8,128)(2,1)}, bf16[2,512,2048]{2,1,0:T(8,128)(2,1)}, bf16[2,4,256,640]{3,2,1,0:T(8,128)(2,1)}, bf16[2,4,256,512]{3,2,...) custom-call(bf16[2,128,2048]{2,1,0:T(8,128)(2,1)} %reshape.712.x_ref, ...), custom_call_target="tpu_custom_call" | custom-call | tf_op jit(solution)/shard_map/pallas_call | solution.py:157
  296.0 5.1 collective-permute-start.1
  306.3 39.9 %collective-permute-start.4 = (f32[4,256]{1,0:T(4,128)S(1)}, f32[4,256]{1,0:T(4,128)S(1)}, u32[]{:S(2)}, u32[]{:S(2)}) collective-permute-start(f32[4,256]{1,0:T(4,128)S(1)} %pad_maximum_fusion.7), channel_id=1, source_target_pairs={{0,16},{4,20},{8,24},{12,28},{16,0},{20,4},{24,8},{28,12},{1,17},{... | collective-permute-start | bytes 12296 | tf_op jit(solution)/shard_map/ppermute | solution.py:175
  367.9 5.5 fusion.49
  380.6 25.2 %collective-permute-done.7 = bf16[2,128,2048]{2,1,0:T(8,128)(2,1)S(1)} collective-permute-done((bf16[2,128,2048]{2,1,0:T(8,128)(2,1)S(1)}, bf16[2,128,2048]{2,1,0:T(8,128)(2,1)S(1)}, u32[]{:S(2)}, u32[]{:S(2)}) %collective-permute-start.7) | collective-permute-done | bytes 1048608 | tf_op jit(solution)/shard_map/ppermute | solution.py:255
  406.9 24.2 %collective-permute-done.8 = bf16[2,128,2048]{2,1,0:T(8,128)(2,1)} collective-permute-done((bf16[2,128,2048]{2,1,0:T(8,128)(2,1)S(1)}, bf16[2,128,2048]{2,1,0:T(8,128)(2,1)}, u32[]{:S(2)}, u32[]{:S(2)}) %collective-permute-start.8) | collective-permute-done | bytes 1048608 | tf_op jit(solution)/shard_map/ppermute | solution.py:255
  431.2 8.4 fusion.110
  449.8 8.5 fusion.109
  458.4 13.3 %multiply_convert_fusion.1 = (bf16[1024,1408]{1,0:T(8,128)(2,1)S(1)}, bf16[1024,1408]{1,0:T(8,128)(2,1)S(1)}, bf16[1024,1408]{1,0:T(8,128)(2,1)S(1)}) fusion(f32[1024,1408]{1,0:T(8,128)} %fusion.110, f32[1024,1408]{1,0:T(8,128)} %fusion.109, bf16[1024,2048]{1,0:T(8,128)(2,1)S(1)} %bitcast.236, bf16[2048,1408]{1,0:T(8,128)(2,1)} %bitcast.302), kind=kOutput, calls=%fused_computation.25 | convolution fusion | flops 5927206912 | bytes 30146560 | tf_op jit(solution)/shard_map/dot_general | solution.py:52
  494.3 7.3 add_convert_fusion.3
  501.7 7.9 convolution_convert_fusion.5
  510.0 7.7 fusion.111
  517.7 7.0 convolution_add_fusion
  527.0 7.1 convert_add_fusion.2
  535.1 7.0 collective-permute-done.48
  542.1 7.0 add_convert_fusion
  549.1 54.8 %collective-permute-done.44 = bf16[1024,1408]{1,0:T(8,128)(2,1)} collective-permute-done((bf16[1024,1408]{1,0:T(8,128)(2,1)}, bf16[1024,1408]{1,0:T(8,128)(2,1)}, u32[]{:S(2)}, u32[]{:S(2)}) %collective-permute-start.44) | collective-permute-done | bytes 2883616 | tf_op jit(solution)/shard_map/ppermute | solution.py:172
  603.9 5.1 add_convert_fusion.1
  609.1 56.2 %collective-permute-done.40 = bf16[1024,1408]{1,0:T(8,128)(2,1)} collective-permute-done((bf16[1024,1408]{1,0:T(8,128)(2,1)}, bf16[1024,1408]{1,0:T(8,128)(2,1)}, u32[]{:S(2)}, u32[]{:S(2)}) %collective-permute-start.40) | collective-permute-done | bytes 2883616 | tf_op jit(solution)/shard_map/ppermute | solution.py:172
  665.3 5.5 add_convert_fusion.2
  688.1 15.5 %collective-permute-done.15 = bf16[2,128,2048]{2,1,0:T(8,128)(2,1)S(1)} collective-permute-done((bf16[2,128,2048]{2,1,0:T(8,128)(2,1)}, bf16[2,128,2048]{2,1,0:T(8,128)(2,1)S(1)}, u32[]{:S(2)}, u32[]{:S(2)}) %collective-permute-start.15) | collective-permute-done | bytes 1048608 | tf_op jit(solution)/shard_map/ppermute | solution.py:255
  730.0 12.7 %fusion = (f32[2,8,512]{2,1,0:T(8,128)S(1)}, f32[2,512,512,8]{2,1,3,0:T(8,128)}) fusion(f32[2,8,512]{2,1,0:T(8,128)S(1)} %copy-done.47, f32[2,8,512]{2,1,0:T(8,128)S(1)} %copy-done.42, f32[2,512,512,8]{2,1,3,0:T(8,128)} %copy-done, pred[2,512,512]{1,2,0:T(8,128)(4,1)S(1)} %copy-done.6, bf16[2,512,8,64]{1,3,2,0:T(8,128)(2,1)S(1)} %copy.102, ...), kind=kOutput, calls=%fused_computation.3 | convolution fusion | flops 566222848 | bytes 35356672 | tf_op jit(solution)/shard_map/mqkgd,mpkd->mkgqp/dot_general | solution.py:360
  742.8 13.5 %fusion.7 = bf16[2,8,512,512]{2,3,1,0:T(8,128)(2,1)S(1)} fusion(f32[2,512,512,8]{2,1,3,0:T(8,128)} %get-tuple-element.133, f32[2,8,512]{2,1,0:T(8,128)S(1)} %get-tuple-element.132, f32[2,8,512]{2,1,0:T(8,128)S(1)} %copy-done.47, f32[2,8,512]{2,1,0:T(8,128)S(1)} %copy-done.42, f32[2,512,512,8]{2,1,3,0:T(8,128)} %copy-done, pred[2,512,512]{1,2,0:T(8,128)(4,1)S(1)} %copy-done.6), kind=kLoop, calls=%fused_computation.11 | loop fusion | flops 37748736 | bytes 42565632 | tf_op jit(solution)/shard_map/reshape.52
  762.0 5.6 fusion.65
  792.8 26.2 %collective-permute-done.46 = bf16[256,1408]{1,0:T(8,128)(2,1)} collective-permute-done((bf16[256,1408]{1,0:T(8,128)(2,1)}, bf16[256,1408]{1,0:T(8,128)(2,1)}, u32[]{:S(2)}, u32[]{:S(2)}) %collective-permute-start.46) | collective-permute-done | bytes 720928 | tf_op jit(solution)/shard_map/ppermute | solution.py:175
  819.0 12.1 %collective-permute-start.41 = (bf16[256,1408]{1,0:T(8,128)(2,1)S(1)}, bf16[256,1408]{1,0:T(8,128)(2,1)S(1)}, u32[]{:S(2)}, u32[]{:S(2)}) collective-permute-start(bf16[256,1408]{1,0:T(8,128)(2,1)S(1)} %copy-done.34), channel_id=1, source_target_pairs={{0,8},{4,12},{8,16},{12,20},{16,24},{20,28},{24,0},{28,4},{1,9},{5... | collective-permute-start | bytes 2162696 | tf_op jit(solution)/shard_map/ppermute | solution.py:175
  854.2 27.8 %collective-permute-done.42 = bf16[256,1408]{1,0:T(8,128)(2,1)S(1)} collective-permute-done((bf16[256,1408]{1,0:T(8,128)(2,1)S(1)}, bf16[256,1408]{1,0:T(8,128)(2,1)S(1)}, u32[]{:S(2)}, u32[]{:S(2)}) %collective-permute-start.42) | collective-permute-done | bytes 720928 | tf_op jit(solution)/shard_map/ppermute | solution.py:175
  882.0 23.2 %collective-permute-start.27 = (bf16[256,640]{0,1:T(8,128)(2,1)S(1)}, bf16[256,640]{0,1:T(8,128)(2,1)S(1)}, u32[]{:S(2)}, u32[]{:S(2)}) collective-permute-start(bf16[256,640]{0,1:T(8,128)(2,1)S(1)} %get-tuple-element.99), channel_id=1, source_target_pairs={{0,8},{4,12},{8,16},{12,20},{16,24},{20,28},{24,0},{28,4},{1,9},{5... | collective-permute-start | bytes 983048 | tf_op jit(solution)/shard_map/ppermute | solution.py:175
  905.2 9.2 collective-permute-start.28
  917.9 9.8 collective-permute-done.32
  931.7 8.6 collective-permute-done.28
  945.8 7.1 collective-permute-done.19
  (391 shorter events, 229.4 us)
Async XLA Ops:
  3.6 292.4 %collective-permute-start = (f32[2,256]{1,0:T(2,128)S(1)}, f32[2,256]{1,0:T(2,128)S(1)}, u32[]{:S(2)}, u32[]{:S(2)}) collective-permute-start(f32[2,256]{1,0:T(2,128)S(1)} %reshape.715), channel_id=1, source_target_pairs={{0,1},{1,0},{2,3},{3,2},{4,5},{5,4},{6,7},{7,6},{8,9},{9,8},{10,11... | collective-permute-start | bytes 6152 | tf_op jit(solution)/shard_map/ppermute | solution.py:251
  306.3 42.5 %collective-permute-start.3 = (f32[4,256]{1,0:T(4,128)S(1)}, f32[4,256]{1,0:T(4,128)S(1)}, u32[]{:S(2)}, u32[]{:S(2)}) collective-permute-start(f32[4,256]{1,0:T(4,128)S(1)} %pad_maximum_fusion.7), channel_id=1, source_target_pairs={{0,24},{4,28},{8,0},{12,4},{16,8},{20,12},{24,16},{28,20},{1,25},{... | collective-permute-start | bytes 12296 | tf_op jit(solution)/shard_map/ppermute | solution.py:175
  306.3 42.5 %collective-permute-start.4 = (f32[4,256]{1,0:T(4,128)S(1)}, f32[4,256]{1,0:T(4,128)S(1)}, u32[]{:S(2)}, u32[]{:S(2)}) collective-permute-start(f32[4,256]{1,0:T(4,128)S(1)} %pad_maximum_fusion.7), channel_id=1, source_target_pairs={{0,16},{4,20},{8,24},{12,28},{16,0},{20,4},{24,8},{28,12},{1,17},{... | collective-permute-start | bytes 12296 | tf_op jit(solution)/shard_map/ppermute | solution.py:175
  380.4 25.3 %collective-permute-start.7 = (bf16[2,128,2048]{2,1,0:T(8,128)(2,1)S(1)}, bf16[2,128,2048]{2,1,0:T(8,128)(2,1)S(1)}, u32[]{:S(2)}, u32[]{:S(2)}) collective-permute-start(bf16[2,128,2048]{2,1,0:T(8,128)(2,1)S(1)} %slice.532), channel_id=1, source_target_pairs={{0,2},{1,3},{2,0},{3,1},{4,6},{5,7},{6,4},{7,5},{8,10},{9,11},{10,... | collective-permute-start | bytes 3145736 | tf_op jit(solution)/shard_map/ppermute | solution.py:255
  406.6 24.5 %collective-permute-start.8 = (bf16[2,128,2048]{2,1,0:T(8,128)(2,1)S(1)}, bf16[2,128,2048]{2,1,0:T(8,128)(2,1)}, u32[]{:S(2)}, u32[]{:S(2)}) collective-permute-start(bf16[2,128,2048]{2,1,0:T(8,128)(2,1)S(1)} %multiply_convert_fusion.4), channel_id=1, source_target_pairs={{0,2},{1,3},{2,0},{3,1},{4,6},{5,7},{6,4},{7,5},{8,10},{9,11},{10,... | collective-permute-start | bytes 3145736 | tf_op jit(solution)/shard_map/ppermute | solution.py:255
  406.9 40.8 %collective-permute-start.9 = (bf16[2,128,2048]{2,1,0:T(8,128)(2,1)S(1)}, bf16[2,128,2048]{2,1,0:T(8,128)(2,1)}, u32[]{:S(2)}, u32[]{:S(2)}) collective-permute-start(bf16[2,128,2048]{2,1,0:T(8,128)(2,1)S(1)} %multiply_convert_fusion.4), channel_id=1, source_target_pairs={{0,1},{1,0},{2,3},{3,2},{4,5},{5,4},{6,7},{7,6},{8,9},{9,8},{10,11... | collective-permute-start | bytes 3145736 | tf_op jit(solution)/shard_map/ppermute | solution.py:251
  476.5 65.6 %collective-permute-start.48 = (bf16[1024,1408]{1,0:T(8,128)(2,1)}, bf16[1024,1408]{1,0:T(8,128)(2,1)}, u32[]{:S(2)}, u32[]{:S(2)}) collective-permute-start(bf16[1024,1408]{1,0:T(8,128)(2,1)} %convolution_convert_fusion), channel_id=1, source_target_pairs={{0,4},{4,0},{8,12},{12,8},{16,20},{20,16},{24,28},{28,24},{1,5},{5... | collective-permute-start | bytes 8650760 | tf_op jit(solution)/shard_map/ppermute | solution.py:172
  481.9 122.0 %collective-permute-start.44 = (bf16[1024,1408]{1,0:T(8,128)(2,1)}, bf16[1024,1408]{1,0:T(8,128)(2,1)}, u32[]{:S(2)}, u32[]{:S(2)}) collective-permute-start(bf16[1024,1408]{1,0:T(8,128)(2,1)} %convolution_convert_fusion.1), channel_id=1, source_target_pairs={{0,4},{4,0},{8,12},{12,8},{16,20},{20,16},{24,28},{28,24},{1,5},{5... | collective-permute-start | bytes 8650760 | tf_op jit(solution)/shard_map/ppermute | solution.py:172
  488.2 177.1 %collective-permute-start.40 = (bf16[1024,1408]{1,0:T(8,128)(2,1)}, bf16[1024,1408]{1,0:T(8,128)(2,1)}, u32[]{:S(2)}, u32[]{:S(2)}) collective-permute-start(bf16[1024,1408]{1,0:T(8,128)(2,1)} %convolution_convert_fusion.2), channel_id=1, source_target_pairs={{0,4},{4,0},{8,12},{12,8},{16,20},{20,16},{24,28},{28,24},{1,5},{5... | collective-permute-start | bytes 8650760 | tf_op jit(solution)/shard_map/ppermute | solution.py:172
  525.4 145.5 %collective-permute-start.14 = (bf16[2,128,2048]{2,1,0:T(8,128)(2,1)S(1)}, bf16[2,128,2048]{2,1,0:T(8,128)(2,1)S(1)}, u32[]{:S(2)}, u32[]{:S(2)}) collective-permute-start(bf16[2,128,2048]{2,1,0:T(8,128)(2,1)S(1)} %slice.530), channel_id=1, source_target_pairs={{0,2},{1,3},{2,0},{3,1},{4,6},{5,7},{6,4},{7,5},{8,10},{9,11},{10,... | collective-permute-start | bytes 3145736 | tf_op jit(solution)/shard_map/ppermute | solution.py:255
  534.3 137.3 %collective-permute-start.12 = (bf16[2,128,2048]{2,1,0:T(8,128)(2,1)S(1)}, bf16[2,128,2048]{2,1,0:T(8,128)(2,1)}, u32[]{:S(2)}, u32[]{:S(2)}) collective-permute-start(bf16[2,128,2048]{2,1,0:T(8,128)(2,1)S(1)} %slice.531), channel_id=1, source_target_pairs={{0,2},{1,3},{2,0},{3,1},{4,6},{5,7},{6,4},{7,5},{8,10},{9,11},{10,... | collective-permute-start | bytes 3145736 | tf_op jit(solution)/shard_map/ppermute | solution.py:255
  678.7 25.0 %collective-permute-start.15 = (bf16[2,128,2048]{2,1,0:T(8,128)(2,1)}, bf16[2,128,2048]{2,1,0:T(8,128)(2,1)S(1)}, u32[]{:S(2)}, u32[]{:S(2)}) collective-permute-start(bf16[2,128,2048]{2,1,0:T(8,128)(2,1)} %get-tuple-element.74), channel_id=1, source_target_pairs={{0,2},{1,3},{2,0},{3,1},{4,6},{5,7},{6,4},{7,5},{8,10},{9,11},{10,... | collective-permute-start | bytes 3145736 | tf_op jit(solution)/shard_map/ppermute | solution.py:255
  683.5 33.2 %collective-permute-start.16 = (bf16[2,128,2048]{2,1,0:T(8,128)(2,1)}, bf16[2,128,2048]{2,1,0:T(8,128)(2,1)}, u32[]{:S(2)}, u32[]{:S(2)}) collective-permute-start(bf16[2,128,2048]{2,1,0:T(8,128)(2,1)} %get-tuple-element.74), channel_id=1, source_target_pairs={{0,1},{1,0},{2,3},{3,2},{4,5},{5,4},{6,7},{7,6},{8,9},{9,8},{10,11... | collective-permute-start | bytes 3145736 | tf_op jit(solution)/shard_map/ppermute | solution.py:251
  705.9 77.4 %collective-permute-start.49 = (bf16[256,1408]{1,0:T(8,128)(2,1)}, bf16[256,1408]{1,0:T(8,128)(2,1)}, u32[]{:S(2)}, u32[]{:S(2)}) collective-permute-start(bf16[256,1408]{1,0:T(8,128)(2,1)} %get-tuple-element.81), channel_id=1, source_target_pairs={{0,8},{4,12},{8,16},{12,20},{16,24},{20,28},{24,0},{28,4},{1,9},{5... | collective-permute-start | bytes 2162696 | tf_op jit(solution)/shard_map/ppermute | solution.py:175
  706.1 81.4 %collective-permute-start.50 = (bf16[256,1408]{1,0:T(8,128)(2,1)}, bf16[256,1408]{1,0:T(8,128)(2,1)}, u32[]{:S(2)}, u32[]{:S(2)}) collective-permute-start(bf16[256,1408]{1,0:T(8,128)(2,1)} %get-tuple-element.83), channel_id=1, source_target_pairs={{0,16},{4,20},{8,24},{12,28},{16,0},{20,4},{24,8},{28,12},{1,17},{... | collective-permute-start | bytes 2162696 | tf_op jit(solution)/shard_map/ppermute | solution.py:175
  713.2 75.9 %collective-permute-start.51 = (bf16[256,1408]{1,0:T(8,128)(2,1)}, bf16[256,1408]{1,0:T(8,128)(2,1)}, u32[]{:S(2)}, u32[]{:S(2)}) collective-permute-start(bf16[256,1408]{1,0:T(8,128)(2,1)} %get-tuple-element.82), channel_id=1, source_target_pairs={{0,24},{4,28},{8,0},{12,4},{16,8},{20,12},{24,16},{28,20},{1,25},{... | collective-permute-start | bytes 2162696 | tf_op jit(solution)/shard_map/ppermute | solution.py:175
  716.7 72.9 %collective-permute-start.45 = (bf16[256,1408]{1,0:T(8,128)(2,1)}, bf16[256,1408]{1,0:T(8,128)(2,1)}, u32[]{:S(2)}, u32[]{:S(2)}) collective-permute-start(bf16[256,1408]{1,0:T(8,128)(2,1)} %get-tuple-element.84), channel_id=1, source_target_pairs={{0,8},{4,12},{8,16},{12,20},{16,24},{20,28},{24,0},{28,4},{1,9},{5... | collective-permute-start | bytes 2162696 | tf_op jit(solution)/shard_map/ppermute | solution.py:175
  717.3 101.7 %collective-permute-start.46 = (bf16[256,1408]{1,0:T(8,128)(2,1)}, bf16[256,1408]{1,0:T(8,128)(2,1)}, u32[]{:S(2)}, u32[]{:S(2)}) collective-permute-start(bf16[256,1408]{1,0:T(8,128)(2,1)} %get-tuple-element.86), channel_id=1, source_target_pairs={{0,16},{4,20},{8,24},{12,28},{16,0},{20,4},{24,8},{28,12},{1,17},{... | collective-permute-start | bytes 2162696 | tf_op jit(solution)/shard_map/ppermute | solution.py:175
  783.3 47.8 %collective-permute-start.47 = (bf16[256,1408]{1,0:T(8,128)(2,1)S(1)}, bf16[256,1408]{1,0:T(8,128)(2,1)S(1)}, u32[]{:S(2)}, u32[]{:S(2)}) collective-permute-start(bf16[256,1408]{1,0:T(8,128)(2,1)S(1)} %copy-done.35), channel_id=1, source_target_pairs={{0,24},{4,28},{8,0},{12,4},{16,8},{20,12},{24,16},{28,20},{1,25},{... | collective-permute-start | bytes 2162696 | tf_op jit(solution)/shard_map/ppermute | solution.py:175
  787.5 50.0 %collective-permute-start.30 = (bf16[1024,512]{1,0:T(8,128)(2,1)S(1)}, bf16[1024,512]{1,0:T(8,128)(2,1)S(1)}, u32[]{:S(2)}, u32[]{:S(2)}) collective-permute-start(bf16[1024,512]{1,0:T(8,128)(2,1)S(1)} %fusion.52), channel_id=1, source_target_pairs={{0,4},{4,0},{8,12},{12,8},{16,20},{20,16},{24,28},{28,24},{1,5},{5... | collective-permute-start | bytes 3145736 | tf_op jit(solution)/shard_map/ppermute | solution.py:172
  789.1 52.1 %collective-permute-start.26 = (bf16[1024,640]{0,1:T(8,128)(2,1)S(1)}, bf16[1024,640]{0,1:T(8,128)(2,1)S(1)}, u32[]{:S(2)}, u32[]{:S(2)}) collective-permute-start(bf16[1024,640]{0,1:T(8,128)(2,1)S(1)} %fusion.44), channel_id=1, source_target_pairs={{0,4},{4,0},{8,12},{12,8},{16,20},{20,16},{24,28},{28,24},{1,5},{5... | collective-permute-start | bytes 3932168 | tf_op jit(solution)/shard_map/ppermute | solution.py:172
  789.6 53.3 %collective-permute-start.18 = (bf16[2,256,2048]{2,1,0:T(8,128)(2,1)S(1)}, bf16[2,256,2048]{2,1,0:T(8,128)(2,1)S(1)}, u32[]{:S(2)}, u32[]{:S(2)}) collective-permute-start(bf16[2,256,2048]{2,1,0:T(8,128)(2,1)S(1)} %convolution_convert_fusion.4), channel_id=1, source_target_pairs={{0,1},{1,0},{2,3},{3,2},{4,5},{5,4},{6,7},{7,6},{8,9},{9,8},{10,11... | collective-permute-start | bytes 6291464 | tf_op jit(solution)/shard_map/ppermute | solution.py:251
  819.0 32.1 %collective-permute-start.41 = (bf16[256,1408]{1,0:T(8,128)(2,1)S(1)}, bf16[256,1408]{1,0:T(8,128)(2,1)S(1)}, u32[]{:S(2)}, u32[]{:S(2)}) collective-permute-start(bf16[256,1408]{1,0:T(8,128)(2,1)S(1)} %copy-done.34), channel_id=1, source_target_pairs={{0,8},{4,12},{8,16},{12,20},{16,24},{20,28},{24,0},{28,4},{1,9},{5... | collective-permute-start | bytes 2162696 | tf_op jit(solution)/shard_map/ppermute | solution.py:175
  831.1 50.9 %collective-permute-start.42 = (bf16[256,1408]{1,0:T(8,128)(2,1)S(1)}, bf16[256,1408]{1,0:T(8,128)(2,1)S(1)}, u32[]{:S(2)}, u32[]{:S(2)}) collective-permute-start(bf16[256,1408]{1,0:T(8,128)(2,1)S(1)} %copy-done.33), channel_id=1, source_target_pairs={{0,16},{4,20},{8,24},{12,28},{16,0},{20,4},{24,8},{28,12},{1,17},{... | collective-permute-start | bytes 2162696 | tf_op jit(solution)/shard_map/ppermute | solution.py:175
  837.5 67.7 %collective-permute-start.43 = (bf16[256,1408]{1,0:T(8,128)(2,1)S(1)}, bf16[256,1408]{1,0:T(8,128)(2,1)S(1)}, u32[]{:S(2)}, u32[]{:S(2)}) collective-permute-start(bf16[256,1408]{1,0:T(8,128)(2,1)S(1)} %copy-done.32), channel_id=1, source_target_pairs={{0,24},{4,28},{8,0},{12,4},{16,8},{20,12},{24,16},{28,20},{1,25},{... | collective-permute-start | bytes 2162696 | tf_op jit(solution)/shard_map/ppermute | solution.py:175
  841.2 73.2 %collective-permute-start.31 = (bf16[256,512]{1,0:T(8,128)(2,1)S(1)}, bf16[256,512]{1,0:T(8,128)(2,1)S(1)}, u32[]{:S(2)}, u32[]{:S(2)}) collective-permute-start(bf16[256,512]{1,0:T(8,128)(2,1)S(1)} %get-tuple-element.102), channel_id=1, source_target_pairs={{0,8},{4,12},{8,16},{12,20},{16,24},{20,28},{24,0},{28,4},{1,9},{5... | collective-permute-start | bytes 786440 | tf_op jit(solution)/shard_map/ppermute | solution.py:175
  842.9 84.7 %collective-permute-start.32 = (bf16[256,512]{1,0:T(8,128)(2,1)S(1)}, bf16[256,512]{1,0:T(8,128)(2,1)S(1)}, u32[]{:S(2)}, u32[]{:S(2)}) collective-permute-start(bf16[256,512]{1,0:T(8,128)(2,1)S(1)} %get-tuple-element.104), channel_id=1, source_target_pairs={{0,16},{4,20},{8,24},{12,28},{16,0},{20,4},{24,8},{28,12},{1,17},{... | collective-permute-start | bytes 786440 | tf_op jit(solution)/shard_map/ppermute | solution.py:175
  851.0 79.7 %collective-permute-start.33 = (bf16[256,512]{1,0:T(8,128)(2,1)S(1)}, bf16[256,512]{1,0:T(8,128)(2,1)S(1)}, u32[]{:S(2)}, u32[]{:S(2)}) collective-permute-start(bf16[256,512]{1,0:T(8,128)(2,1)S(1)} %get-tuple-element.103), channel_id=1, source_target_pairs={{0,24},{4,28},{8,0},{12,4},{16,8},{20,12},{24,16},{28,20},{1,25},{... | collective-permute-start | bytes 786440 | tf_op jit(solution)/shard_map/ppermute | solution.py:175
  882.0 49.7 %collective-permute-start.27 = (bf16[256,640]{0,1:T(8,128)(2,1)S(1)}, bf16[256,640]{0,1:T(8,128)(2,1)S(1)}, u32[]{:S(2)}, u32[]{:S(2)}) collective-permute-start(bf16[256,640]{0,1:T(8,128)(2,1)S(1)} %get-tuple-element.99), channel_id=1, source_target_pairs={{0,8},{4,12},{8,16},{12,20},{16,24},{20,28},{24,0},{28,4},{1,9},{5... | collective-permute-start | bytes 983048 | tf_op jit(solution)/shard_map/ppermute | solution.py:175
  905.2 35.1 %collective-permute-start.28 = (bf16[256,640]{0,1:T(8,128)(2,1)S(1)}, bf16[256,640]{0,1:T(8,128)(2,1)S(1)}, u32[]{:S(2)}, u32[]{:S(2)}) collective-permute-start(bf16[256,640]{0,1:T(8,128)(2,1)S(1)} %get-tuple-element.101), channel_id=1, source_target_pairs={{0,16},{4,20},{8,24},{12,28},{16,0},{20,4},{24,8},{28,12},{1,17},{... | collective-permute-start | bytes 983048 | tf_op jit(solution)/shard_map/ppermute | solution.py:175
  914.4 25.8 %collective-permute-start.29 = (bf16[256,640]{0,1:T(8,128)(2,1)S(1)}, bf16[256,640]{0,1:T(8,128)(2,1)S(1)}, u32[]{:S(2)}, u32[]{:S(2)}) collective-permute-start(bf16[256,640]{0,1:T(8,128)(2,1)S(1)} %get-tuple-element.100), channel_id=1, source_target_pairs={{0,24},{4,28},{8,0},{12,4},{16,8},{20,12},{24,16},{28,20},{1,25},{... | collective-permute-start | bytes 983048 | tf_op jit(solution)/shard_map/ppermute | solution.py:175
  927.6 25.3 %collective-permute-start.19 = (bf16[2,128,2048]{2,1,0:T(8,128)(2,1)}, bf16[2,128,2048]{2,1,0:T(8,128)(2,1)}, u32[]{:S(2)}, u32[]{:S(2)}) collective-permute-start(bf16[2,128,2048]{2,1,0:T(8,128)(2,1)} %slice.529), channel_id=1, source_target_pairs={{0,2},{1,3},{2,0},{3,1},{4,6},{5,7},{6,4},{7,5},{8,10},{9,11},{10,... | collective-permute-start | bytes 3145736 | tf_op jit(solution)/shard_map/ppermute | solution.py:255
  (92 other events, 1287.0 us)

commit v3 on v2

--- a/solution.py
+++ b/solution.py
@@ -62,166 +62,792 @@
 
 MESH_ID = pl.DeviceIdType.MESH
 HBM = pl.BlockSpec(memory_space=pl.ANY)
-
-
-def gather_kernel(x_ref, c_ref, *refs):
-    count = (len(refs) - 5) // 2
-    shards, refs = refs[:count], refs[count:]
-    x_full, c_full, refs = refs[0], refs[1], refs[2:]
-    fulls, (send, recv, local) = refs[:count], refs[count:]
-    rows = x_ref.shape[1]
-    dp, sq = lax.axis_index("dp"), lax.axis_index("seq")
-    across = [(lax.rem(dp + 2 * r, 8), sq) for r in range(4)]
-    x_peer = (dp + 1 - 2 * lax.rem(dp, 2), sq)
-    core_peer = (dp, sq + 1 - 2 * lax.rem(sq, 2))
-    y_peer = (dp, lax.rem(sq + 2, 4))
-    peers = across[1:] + [x_peer, core_peer, y_peer]
-    barrier = pltpu.get_barrier_semaphore()
-    for peer in peers:
-        pl.semaphore_signal(barrier, inc=1, device_id=peer, device_id_type=MESH_ID)
-    pl.semaphore_wait(barrier, len(peers))
-    remote, own = [], []
-
-    def put(src, dst, peer):
-        i = len(remote)
+VMEM = pl.BlockSpec(memory_space=pltpu.VMEM)
+ROWS = 128
+LEN4 = 512
+HALF = 256
+DM = 2048
+LIMIT = 60 * 1024 * 1024
+LIMIT_B = 62 * 1024 * 1024
+
+
+def nt(a, b):
+    return lax.dot_general(a, b, (((1,), (1,)), ((), ())), preferred_element_type=F32)
+
+
+def tn(a, b):
+    return lax.dot_general(a, b, (((0,), (0,)), ((), ())), preferred_element_type=F32)
+
+
+def nn(a, b):
+    return jnp.dot(a, b, preferred_element_type=F32)
+
+
+class Links:
+    def __init__(self, send, recv, local):
+        self.send, self.recv, self.local = send, recv, local
+        self.remote, self.own = [], []
+        self.seen, self.gone = set(), set()
+        dp, sq = lax.axis_index("dp"), lax.axis_index("seq")
+        self.dp, self.sq = dp, sq
+        self.z = [(lax.rem(dp + 2 * r, 8), sq) for r in range(4)]
+        self.x = (dp + 1 - 2 * lax.rem(dp, 2), sq)
+        core = sq + 1 - 2 * lax.rem(sq, 2)
+        self.core = (dp, core)
+        self.y = (dp, lax.rem(sq + 2, 4))
+        self.both = (dp, lax.rem(core + 2, 4))
+        peers = self.z[1:] + [self.x, self.core, self.y, self.both]
+        barrier = pltpu.get_barrier_semaphore()
+        for peer in peers:
+            pl.semaphore_signal(barrier, inc=1, device_id=peer, device_id_type=MESH_ID)
+        pl.semaphore_wait(barrier, len(peers))
+
+    def put(self, src, dst, peer):
+        i = len(self.remote)
         copy = pltpu.make_async_remote_copy(
             src_ref=src,
             dst_ref=dst,
-            send_sem=send.at[i],
-            recv_sem=recv.at[i],
+            send_sem=self.send.at[i],
+            recv_sem=self.recv.at[i],
             device_id=peer,
             device_id_type=MESH_ID,
         )
         copy.start()
-        remote.append([copy, False])
+        self.remote.append(copy)
         return i
 
-    def arrived(i):
-        remote[i][0].wait_recv()
-        remote[i][1] = True
-
-    def keep(src, dst):
-        copy = pltpu.make_async_copy(src, dst, local.at[len(own)])
+    def arrived(self, *ids):
+        for i in ids:
+            if i not in self.seen:
+                self.seen.add(i)
+                self.remote[i].wait_recv()
+
+    def sent(self, *ids):
+        for i in ids:
+            if i not in self.gone:
+                self.gone.add(i)
+                self.remote[i].wait_send()
+
+    def keep(self, src, dst):
+        copy = pltpu.make_async_copy(src, dst, self.local.at[len(self.own)])
         copy.start()
-        own.append(copy)
+        self.own.append([copy, False])
+        return len(self.own) - 1
+
+    def kept(self, *ids):
+        for i in ids:
+            if not self.own[i][1]:
+                self.own[i][1] = True
+                self.own[i][0].wait()
+
+    def finish(self):
+        self.sent(*range(len(self.remote)))
+        self.arrived(*range(len(self.remote)))
+        self.kept(*range(len(self.own)))
+
+
+def rope_tile(t, cosine, sine):
+    lane = lax.broadcasted_iota(jnp.int32, t.shape, 1)
+    turned = jnp.where(lax.rem(lane, 64) < 32, pltpu.roll(t, 96, 1), pltpu.roll(t, 32, 1))
+    return t * cosine + turned * sine
+
+
+def forward_kernel(
+    x_ref, c_ref, g_ref, table, mask, wqkv_s, wo_s, wg_s, wu_s, wd_s,
+    c_full, wqkv_f, wo_f, wg_f, wu_f, wd_f, na_o, qkv_o, att_o, res_o, nm_o, gain_o, prod_o, fa_o, fb_o, down_o,
+    xf, nm, wqkv_v, wo_v, qkv, att, far, far_in, near, ysend, yin, own_x, gseq, gfull, gown, prod, fa, fb, wt, lbuf, gbuf,
+    send, recv, local, wsem, lsem, gsem,
+):
+    links = Links(send, recv, local)
+    put, arrived = links.put, links.arrived
+    shards = [wqkv_s, wo_s, wg_s, wu_s, wd_s]
+    fulls = [wqkv_f, wo_f, wg_f, wu_f, wd_f]
 
     def part(full, k):
-        return full.at[:, pl.ds(k * rows, rows)]
+        return full.at[:, pl.ds(k * ROWS, ROWS)]
 
     def seq_start(src, full):
-        i = put(src, part(full, 1), y_peer)
-        put(src, part(full, 2), core_peer)
-        keep(src, part(full, 0))
-        return i
-
-    def seq_forward(full, i):
-        arrived(i)
-        put(part(full, 1), part(full, 3), core_peer)
+        return [put(src, part(full, 1), links.y), put(src, part(full, 2), links.core)]
+
+    def seq_forward(full, ids):
+        arrived(ids[0])
+        ids.append(put(part(full, 1), part(full, 3), links.core))
+
+    placed = []
 
     def z_start(i):
-        keep(shards[i], fulls[i].at[0, 0])
-        copies = [put(shards[i], fulls[i].at[0, r], across[4 - r]) for r in (1, 2, 3)]
-        put(shards[i], fulls[i].at[1, 0], x_peer)
-        return copies
-
-    def x_forward(i, copies):
-        for r in (1, 3, 2):
+        placed.append(links.keep(shards[i], fulls[i].at[0, 0]))
+        return [put(shards[i], fulls[i].at[0, r], links.z[4 - r]) for r in (1, 2, 3)]
+
+    def x_own(i):
+        return [put(shards[i], fulls[i].at[1, 0], links.x)]
+
+    def x_forward(i, copies, ids, order=(1, 3, 2)):
+        for r in order:
             arrived(copies[r - 1])
-            put(fulls[i].at[0, r], fulls[i].at[1, r], x_peer)
-
-    xs = seq_start(x_ref, x_full)
-    zs = [z_start(0), z_start(1)]
-    seq_forward(x_full, xs)
-    x_forward(0, zs[0])
+            ids.append(put(fulls[i].at[0, r], fulls[i].at[1, r], links.x))
+
+    xs = seq_start(x_ref, xf)
+    own0 = links.keep(x_ref, part(xf, 0))
+    own1 = links.keep(x_ref, own_x)
+    gs = [put(g_ref, gseq.at[k], p) for k, p in ((1, links.core), (2, links.y), (3, links.both))]
+    z0 = z_start(0)
+    x0 = x_own(0)
+    arrived(*gs)
+    gown[...] = g_ref[...] + gseq[1] + gseq[2] + gseq[3]
+    gfull[0, 0] = gown[...]
+    gz = [put(gown, gfull.at[0, r], links.z[4 - r]) for r in (1, 2, 3)]
+    gx = [put(gown, gfull.at[1, 0], links.x)]
+    z1 = z_start(1)
+    for r in (1, 2, 3):
+        arrived(gz[r - 1])
+        gx.append(put(gfull.at[0, r], gfull.at[1, r], links.x))
+    seq_forward(xf, xs)
+    x_forward(0, z0, x0)
+    x1 = x_own(1)
+    arrived(*gx)
+    for b in range(8):
+        gain_o[:, b * 256 : (b + 1) * 256] = gfull[b // 4, b % 4]
+    z2 = z_start(2)
+    x2 = x_own(2)
+    arrived(*xs)
+    links.sent(xs[2])
+    links.kept(own0, own1)
+
+    @pl.loop(0, 16)
+    def _(i):
+        m, r = i // 8, pl.multiple_of(lax.rem(i, 8) * 64, 64)
+        v = xf[m, pl.ds(r, 64), :].astype(F32)
+        inverse = lax.rsqrt(jnp.mean(v * v, axis=-1, keepdims=True) + EPS)
+        xf[m, pl.ds(r, 64), :] = (v * inverse * gain_o[0:1, :]).astype(BF)
+
+    na_copy = links.keep(xf, na_o)
+    x_forward(1, z1, x1)
+    arrived(*x0)
+    links.kept(placed[0])
+    load0 = links.keep(wqkv_f, wqkv_v)
+    links.kept(load0)
+
+    @pl.loop(0, 4)
+    def _(i):
+        m, r = i // 2, pl.multiple_of(lax.rem(i, 2) * 256, 256)
+        rows = pl.ds(r, 256)
+        a = xf[m, rows, :]
+        cq, sq = table[0, rows, :], table[1, rows, :]
+        for n in range(2):
+            t = nn(a, wqkv_v[:, :, :, n * 256 : (n + 1) * 256].reshape(DM, 256))
+            for j in range(2):
+                lanes = slice(n * 256 + j * 128, n * 256 + (j + 1) * 128)
+                qkv[m, rows, lanes] = rope_tile(t[:, j * 128 : (j + 1) * 128], cq, sq).astype(BF)
+        t = nn(a, wqkv_v[:, :, :, 512:640].reshape(DM, 128))
+        qkv[m, rows, 512:640] = rope_tile(t, table[2, rows, :], table[3, rows, :]).astype(BF)
+
+    links.keep(qkv, qkv_o)
+
+    def attend(m):
+        kv = qkv[m, :, 512:640].astype(F32)
+        lane = lax.broadcasted_iota(jnp.int32, (LEN4, 128), 1)
+        ka = jnp.where(lane < 64, kv, 0.0)
+        vb = jnp.where(lane < 64, 0.0, kv)
+        ks = [ka.astype(BF), pltpu.roll(ka, 64, 1).astype(BF)]
+        vs = [pltpu.roll(vb, 64, 1).astype(BF), vb.astype(BF)]
+
+        @pl.loop(0, 8)
+        def _(i):
+            lanes = pl.ds(pl.multiple_of(i // 2 * 128, 128), 128)
+            rows = pl.ds(pl.multiple_of(lax.rem(i, 2) * 256, 256), 256)
+            q = qkv[m, rows, lanes]
+            bias = mask[m, rows, :].astype(F32)
+            out = jnp.zeros((256, 128), F32)
+            for k, v in zip(ks, vs):
+                s = nt(q, k) * 0.125 + bias
+                e = jnp.exp(s - jnp.max(s, axis=-1, keepdims=True))
+                p = (e / jnp.sum(e, axis=-1, keepdims=True)).astype(BF)
+                out = out + nn(p, v)
+            att[m, rows, lanes] = out.astype(BF)
+
+    attend(0)
+    z3 = z_start(3)
+    attend(1)
+    links.keep(att, att_o)
+    arrived(*x1)
+    links.kept(placed[1])
+    load1 = links.keep(wo_f, wo_v)
+    links.kept(load1)
+
+    def out_rows(m, row, dst, dtype):
+        @pl.loop(0, 8)
+        def _(n):
+            w = wo_v[n // 4, lax.rem(n, 4)]
+            lanes = pl.ds(pl.multiple_of(n * 256, 256), 256)
+            dst[m, :, lanes] = nt(att[m, row : row + HALF, :], w).astype(dtype)
+
+    for m in range(2):
+        out_rows(m, HALF, far, BF)
+    fc = put(far, far_in, links.core)
+    for m in range(2):
+        out_rows(m, 0, near, F32)
+    arrived(fc)
+
+    @pl.loop(0, 4)
+    def _(i):
+        m, r = i // 2, pl.multiple_of(lax.rem(i, 2) * 64, 64)
+        rows = pl.ds(r + ROWS, 64)
+        ysend[m, pl.ds(r, 64), :] = (near[m, rows, :] + far_in[m, rows, :].astype(F32)).astype(BF)
+
+    yc = put(ysend, yin, links.y)
+    x_forward(2, z2, x2)
+    x3 = x_own(3)
+    z4 = z_start(4)
+    arrived(yc)
+
+    @pl.loop(0, 4)
+    def _(i):
+        m, r = i // 2, pl.multiple_of(lax.rem(i, 2) * 64, 64)
+        rows = pl.ds(r, 64)
+        v = near[m, rows, :] + far_in[m, rows, :].astype(F32) + yin[m, rows, :].astype(F32) + own_x[m, rows, :].astype(F32)
+        res_o[m, rows, :] = v
+        inverse = lax.rsqrt(jnp.mean(v * v, axis=-1, keepdims=True) + EPS)
+        nm[m, rows, :] = (v * inverse * gain_o[1:2, :]).astype(BF)
+
+    ns = seq_start(part(nm, 0), nm)
+    seq_forward(nm, ns)
     cs = seq_start(c_ref, c_full)
-    zs.append(z_start(2))
-    x_forward(1, zs[1])
-    zs.append(z_start(3))
+    c_own = links.keep(c_ref, part(c_full, 0))
+    x_forward(3, z3, x3)
+    x4 = x_own(4)
+    arrived(*ns)
+    links.keep(nm, nm_o)
+    arrived(*x2)
     seq_forward(c_full, cs)
-    x_forward(2, zs[2])
-    zs.append(z_start(4))
-    x_forward(3, zs[3])
-    x_forward(4, zs[4])
-    for copy, seen in remote:
-        copy.wait_send()
-        if not seen:
-            copy.wait_recv()
-    for copy in own:
-        copy.wait()
-
-
-def gather_all(x, c, shards):
+    arrived(*x3)
+    links.kept(placed[2], placed[3])
+
+    def load(t, slot):
+        lanes = pl.ds(pl.multiple_of(t * 128, 128), 128)
+        return [
+            pltpu.make_async_copy(w.at[:, :, :, lanes], wt.at[slot, :, :, :, pl.ds(k * 128, 128)], wsem.at[slot, k])
+            for k, w in enumerate((wg_f, wu_f))
+        ]
+
+    def up_tile(t, slot):
+        lanes = pl.ds(pl.multiple_of(t * 128, 128), 128)
+
+        @pl.loop(0, 4)
+        def _(i):
+            m, rows = i // 2, pl.ds(pl.multiple_of(lax.rem(i, 2) * 256, 256), 256)
+            r = nn(nm[m, rows, :], wt[slot].reshape(DM, 256))
+            g, u = r[:, :128], r[:, 128:]
+            s = jax.nn.sigmoid(g)
+            active = g * s
+            prod[m, rows, lanes] = (active * u).astype(BF)
+            fa[m, rows, lanes] = (u * s * (1.0 + g * (1.0 - s))).astype(BF)
+            fb[m, rows, lanes] = active.astype(BF)
+
+    for c in load(0, 0):
+        c.start()
+    tiles = wg_s.shape[1] // 128
+
+    def tile_step(t):
+        slot = lax.rem(t, 2)
+
+        @pl.when(t + 1 < tiles)
+        def _():
+            for c in load(t + 1, 1 - slot):
+                c.start()
+
+        for c in load(t, slot):
+            c.wait()
+        up_tile(t, slot)
+
+    pl.loop(0, 5)(tile_step)
+    arrived(z4[0])
+    x_forward(4, z4, x4)
+    pl.loop(5, tiles)(tile_step)
+    links.keep(prod, prod_o)
+    links.keep(fa, fa_o)
+    links.keep(fb, fb_o)
+    arrived(*cs)
+    links.kept(c_own)
+
+    def load_left(b, slot):
+        lanes = pl.ds(pl.multiple_of(b * 256, 256), 256)
+        return pltpu.make_async_copy(c_full.at[:, :, lanes], lbuf.at[slot], lsem.at[slot])
+
+    def store_grad(b, slot):
+        return pltpu.make_async_copy(gbuf.at[slot], down_o.at[b // 4, lax.rem(b, 4)], gsem.at[slot])
+
+    load_left(0, 0).start()
+
+    @pl.loop(0, 8)
+    def _(b):
+        slot = lax.rem(b, 2)
+
+        @pl.when(b + 1 < 8)
+        def _():
+            load_left(b + 1, 1 - slot).start()
+
+        load_left(b, slot).wait()
+
+        @pl.when(b >= 2)
+        def _():
+            store_grad(b - 2, slot).wait()
+
+        gbuf[slot] = (tn(lbuf[slot, 0], prod[0]) + tn(lbuf[slot, 1], prod[1])).astype(BF)
+        store_grad(b, slot).start()
+
+    store_grad(6, 0).wait()
+    store_grad(7, 1).wait()
+    links.finish()
+
+
+def forward(x, c, g, table, mask, shards):
     micro, rows, d = x.shape
-    tokens = jax.ShapeDtypeStruct((micro, 4 * rows, d), x.dtype)
-    fulls = [jax.ShapeDtypeStruct((2, 4) + w.shape, w.dtype) for w in shards]
-    outs = pl.pallas_call(
-        gather_kernel,
-        out_shape=[tokens, tokens] + fulls,
-        in_specs=[HBM] * (2 + len(shards)),
-        out_specs=[HBM] * (2 + len(shards)),
-        scratch_shapes=[pltpu.SemaphoreType.DMA((48,)), pltpu.SemaphoreType.DMA((48,)), pltpu.SemaphoreType.DMA((8,))],
-        compiler_params=pltpu.CompilerParams(collective_id=0, has_side_effects=True),
-    )(x, c, *shards)
-    return outs[0], outs[1], [w.reshape(-1, w.shape[-1]) for w in outs[2:]]
-
-
-class Mesh2D:
-    n = 8
-
-    def shift_x(self, a):
-        return lax.ppermute(a, "dp", [(i, i ^ 1) for i in range(8)])
-
-    def shift_z(self, a, r):
-        return lax.ppermute(a, "dp", [(i, (i + 2 * r) % 8) for i in range(8)])
-
-    def gather(self, x, c, shards):
-        return gather_all(x, c, shards)
-
-    def gather_gains(self, g):
-        g = jnp.zeros((2, 4, g.shape[1]), F32).at[:, lax.axis_index("seq")].set(g).reshape(2, -1)
-        g = g + shift_core(g)
-        g = g + shift_y(g)
-        g = jnp.concatenate([g, self.shift_x(g)], axis=0)
-        g = jnp.stack([g] + [self.shift_z(g, -r) for r in (1, 2, 3)])
-        return jnp.transpose(g.reshape(4, 2, 2, -1), (2, 1, 0, 3)).reshape(2, -1)
-
-    def scatter_gain(self, g):
-        g = g.reshape(2, -1)
-        g = (g[0] + self.shift_x(g[1])).reshape(4, -1)
-        g = g[0] + self.shift_z(g[1], 1) + self.shift_z(g[2], 2) + self.shift_z(g[3], 3)
-        g = g + shift_core(g)
-        g = g + shift_y(g)
-        size = g.shape[0] // 4
-        return lax.dynamic_slice_in_dim(g, lax.axis_index("seq") * size, size, 0)
-
-    def scatter(self, left, right):
-        half = left.shape[1] // 2
-        far = outer_sum(left[:, half:], right).astype(BF)
-        got = self.shift_x(far)
-        near = (outer_sum(left[:, :half], right) + got.astype(F32)).astype(BF)
-        blocks = near.reshape(4, half // 4, -1)
-        total = blocks[0].astype(F32)
+    sd = jax.ShapeDtypeStruct
+    toks = (micro, 4 * rows, d)
+    nq, nf = shards[1].shape[1], shards[2].shape[1]
+    fulls = [sd((2, 4) + w.shape, BF) for w in shards]
+    ffn = sd((micro, 4 * rows, nf), BF)
+    out_shape = [sd(toks, BF)] + fulls + [
+        sd(toks, BF), sd((micro, 4 * rows, 640), BF), sd((micro, 4 * rows, nq), BF),
+        sd((micro, rows, d), F32), sd(toks, BF), sd((8, d), F32), ffn, ffn, ffn, sd((2, 4, 256, nf), BF),
+    ]
+    v = pltpu.VMEM
+    scratch = [
+        v(toks, BF), v(toks, BF), v((2, 4, 256, 640), BF), v((2, 4, 256, 512), BF), v((2, 512, 640), BF),
+        v((2, 512, 512), BF), v((2, 256, d), BF), v((2, 256, d), BF), v((2, 256, d), F32), v((2, 128, d), BF),
+        v((2, 128, d), BF), v((2, 128, d), BF), v((4, 8, 256), F32), v((2, 4, 8, 256), F32), v((8, 256), F32),
+        v((2, 512, nf), BF), v((2, 512, nf), BF), v((2, 512, nf), BF), v((2, 2, 4, 256, 256), BF), v((2, 2, 512, 256), BF), v((2, 256, nf), BF),
+        pltpu.SemaphoreType.DMA((72,)), pltpu.SemaphoreType.DMA((72,)), pltpu.SemaphoreType.DMA((24,)),
+        pltpu.SemaphoreType.DMA((2, 2)), pltpu.SemaphoreType.DMA((2,)), pltpu.SemaphoreType.DMA((2,)),
+    ]
+    return pl.pallas_call(
+        forward_kernel,
+        out_shape=out_shape,
+        in_specs=[HBM, HBM, VMEM, VMEM, VMEM] + [HBM] * 5,
+        out_specs=[HBM] * 9 + [VMEM, HBM, VMEM] + [HBM] * 4,
+        scratch_shapes=scratch,
+        compiler_params=pltpu.CompilerParams(collective_id=0, has_side_effects=True, vmem_limit_bytes=LIMIT),
+    )(x, c, g, table, mask, *shards)
+
+
+ORDER = (2, 1, 3, 0)
+
+
+def backward_kernel(
+    table, mask_t, gain, x_ref, c_full, wqkv_f, wo_f, wg_f, wu_f, wd_f, na_h, qkv_h, att_h, res_h, nm_h, prod_h, fa_h,
+    fb_h, down_h,
+    out_o, din_o, gain_o, gq_o, go_o, gg_o, gu_o, gd_o, xin_f, xin_o, xin_q, zin_f, zin_o, zin_q, fin, yin,
+    cot, nm, dr, dg, du, grads, stage, ostage, wcol, wrow, far, far_st, ysend, acc_m, acc_o, res, qkv, att, datt, dqkv,
+    obuf, dkacc, dvacc, gacc, gxin, gnear, gzin, gown, gsin,
+    send, recv, local, csem, rsem, ssem, osem,
+):
+    links = Links(send, recv, local)
+    put, arrived, sent, keep, kept = links.put, links.arrived, links.sent, links.keep, links.kept
+    ff = fa_h.shape[2]
+    prod = dr.at[:, :, pl.ds(0, ff)]
+
+    def wide(k):
+        return lambda r: grads.at[k, r]
+
+    def cut(start, width):
+        return lambda r: grads.at[0, r, :, pl.ds(start, width)]
+
+    spec = {
+        "down": (None, None, wide(0), xin_f.at[0], zin_f.at[0], ff, gd_o),
+        "gate": (nm, dg, wide(1), xin_f.at[1], zin_f.at[1], ff, gg_o),
+        "up": (nm, du, wide(2), xin_f.at[2], zin_f.at[2], ff, gu_o),
+        "out": (dr, att, cut(0, 512), xin_o, zin_o, 512, go_o),
+        "qkv": (cot, dqkv, cut(512, 640), xin_q, zin_q, 640, gq_o),
+    }
+    xid = {name: {} for name in spec}
+    zid = {name: {} for name in spec}
+
+    def block_of(name, b):
+        left, right = spec[name][:2]
+        lanes = pl.ds(b * 256, 256)
+        return tn(left[0, :, lanes], right[0]) + tn(left[1, :, lanes], right[1])
+
+    def grad_far(name):
+        buffer, landing = spec[name][2:4]
+        for r in ORDER:
+            if name == "down":
+                xid[name][r] = put(down_h.at[1, r], landing.at[r], links.x)
+            else:
+                buffer(r)[...] = block_of(name, 4 + r).astype(BF)
+                xid[name][r] = put(buffer(r), landing.at[r], links.x)
+
+    def grad_near(name, r):
+        buffer, landing, zland, width = spec[name][2:6]
+        arrived(xid[name][r])
+        got = stage.at[0, :, pl.ds(0, width)]
+        copies = [pltpu.make_async_copy(landing.at[r], got, ssem.at[0])]
+        if name == "down":
+            copies.append(pltpu.make_async_copy(down_h.at[0, r], stage.at[1], ssem.at[1]))
+        for c in copies:
+            c.start()
+        if name != "down":
+            mine = block_of(name, r)
+            sent(xid[name][r])
+        for c in copies:
+            c.wait()
+        if name == "down":
+            mine = stage[1].astype(F32)
+        buffer(r)[...] = (mine + got[...].astype(F32)).astype(BF)
+        if r:
+            zid[name][r] = put(buffer(r), zland.at[r - 1], links.z[r])
+
+    writing = []
+
+    def grad_final(name):
+        buffer, _, zland, width, result = spec[name][2:]
+        copies = []
         for r in (1, 2, 3):
-            total = total + self.shift_z(blocks[r], r).astype(F32)
-        return total
-
-    def to_relative(self, a):
-        dp = lax.axis_index("dp")
-        z, x = dp // 2, dp % 2
-        lead = a.shape[:-1]
-        a = a.reshape(lead + (4, 2, -1))
-        a = jnp.where(x == 0, a, jnp.flip(a, -2))
-        a = lax.dynamic_slice_in_dim(jnp.concatenate([a, a], -3), z, 4, len(lead))
-        return jnp.swapaxes(a, -2, -3).reshape(lead + (-1,))
-
-    def from_relative(self, a):
-        dp = lax.axis_index("dp")
-        z, x = dp // 2, dp % 2
-        lead = a.shape[:-1]
-        a = jnp.swapaxes(a.reshape(lead + (2, 4, -1)), -2, -3)
-        a = jnp.where(x == 0, a, jnp.flip(a, -2))
-        a = lax.dynamic_slice_in_dim(jnp.concatenate([a, a], -3), 4 - z, 4, len(lead))
-        return a.reshape(lead + (-1,))
+            arrived(zid[name][r])
+            copies.append(pltpu.make_async_copy(zland.at[r - 1], stage.at[r - 1, :, pl.ds(0, width)], ssem.at[r - 1]))
+            copies[-1].start()
+        for c in copies + writing:
+            c.wait()
+        lanes = slice(0, width)
+        total = buffer(0)[...].astype(F32) + stage[0, :, lanes].astype(F32)
+        ostage[:, lanes] = total + stage[1, :, lanes].astype(F32) + stage[2, :, lanes].astype(F32)
+        writing[:] = [pltpu.make_async_copy(ostage.at[:, pl.ds(0, width)], result, osem.at[0])]
+        writing[0].start()
+
+    def sweep(terms, row, use):
+        def load(b, slot):
+            return [
+                pltpu.make_async_copy(
+                    w.at[b // 4, lax.rem(b, 4)], wrow.at[slot, k, :, pl.ds(0, width)], rsem.at[slot, k]
+                )
+                for k, (_, w, width) in enumerate(terms)
+            ]
+
+        for c in load(0, 0):
+            c.start()
+
+        @pl.loop(0, 8)
+        def _(b):
+            slot = lax.rem(b, 2)
+
+            @pl.when(b + 1 < 8)
+            def _():
+                for c in load(b + 1, 1 - slot):
+                    c.start()
+
+            for c in load(b, slot):
+                c.wait()
+            lanes = pl.ds(pl.multiple_of(b * 256, 256), 256)
+            for m in range(2):
+                total = None
+                for k, (left, _, width) in enumerate(terms):
+                    t = nt(left[m, row : row + HALF, 0:width], wrow[slot, k, :, 0:width])
+                    total = t if total is None else total + t
+                use(m, lanes, total)
+
+    fid, yid = [], []
+
+    def rows_far(i, terms):
+        sent(*fid)
+
+        def use(m, lanes, total):
+            far[m, :, lanes] = total.astype(BF)
+
+        sweep(terms, HALF, use)
+        fid.append(put(far, fin.at[i], links.core))
+
+    def rows_near(i, terms, acc):
+        sent(*yid)
+        arrived(fid[i])
+        kept(keep(fin.at[i], far_st))
+
+        def use(m, lanes, total):
+            total = total + far_st[m, :, lanes].astype(F32)
+            acc[m, :, lanes] = total[:ROWS]
+            ysend[m, :, lanes] = total[ROWS:].astype(BF)
+
+        sweep(terms, 0, use)
+        yid.append(put(ysend, yin.at[i], links.y))
+
+    def rows_final(i):
+        arrived(yid[i])
+        kept(keep(yin.at[i], far_st.at[:, pl.ds(0, ROWS)]))
+
+    def chunks(body):
+        @pl.loop(0, 4)
+        def _(i):
+            body(i // 2, pl.ds(pl.multiple_of(lax.rem(i, 2) * 64, 64), 64))
+
+    def norm_back(v, e, row):
+        inverse = lax.rsqrt(jnp.mean(v * v, axis=-1, keepdims=True) + EPS)
+        u = v * inverse
+        gacc[row : row + 1, :] += jnp.sum(e * u, axis=0, keepdims=True)
+        w = e * gain[row : row + 1, :]
+        return inverse * (w - u * jnp.mean(w * u, axis=-1, keepdims=True))
+
+    grad_far("down")
+    prod_in = keep(prod_h, prod)
+    cot_in = keep(c_full, cot)
+    ffn_in = [keep(fa_h, dg), keep(fb_h, du)]
+    late = [keep(nm_h, nm), keep(res_h, res), keep(qkv_h, qkv), keep(att_h, att)]
+    gacc[...] = jnp.zeros_like(gacc)
+
+    def load_col(t, slot):
+        lanes = pl.ds(pl.multiple_of(t * 256, 256), 256)
+        return pltpu.make_async_copy(wd_f.at[:, :, :, lanes], wcol.at[slot], csem.at[slot])
+
+    load_col(0, 0).start()
+    kept(prod_in)
+    out_terms = [(prod, wd_f, ff)]
+    rows_far(0, out_terms)
+    kept(cot_in, *ffn_in)
+    tiles = ff // 256
+    rest = ff - tiles * 256
+
+    def product_rows(slot, width, start):
+        @pl.loop(0, 4)
+        def _(i):
+            m, rows = i // 2, pl.ds(pl.multiple_of(lax.rem(i, 2) * 256, 256), 256)
+            lanes = pl.ds(start, width)
+            d = nn(cot[m, rows, :], wcol[slot, :, :, :, 0:width].reshape(DM, width))
+            dg[m, rows, lanes] = (d * dg[m, rows, lanes].astype(F32)).astype(BF)
+            du[m, rows, lanes] = (d * du[m, rows, lanes].astype(F32)).astype(BF)
+
+    last = pltpu.make_async_copy(
+        wd_f.at[:, :, :, pl.ds(tiles * 256, rest)], wcol.at[tiles % 2, :, :, :, pl.ds(0, rest)], csem.at[tiles % 2]
+    )
+
+    @pl.loop(0, tiles)
+    def _(t):
+        slot = lax.rem(t, 2)
+
+        @pl.when(t + 1 < tiles)
+        def _():
+            load_col(t + 1, 1 - slot).start()
+
+        load_col(t, slot).wait()
+        product_rows(slot, 256, pl.multiple_of(t * 256, 256))
+
+    last.start()
+    last.wait()
+    product_rows(tiles % 2, rest, tiles * 256)
+
+    rows_near(0, out_terms, acc_o)
+    ffn_terms = [(dg, wg_f, ff), (du, wu_f, ff)]
+    rows_far(1, ffn_terms)
+    kept(*late)
+    grad_far("gate")
+    rows_near(1, ffn_terms, acc_m)
+    grad_far("up")
+    grad_near("down", 2)
+    grad_near("down", 1)
+    rows_final(0)
+
+    def output_rows(m, rows):
+        total = res[m, rows, :] + acc_o[m, rows, :] + far_st[m, rows, :].astype(F32)
+        obuf[m, rows, :] = total.astype(BF)
+
+    chunks(output_rows)
+    keep(obuf, out_o)
+    grad_near("down", 3)
+    rows_final(1)
+
+    def middle(m, rows):
+        e = acc_m[m, rows, :] + far_st[m, rows, :].astype(F32)
+        d = norm_back(res[m, rows, :], e, 1) + cot[m, rows, :].astype(F32)
+        acc_m[m, rows, :] = d
+        dr[m, rows, :] = d.astype(BF)
+
+    chunks(middle)
+    own = dr.at[:, pl.ds(0, ROWS)]
+    ds = [put(own, dr.at[:, pl.ds(ROWS, ROWS)], links.y), put(own, dr.at[:, pl.ds(2 * ROWS, ROWS)], links.core)]
+    na_in = keep(na_h, cot)
+    wo_in = [keep(wo_f.at[:, :, :, pl.ds(k * 256, 256)], wcol.at[k]) for k in range(2)]
+    grad_near("down", 0)
+    arrived(ds[0])
+    ds.append(put(dr.at[:, pl.ds(ROWS, ROWS)], dr.at[:, pl.ds(3 * ROWS, ROWS)], links.core))
+    kept(*wo_in)
+    arrived(*ds)
+
+    @pl.loop(0, 4)
+    def _(i):
+        m, rows = i // 2, pl.ds(pl.multiple_of(lax.rem(i, 2) * 256, 256), 256)
+        for k in range(2):
+            datt[m, rows, k * 256 : (k + 1) * 256] = nn(dr[m, rows, :], wcol[k].reshape(DM, 256)).astype(BF)
+
+    def attend_back(m):
+        kv = qkv[m, :, 512:640].astype(F32)
+        lane = lax.broadcasted_iota(jnp.int32, (LEN4, 128), 1)
+        half = lax.broadcasted_iota(jnp.int32, (256, 128), 1) < 64
+        ka = jnp.where(lane < 64, kv, 0.0)
+        vb = jnp.where(lane < 64, 0.0, kv)
+        kb, va = pltpu.roll(ka, 64, 1), pltpu.roll(vb, 64, 1)
+        heads = [
+            (k.astype(BF), k.T.astype(BF), v.astype(BF), keep_lanes)
+            for k, v, keep_lanes in ((ka, va, half), (kb, vb, jnp.logical_not(half)))
+        ]
+        dkacc[...] = jnp.zeros_like(dkacc)
+        dvacc[...] = jnp.zeros_like(dvacc)
+
+        @pl.loop(0, 8)
+        def _(i):
+            lanes = pl.ds(pl.multiple_of(i // 2 * 128, 128), 128)
+            rows = pl.ds(pl.multiple_of(lax.rem(i, 2) * 256, 256), 256)
+            q, do = qkv[m, rows, lanes], datt[m, rows, lanes]
+            bias = mask_t[m, :, rows].astype(F32)
+            dq_t = jnp.zeros((128, 256), F32)
+            for k, k_t, v, keep_lanes in heads:
+                s = nt(k, q) * 0.125 + bias
+                e = jnp.exp(s - jnp.max(s, axis=0, keepdims=True))
+                p = e * (1.0 / jnp.sum(e, axis=0, keepdims=True))
+                d = nt(v, do)
+                ds_ = (p * (d - jnp.sum(p * d, axis=0, keepdims=True)) * 0.125).astype(BF)
+                dq_t = dq_t + nn(k_t, ds_)
+                zero = jnp.zeros_like(q)
+                dkacc[...] += nn(ds_, jnp.where(keep_lanes, q, zero))
+                dvacc[...] += nn(p.astype(BF), jnp.where(keep_lanes, do, zero))
+            dqkv[m, rows, lanes] = rope_tile(dq_t.T, table[0, rows, :], -table[1, rows, :]).astype(BF)
+
+        dk = dkacc[...] + pltpu.roll(dkacc[...], 64, 1)
+        dv = dvacc[...] + pltpu.roll(dvacc[...], 64, 1)
+        dk = rope_tile(dk, table[0], -table[1])
+        dqkv[m, :, 512:640] = jnp.where(lane < 64, dk, dv).astype(BF)
+
+    attend_back(0)
+    grad_near("gate", 2)
+    grad_near("gate", 1)
+    attend_back(1)
+    na_terms = [(dqkv, wqkv_f, 640)]
+    rows_far(2, na_terms)
+    grad_final("down")
+    sent(*zid["down"].values())
+    kept(na_in)
+    grad_far("out")
+    grad_far("qkv")
+    rows_near(2, na_terms, acc_o)
+    grad_near("gate", 3)
+    grad_near("gate", 0)
+    rows_final(2)
+    own_x = far_st.at[:, pl.ds(ROWS, ROWS)]
+    kept(keep(x_ref, own_x))
+
+    def last_rows(m, rows):
+        e = acc_o[m, rows, :] + far_st[m, rows, :].astype(F32)
+        v = own_x[m, rows, :].astype(F32)
+        acc_m[m, rows, :] += norm_back(v, e, 0)
+
+    chunks(last_rows)
+    keep(acc_m, din_o)
+    gx = put(gacc.at[:, pl.ds(1024, 1024)], gxin, links.x)
+    arrived(gx)
+    gnear[...] = gacc[:, 0:1024] + gxin[...]
+    gz = [put(gnear.at[:, pl.ds(r * 256, 256)], gzin.at[r - 1], links.z[r]) for r in (1, 2, 3)]
+    grad_near("up", 2)
+    arrived(*gz)
+    gown[...] = gnear[:, 0:256] + gzin[0] + gzin[1] + gzin[2]
+    gs = [put(gown, gsin.at[k], p) for k, p in enumerate((links.core, links.y, links.both))]
+    grad_near("up", 1)
+    arrived(*gs)
+    gain_o[...] = gown[...] + gsin[0] + gsin[1] + gsin[2]
+    grad_near("up", 3)
+    grad_final("gate")
+    grad_near("up", 0)
+    for name in ("out", "qkv"):
+        for r in ORDER:
+            grad_near(name, r)
+    for name in ("up", "out", "qkv"):
+        grad_final(name)
+    for c in writing:
+        c.wait()
+    links.finish()
+
+
+def backward(table, mask_t, gain, x, arrays):
+    micro, rows, d = x.shape
+    sd = jax.ShapeDtypeStruct
+    ff = arrays[-4].shape[2]
+    v = pltpu.VMEM
+    out_shape = [
+        sd(x.shape, BF), sd(x.shape, F32), sd((8, 256), F32), sd((256, 640), F32), sd((256, 512), F32),
+        sd((256, ff), F32), sd((256, ff), F32), sd((256, ff), F32), sd((3, 4, 256, ff), BF), sd((4, 256, 512), BF),
+        sd((4, 256, 640), BF), sd((3, 3, 256, ff), BF), sd((3, 256, 512), BF), sd((3, 256, 640), BF),
+        sd((3, 2, 256, d), BF), sd((3, 2, 128, d), BF),
+    ]
+    toks = (2, 512, d)
+    scratch = [
+        v(toks, BF), v(toks, BF), v(toks, BF), v((2, 512, ff), BF), v((2, 512, ff), BF), v((3, 4, 256, ff), BF),
+        v((3, 256, ff), BF), v((256, ff), F32), v((2, 2, 4, 256, 256), BF), v((2, 2, 256, ff), BF),
+        v((2, 256, d), BF), v((2, 256, d), BF), v((2, 128, d), BF), v((2, 128, d), F32), v((2, 128, d), F32),
+        v((2, 128, d), F32), v((2, 512, 640), BF), v((2, 512, 512), BF), v((2, 512, 512), BF), v((2, 512, 640), BF),
+        v((2, 128, d), BF), v((512, 128), F32), v((512, 128), F32), v((8, d), F32), v((8, 1024), F32),
+        v((8, 1024), F32), v((3, 8, 256), F32), v((8, 256), F32), v((3, 8, 256), F32),
+        pltpu.SemaphoreType.DMA((64,)), pltpu.SemaphoreType.DMA((64,)), pltpu.SemaphoreType.DMA((32,)),
+        pltpu.SemaphoreType.DMA((2,)), pltpu.SemaphoreType.DMA((2, 2)), pltpu.SemaphoreType.DMA((3,)),
+        pltpu.SemaphoreType.DMA((1,)),
+    ]
+    return pl.pallas_call(
+        backward_kernel,
+        out_shape=out_shape,
+        in_specs=[VMEM] * 3 + [HBM] * (1 + len(arrays)),
+        out_specs=[HBM] * 2 + [VMEM] + [HBM] * 13,
+        scratch_shapes=scratch,
+        compiler_params=pltpu.CompilerParams(collective_id=1, has_side_effects=True, vmem_limit_bytes=LIMIT_B),
+    )(table, mask_t, gain, x, *arrays)
+
+
+def to_relative(a):
+    dp = lax.axis_index("dp")
+    z, x = dp // 2, dp % 2
+    lead = a.shape[:-1]
+    a = a.reshape(lead + (4, 2, -1))
+    a = jnp.where(x == 0, a, jnp.flip(a, -2))
+    a = lax.dynamic_slice_in_dim(jnp.concatenate([a, a], -3), z, 4, len(lead))
+    return jnp.swapaxes(a, -2, -3).reshape(lead + (-1,))
+
+def from_relative(a):
+    dp = lax.axis_index("dp")
+    z, x = dp // 2, dp % 2
+    lead = a.shape[:-1]
+    a = jnp.swapaxes(a.reshape(lead + (2, 4, -1)), -2, -3)
+    a = jnp.where(x == 0, a, jnp.flip(a, -2))
+    a = lax.dynamic_slice_in_dim(jnp.concatenate([a, a], -3), 4 - z, 4, len(lead))
+    return a.reshape(lead + (-1,))
+
+
+def per_device_grid(
+    inputs, segments, cotangent, attn_gain, w_query, w_key, w_value, w_out, mlp_gain, w_gate, w_up, w_down,
+):
+    rows = inputs.shape[1]
+    nq, nk = w_query.shape[1], w_key.shape[1]
+    w_qkv = jnp.concatenate([w_query, w_key, w_value], axis=1)
+    x = to_relative(inputs)
+    c = to_relative(cotangent)
+    me = lax.axis_index("seq")
+    order = [me, me ^ 2, me ^ 1, me ^ 3]
+    pos = jnp.concatenate([j * rows + jnp.arange(rows, dtype=jnp.int32) for j in order])
+    segs = jnp.concatenate([lax.dynamic_slice_in_dim(segments, j * rows, rows, 1) for j in order], axis=1)
+    cosine, sine = rope_tables(pos)
+    c4 = jnp.tile(cosine, (1, 4))
+    s4 = jnp.concatenate([-sine, sine, -sine, sine], axis=1)
+    one, zero = jnp.ones_like(c4[:, :64]), jnp.zeros_like(c4[:, :64])
+    table = jnp.stack(
+        [c4, s4, jnp.concatenate([c4[:, :64], one], axis=1), jnp.concatenate([s4[:, :64], zero], axis=1)]
+    )
+    same = segs[:, :, None] == segs[:, None, :]
+    mask = jnp.where((pos[None, :] <= pos[:, None])[None] & same, 0.0, NEGATIVE).astype(BF)
+    mask_t = jnp.where((pos[None, :] >= pos[:, None])[None] & same, 0.0, NEGATIVE).astype(BF)
+    size = attn_gain.shape[0]
+    g = jnp.zeros((8, 4, size), F32).at[:2, me].set(jnp.stack([attn_gain, mlp_gain]).astype(F32))
+    made = forward(x, c, g.reshape(8, 4 * size), table, mask, [w_qkv, w_out, w_gate, w_up, w_down])
+    c_full, wqkv, wo, wg, wu, wd, na, qkv, att, res, nm, gain, prod, fa, fb, down = made
+    arrays = [c_full, wqkv, wo, wg, wu, wd, na, qkv, att, res, nm, prod, fa, fb, down]
+    back = backward(table, mask_t, gain, x, arrays)
+    output, d_input, gains, gq, go, gg, gu, gd = back[:8]
+    gains = lax.dynamic_slice_in_dim(gains, me * size, size, 1)
+    return (
+        from_relative(output), from_relative(d_input), gains[0], gq[:, :nq], gq[:, nq : nq + nk], gq[:, nq + nk :],
+        go, gains[1], gg, gu, gd,
+    )
 
 
 class AnyMesh:
@@ -276,7 +902,7 @@
     length = rows * seq
     full = micro * length
     half = length // 2
-    grid = Mesh2D() if lax.axis_size("dp") == 8 else AnyMesh()
+    grid = AnyMesh()
 
     nq, nk = w_query.shape[1], w_key.shape[1]
     heads, kv_heads = nq // HD, nk // HD
@@ -389,8 +1015,9 @@
 
 def solution(mesh):
     tok, wt, gn = P(None, ("dp", "seq"), None), P("dp", "seq"), P(("dp", "seq"))
+    grid = mesh.shape["dp"] == 8 and mesh.shape["seq"] == 4
     return jax.shard_map(
-        per_device,
+        per_device_grid if grid else per_device,
         mesh=mesh,
         in_specs=(tok, P(None, "dp"), tok, gn, wt, wt, wt, wt, gn, wt, wt, wt),
         out_specs=(tok, tok, gn, wt, wt, wt, wt, gn, wt, wt, wt),

time: 987 us -> 723 us (0.73)
  Pallas kernels: 273 us -> 663 us
  waiting for transfers between devices: 283 us -> 0 us
  matrix products: 155 us -> 0 us
  starting transfers between devices: 136 us -> 0 us
  other arithmetic: 71.2 us -> 19.6 us
  local copies, waits for them, and re-layouts: 57.2 us -> 30.1 us
    pallas_call x1 -> x2, Pallas kernels: 273 us -> 663 us  [the longest x1 366 us: backward(): pl.pallas_call(backward_kernel, out_shape=out_shape, in_specs=[VMEM] * 3...]
    ppermute x52 -> x0, waiting for transfers between devices: 283 us -> none  [the longest x8 125 us: shift_x(): return lax.ppermute(a, 'dp', [(i, i ^ 1) for i in range(8)])]
    dot_general x31 -> x0, matrix products: 155 us -> none  [the longest x10 48.3 us: project_back(): lax.dot_general(a, b, (((1,), (1,)), ((), ())), preferred_element_type=F32)]
    ppermute x52 -> x0, starting transfers between devices: 136 us -> none  [the longest x24 118 us: shift_z(): return lax.ppermute(a, 'dp', [(i, (i + 2 * r) % 8) for i in range(8)])]
    add x20 -> x2, other arithmetic: 14.3 us -> 0.01 us  [per_device_grid(): j * rows + jnp.arange(rows, dtype=jnp.int32)]
    another operation x6 -> x4, other arithmetic: 16.7 us -> 4.01 us
    reduce_sum x5 -> x0, other arithmetic: 11.5 us -> none  [the longest x1 4.46 us: per_device(): denominator = jnp.sum(weights, axis=-1, keepdims=True)]
  transfers between devices with their start and end apart: 52 -> 0, of which waited for: 20 -> 0; matrix products, arithmetic and copies ran while one was open for 22% -> 0% of each run, Pallas kernels for 28% -> 0%
where the time goes in v3:
time: 723 us; the launch traced here: 714 us
  Pallas kernels  663 us (92%)
  local copies, waits for them, and re-layouts  30.1 us (4%)
  other arithmetic  19.6 us (3%)
    pallas_call x1, Pallas kernels, backward(): pl.pallas_call(backward_kernel, out_shape=out_shape, in_specs=[VMEM] * 3...  366 us
    pallas_call x1, Pallas kernels, forward(): pl.pallas_call(forward_kernel, out_shape=out_shape, in_specs=[HBM, HBM, V...  297 us

profile of v3, /device:TPU:0, one launch (start us, length us, event | category | flops | bytes accessed | tf_op | source)
XLA Modules:
  0.0 713.9 jit_solution(7011021516031153040)
XLA Ops:
  0.7 1.4 and_reduce_fusion
  2.1 1.3 broadcast_select_fusion.1
  3.4 0.7 constant_dynamic-slice_fusion.4
  4.9 0.9 copy.54
  5.8 0.9 copy.55
  6.7 1.8 pad_maximum_fusion.1.wqkv_s
  8.4 1.1 broadcast_compare_fusion
  9.5 1.0 multiply_cosine_fusion
  11.1 1.0 pad_maximum_fusion.table
  12.1 1.3 reshape.251
  14.7 0.8 reshape.253
  16.5 4.1 fusion.3
  20.7 1.6 reshape.254.c_ref
  22.3 1.6 reshape.252.x_ref
  23.8 2.1 select_convert_fusion
  25.9 296.7 %shard_map.203 = (bf16[2,512,2048]{2,1,0:T(8,128)(2,1)}, bf16[2,4,256,640]{3,2,1,0:T(8,128)(2,1)}, bf16[2,4,256,512]{3,2,1,0:T(8,128)(2,1)}, bf16[2,4,256,1408]{...) custom-call(bf16[2,128,2048]{2,1,0:T(8,128)(2,1)} %reshape.252.x_ref, ...), custom_call_target="tpu_custom_call" | custom-call | tf_op jit(solution)/shard_map/pallas_call | solution.py:424
  322.6 366.4 %shard_map.204 = (bf16[2,128,2048]{2,1,0:T(8,128)(2,1)}, f32[2,128,2048]{2,1,0:T(8,128)}, f32[8,256]{1,0:T(8,128)}, f32[256,640]{1,0:T(8,128)}, f32[256,512]{1,0...) custom-call(f32[4,512,128]{2,1,0:T(8,128)} %pad_maximum_fusion.table, ...), custom_call_target="tpu_custom_call" | custom-call | tf_op jit(solution)/shard_map/pallas_call | solution.py:788
  689.0 2.0 reshape.256
  691.6 1.9 fusion.1
  693.5 1.1 copy.56
  694.6 1.6 reshape.257
  696.9 0.9 slice.44
  697.8 0.7 copy.59
  699.2 2.7 reshape.258
  702.4 1.5 fusion
  703.9 1.1 copy.57
  705.0 2.7 reshape.259
  707.7 2.0 copy.65
  709.7 1.1 copy.66
  710.8 1.1 copy.67
  711.9 0.8 copy-done
  712.7 1.1 copy.68
  (40 shorter events, 6.1 us)
Async XLA Ops:
  0.6 10.1 %copy-start.8 = (pred[128]{0:T(512)(128)(4,1)S(1)}, pred[128]{0:T(512)(128)(4,1)}, u32[]{:S(2)}) copy-start(pred[128]{0:T(512)(128)(4,1)} %constant.88.clone.1) | copy-start | bytes 388
  10.6 1.5 copy-start.4
  13.4 1.2 copy-start.5
  20.7 3.2 copy-start.3
  693.5 2.7 copy-start.7
  693.5 3.3 copy-start.6
  705.0 4.7 copy-start.2
  707.7 3.1 copy-start.1
  710.8 1.9 copy-start

commit v4 on v3

--- a/solution.py
+++ b/solution.py
@@ -1,5 +1,6 @@
 import jax
 import jax.numpy as jnp
+import numpy as np
 from jax import lax
 from jax.experimental import pallas as pl
 from jax.experimental.pallas import tpu as pltpu
@@ -87,9 +88,12 @@
     def __init__(self, send, recv, local):
         self.send, self.recv, self.local = send, recv, local
         self.remote, self.own = [], []
-        self.seen, self.gone = set(), set()
+        self.seen, self.gone, self.middle_only = set(), set(), set()
         dp, sq = lax.axis_index("dp"), lax.axis_index("seq")
         self.dp, self.sq = dp, sq
+        height = lax.div(dp, 2)
+        self.middle = jnp.logical_and(height >= 1, height <= 2)
+        self.low = height <= 1
         self.z = [(lax.rem(dp + 2 * r, 8), sq) for r in range(4)]
         self.x = (dp + 1 - 2 * lax.rem(dp, 2), sq)
         core = sq + 1 - 2 * lax.rem(sq, 2)
@@ -102,19 +106,35 @@
             pl.semaphore_signal(barrier, inc=1, device_id=peer, device_id_type=MESH_ID)
         pl.semaphore_wait(barrier, len(peers))
 
-    def put(self, src, dst, peer):
+    def lanes(self, b):
+        z, x = lax.div(self.dp, 2), lax.rem(self.dp, 2)
+        at = lax.rem(z + b % 4, 4) * 2 + (x if b < 4 else 1 - x)
+        return pl.ds(pl.multiple_of(at * 256, 256), 256)
+
+    def order(self, k):
+        return (self.sq, self.y[1], self.core[1], self.both[1])[k]
+
+    def describe(self, src, dst, peer, landing=None):
         i = len(self.remote)
         copy = pltpu.make_async_remote_copy(
             src_ref=src,
             dst_ref=dst,
             send_sem=self.send.at[i],
-            recv_sem=self.recv.at[i],
+            recv_sem=self.recv.at[i if landing is None else landing],
             device_id=peer,
             device_id_type=MESH_ID,
         )
-        copy.start()
         self.remote.append(copy)
         return i
+
+    def put(self, src, dst, peer):
+        i = self.describe(src, dst, peer)
+        self.remote[i].start()
+        return i
+
+    def start_in_middle(self, i):
+        self.middle_only.add(i)
+        pl.when(self.middle)(self.remote[i].start)
 
     def arrived(self, *ids):
         for i in ids:
@@ -126,7 +146,10 @@
         for i in ids:
             if i not in self.gone:
                 self.gone.add(i)
-                self.remote[i].wait_send()
+                if i in self.middle_only:
+                    pl.when(self.middle)(self.remote[i].wait_send)
+                else:
+                    self.remote[i].wait_send()
 
     def keep(self, src, dst):
         copy = pltpu.make_async_copy(src, dst, self.local.at[len(self.own)])
@@ -146,6 +169,32 @@
         self.kept(*range(len(self.own)))
 
 
+def load_table(links, table_h, table):
+    return [
+        links.keep(
+            table_h.at[:, pl.ds(pl.multiple_of(links.order(k) * ROWS, ROWS), ROWS)],
+            table.at[:, pl.ds(k * ROWS, ROWS)],
+        )
+        for k in range(4)
+    ]
+
+
+def make_mask(links, seg, keys, mask, by_key):
+    for k in range(4):
+        at = pl.ds(k * ROWS, ROWS)
+        place = links.order(k) * ROWS
+        keys[0:2, at] = seg[:, pl.ds(pl.multiple_of(place, ROWS), ROWS)].astype(F32)
+        keys[2:3, at] = (lax.broadcasted_iota(jnp.int32, (1, ROWS), 1) + place).astype(F32)
+    columns = keys[...].T
+    for m in range(2):
+        for k in range(4):
+            at = slice(k * ROWS, (k + 1) * ROWS)
+            same = columns[at, m : m + 1] == keys[m : m + 1, :]
+            a, b = columns[at, 2:3], keys[2:3, :]
+            ahead = (a <= b) if by_key else (b <= a)
+            mask[m, at, :] = jnp.where(jnp.logical_and(same, ahead), 0.0, NEGATIVE).astype(BF)
+
+
 def rope_tile(t, cosine, sine):
     lane = lax.broadcasted_iota(jnp.int32, t.shape, 1)
     turned = jnp.where(lax.rem(lane, 64) < 32, pltpu.roll(t, 96, 1), pltpu.roll(t, 32, 1))
@@ -153,15 +202,16 @@
 
 
 def forward_kernel(
-    x_ref, c_ref, g_ref, table, mask, wqkv_s, wo_s, wg_s, wu_s, wd_s,
+    x_ref, c_ref, g_ref, seg, table_h, wqkv_s, wo_s, wg_s, wu_s, wd_s,
     c_full, wqkv_f, wo_f, wg_f, wu_f, wd_f, na_o, qkv_o, att_o, res_o, nm_o, gain_o, prod_o, fa_o, fb_o, down_o,
-    xf, nm, wqkv_v, wo_v, qkv, att, far, far_in, near, ysend, yin, own_x, gseq, gfull, gown, prod, fa, fb, wt, lbuf, gbuf,
+    xf, nm, wqkv_v, wo_v, qkv, att, far, far_in, near, ysend, yin, own_x, gseq, gfull, gown, prod, fa, fb, wt, lbuf, gbuf, table, mask, keys,
     send, recv, local, wsem, lsem, gsem,
 ):
     links = Links(send, recv, local)
     put, arrived = links.put, links.arrived
-    shards = [wqkv_s, wo_s, wg_s, wu_s, wd_s]
-    fulls = [wqkv_f, wo_f, wg_f, wu_f, wd_f]
+    first, rest = pl.ds(0, 768), pl.ds(768, wg_s.shape[1] - 768)
+    shards = [wqkv_s, wo_s] + [w.at[:, s] for s in (first, rest) for w in (wg_s, wu_s)] + [wd_s]
+    fulls = [wqkv_f, wo_f] + [w.at[:, :, :, s] for s in (first, rest) for w in (wg_f, wu_f)] + [wd_f]
 
     def part(full, k):
         return full.at[:, pl.ds(k * ROWS, ROWS)]
@@ -177,42 +227,71 @@
 
     def z_start(i):
         placed.append(links.keep(shards[i], fulls[i].at[0, 0]))
-        return [put(shards[i], fulls[i].at[0, r], links.z[4 - r]) for r in (1, 2, 3)]
+        return {r: put(shards[i], fulls[i].at[0, r], links.z[4 - r]) for r in (1, 3)}
 
     def x_own(i):
         return [put(shards[i], fulls[i].at[1, 0], links.x)]
 
-    def x_forward(i, copies, ids, order=(1, 3, 2)):
-        for r in order:
-            arrived(copies[r - 1])
-            ids.append(put(fulls[i].at[0, r], fulls[i].at[1, r], links.x))
-
-    xs = seq_start(x_ref, xf)
-    own0 = links.keep(x_ref, part(xf, 0))
-    own1 = links.keep(x_ref, own_x)
+    def x_near(i, copies, ids):
+        full = fulls[i]
+        relay = {1: links.describe(full.at[0, 1], full.at[0, 2], links.z[3])}
+        copies[2] = relay[1]
+        relay[3] = links.describe(full.at[0, 3], full.at[0, 2], links.z[1], relay[1])
+        links.seen.add(relay[3])
+        for r in (1, 3):
+            arrived(copies[r])
+            links.start_in_middle(relay[r])
+            ids.append(put(full.at[0, r], full.at[1, r], links.x))
+
+    def x_far(i, copies, ids):
+        arrived(copies[2])
+        ids.append(put(fulls[i].at[0, 2], fulls[i].at[1, 2], links.x))
+
+    placing = [links.keep(x_ref.at[:, :, links.lanes(b)], xf.at[:, pl.ds(0, ROWS), pl.ds(b * 256, 256)]) for b in range(8)]
+    c_own = [links.keep(c_ref.at[:, :, links.lanes(b)], c_full.at[:, pl.ds(0, ROWS), pl.ds(b * 256, 256)]) for b in range(8)]
+    table_in = load_table(links, table_h, table)
     gs = [put(g_ref, gseq.at[k], p) for k, p in ((1, links.core), (2, links.y), (3, links.both))]
-    z0 = z_start(0)
-    x0 = x_own(0)
+    zs, xd = {}, {}
+
+    def start(i):
+        zs[i] = z_start(i)
+
+    def across(i):
+        xd[i] = x_own(i)
+
+    def near_blocks(i):
+        x_near(i, zs[i], xd[i])
+
+    def far_block(i):
+        x_far(i, zs[i], xd[i])
+
+    start(0)
+    across(0)
+    links.kept(*placing)
+    xs = seq_start(part(xf, 0), xf)
+    own1 = links.keep(part(xf, 0), own_x)
     arrived(*gs)
     gown[...] = g_ref[...] + gseq[1] + gseq[2] + gseq[3]
     gfull[0, 0] = gown[...]
     gz = [put(gown, gfull.at[0, r], links.z[4 - r]) for r in (1, 2, 3)]
     gx = [put(gown, gfull.at[1, 0], links.x)]
-    z1 = z_start(1)
+    start(1)
+    near_blocks(0)
+    make_mask(links, seg, keys, mask, False)
+    links.kept(*table_in)
     for r in (1, 2, 3):
         arrived(gz[r - 1])
         gx.append(put(gfull.at[0, r], gfull.at[1, r], links.x))
+    far_block(0)
+    across(1)
+    start(2)
     seq_forward(xf, xs)
-    x_forward(0, z0, x0)
-    x1 = x_own(1)
     arrived(*gx)
     for b in range(8):
         gain_o[:, b * 256 : (b + 1) * 256] = gfull[b // 4, b % 4]
-    z2 = z_start(2)
-    x2 = x_own(2)
     arrived(*xs)
-    links.sent(xs[2])
-    links.kept(own0, own1)
+    links.sent(*xs)
+    links.kept(own1)
 
     @pl.loop(0, 16)
     def _(i):
@@ -222,8 +301,8 @@
         xf[m, pl.ds(r, 64), :] = (v * inverse * gain_o[0:1, :]).astype(BF)
 
     na_copy = links.keep(xf, na_o)
-    x_forward(1, z1, x1)
-    arrived(*x0)
+    near_blocks(1)
+    arrived(*xd[0])
     links.kept(placed[0])
     load0 = links.keep(wqkv_f, wqkv_v)
     links.kept(load0)
@@ -243,6 +322,10 @@
         qkv[m, rows, 512:640] = rope_tile(t, table[2, rows, :], table[3, rows, :]).astype(BF)
 
     links.keep(qkv, qkv_o)
+    far_block(1)
+    across(2)
+    start(3)
+    across(3)
 
     def attend(m):
         kv = qkv[m, :, 512:640].astype(F32)
@@ -267,10 +350,12 @@
             att[m, rows, lanes] = out.astype(BF)
 
     attend(0)
-    z3 = z_start(3)
+    near_blocks(2)
+    start(4)
     attend(1)
+    far_block(2)
     links.keep(att, att_o)
-    arrived(*x1)
+    arrived(*xd[1])
     links.kept(placed[1])
     load1 = links.keep(wo_f, wo_v)
     links.kept(load1)
@@ -285,6 +370,7 @@
     for m in range(2):
         out_rows(m, HALF, far, BF)
     fc = put(far, far_in, links.core)
+    near_blocks(3)
     for m in range(2):
         out_rows(m, 0, near, F32)
     arrived(fc)
@@ -296,9 +382,10 @@
         ysend[m, pl.ds(r, 64), :] = (near[m, rows, :] + far_in[m, rows, :].astype(F32)).astype(BF)
 
     yc = put(ysend, yin, links.y)
-    x_forward(2, z2, x2)
-    x3 = x_own(3)
-    z4 = z_start(4)
+    far_block(3)
+    across(4)
+    start(5)
+    across(5)
     arrived(yc)
 
     @pl.loop(0, 4)
@@ -311,16 +398,15 @@
         nm[m, rows, :] = (v * inverse * gain_o[1:2, :]).astype(BF)
 
     ns = seq_start(part(nm, 0), nm)
+    near_blocks(4)
+    far_block(4)
+    start(6)
     seq_forward(nm, ns)
-    cs = seq_start(c_ref, c_full)
-    c_own = links.keep(c_ref, part(c_full, 0))
-    x_forward(3, z3, x3)
-    x4 = x_own(4)
+    links.kept(*c_own)
+    cs = seq_start(part(c_full, 0), c_full)
     arrived(*ns)
     links.keep(nm, nm_o)
-    arrived(*x2)
-    seq_forward(c_full, cs)
-    arrived(*x3)
+    arrived(*xd[2], *xd[3])
     links.kept(placed[2], placed[3])
 
     def load(t, slot):
@@ -360,15 +446,22 @@
             c.wait()
         up_tile(t, slot)
 
-    pl.loop(0, 5)(tile_step)
-    arrived(z4[0])
-    x_forward(4, z4, x4)
-    pl.loop(5, tiles)(tile_step)
+    pl.loop(0, 3)(tile_step)
+    near_blocks(5)
+    far_block(5)
+    across(6)
+    pl.loop(3, 5)(tile_step)
+    near_blocks(6)
+    seq_forward(c_full, cs)
+    arrived(*xd[4], *xd[5])
+    links.kept(placed[4], placed[5])
+    pl.loop(5, 7)(tile_step)
+    far_block(6)
+    pl.loop(7, tiles)(tile_step)
     links.keep(prod, prod_o)
     links.keep(fa, fa_o)
     links.keep(fb, fb_o)
     arrived(*cs)
-    links.kept(c_own)
 
     def load_left(b, slot):
         lanes = pl.ds(pl.multiple_of(b * 256, 256), 256)
@@ -401,7 +494,7 @@
     links.finish()
 
 
-def forward(x, c, g, table, mask, shards):
+def forward(x, c, g, seg, table, shards):
     micro, rows, d = x.shape
     sd = jax.ShapeDtypeStruct
     toks = (micro, 4 * rows, d)
@@ -418,28 +511,29 @@
         v((2, 512, 512), BF), v((2, 256, d), BF), v((2, 256, d), BF), v((2, 256, d), F32), v((2, 128, d), BF),
         v((2, 128, d), BF), v((2, 128, d), BF), v((4, 8, 256), F32), v((2, 4, 8, 256), F32), v((8, 256), F32),
         v((2, 512, nf), BF), v((2, 512, nf), BF), v((2, 512, nf), BF), v((2, 2, 4, 256, 256), BF), v((2, 2, 512, 256), BF), v((2, 256, nf), BF),
-        pltpu.SemaphoreType.DMA((72,)), pltpu.SemaphoreType.DMA((72,)), pltpu.SemaphoreType.DMA((24,)),
+        v((4, 512, 128), F32), v((2, 512, 512), BF), v((8, 512), F32),
+        pltpu.SemaphoreType.DMA((96,)), pltpu.SemaphoreType.DMA((96,)), pltpu.SemaphoreType.DMA((56,)),
         pltpu.SemaphoreType.DMA((2, 2)), pltpu.SemaphoreType.DMA((2,)), pltpu.SemaphoreType.DMA((2,)),
     ]
     return pl.pallas_call(
         forward_kernel,
         out_shape=out_shape,
-        in_specs=[HBM, HBM, VMEM, VMEM, VMEM] + [HBM] * 5,
+        in_specs=[HBM, HBM, VMEM, VMEM, HBM] + [HBM] * 5,
         out_specs=[HBM] * 9 + [VMEM, HBM, VMEM] + [HBM] * 4,
         scratch_shapes=scratch,
         compiler_params=pltpu.CompilerParams(collective_id=0, has_side_effects=True, vmem_limit_bytes=LIMIT),
-    )(x, c, g, table, mask, *shards)
+    )(x, c, g, seg, table, *shards)
 
 
 ORDER = (2, 1, 3, 0)
 
 
 def backward_kernel(
-    table, mask_t, gain, x_ref, c_full, wqkv_f, wo_f, wg_f, wu_f, wd_f, na_h, qkv_h, att_h, res_h, nm_h, prod_h, fa_h,
+    seg, gain, table_h, x_ref, c_full, wqkv_f, wo_f, wg_f, wu_f, wd_f, na_h, qkv_h, att_h, res_h, nm_h, prod_h, fa_h,
     fb_h, down_h,
     out_o, din_o, gain_o, gq_o, go_o, gg_o, gu_o, gd_o, xin_f, xin_o, xin_q, zin_f, zin_o, zin_q, fin, yin,
     cot, nm, dr, dg, du, grads, stage, ostage, wcol, wrow, far, far_st, ysend, acc_m, acc_o, res, qkv, att, datt, dqkv,
-    obuf, dkacc, dvacc, gacc, gxin, gnear, gzin, gown, gsin,
+    obuf, dkacc, dvacc, gacc, gxin, gnear, gzin, gown, gsin, table, mask_t, keys,
     send, recv, local, csem, rsem, ssem, osem,
 ):
     links = Links(send, recv, local)
@@ -460,6 +554,7 @@
         "out": (dr, att, cut(0, 512), xin_o, zin_o, 512, go_o),
         "qkv": (cot, dqkv, cut(512, 640), xin_q, zin_q, 640, gq_o),
     }
+    relays = {}
     xid = {name: {} for name in spec}
     zid = {name: {} for name in spec}
 
@@ -494,23 +589,49 @@
         if name == "down":
             mine = stage[1].astype(F32)
         buffer(r)[...] = (mine + got[...].astype(F32)).astype(BF)
-        if r:
-            zid[name][r] = put(buffer(r), zland.at[r - 1], links.z[r])
+        if r == 2:
+            low = links.describe(buffer(2), zland.at[2], links.z[1])
+            high = links.describe(buffer(2), zland.at[3], links.z[3])
+            pl.when(links.low)(links.remote[low].start)
+            pl.when(jnp.logical_not(links.low))(links.remote[high].start)
+            links.seen.update((low, high))
+            links.gone.update((low, high))
+            relays[name] = (low, high)
+
+    def grad_on(name):
+        buffer, _, zland, width = spec[name][2:6]
+        got = stage.at[0, :, pl.ds(0, width)]
+        for k, r in enumerate((1, 3)):
+            copy = pltpu.make_async_copy(zland.at[2 + k], got, ssem.at[0])
+
+            @pl.when(links.middle)
+            def _():
+                links.remote[relays[name][k]].wait_recv()
+                copy.start()
+                copy.wait()
+                buffer(r)[...] = (buffer(r)[...].astype(F32) + got[...].astype(F32)).astype(BF)
+
+            zid[name][r] = put(buffer(r), zland.at[k], links.z[r])
+
+    def far_sent(name):
+        low, high = relays[name]
+        pl.when(links.low)(links.remote[low].wait_send)
+        pl.when(jnp.logical_not(links.low))(links.remote[high].wait_send)
 
     writing = []
 
     def grad_final(name):
         buffer, _, zland, width, result = spec[name][2:]
         copies = []
-        for r in (1, 2, 3):
+        for k, r in enumerate((1, 3)):
             arrived(zid[name][r])
-            copies.append(pltpu.make_async_copy(zland.at[r - 1], stage.at[r - 1, :, pl.ds(0, width)], ssem.at[r - 1]))
+            copies.append(pltpu.make_async_copy(zland.at[k], stage.at[k, :, pl.ds(0, width)], ssem.at[k]))
             copies[-1].start()
         for c in copies + writing:
             c.wait()
         lanes = slice(0, width)
         total = buffer(0)[...].astype(F32) + stage[0, :, lanes].astype(F32)
-        ostage[:, lanes] = total + stage[1, :, lanes].astype(F32) + stage[2, :, lanes].astype(F32)
+        ostage[:, lanes] = total + stage[1, :, lanes].astype(F32)
         writing[:] = [pltpu.make_async_copy(ostage.at[:, pl.ds(0, width)], result, osem.at[0])]
         writing[0].start()
 
@@ -590,6 +711,7 @@
     cot_in = keep(c_full, cot)
     ffn_in = [keep(fa_h, dg), keep(fb_h, du)]
     late = [keep(nm_h, nm), keep(res_h, res), keep(qkv_h, qkv), keep(att_h, att)]
+    late += load_table(links, table_h, table)
     gacc[...] = jnp.zeros_like(gacc)
 
     def load_col(t, slot):
@@ -632,15 +754,18 @@
     last.wait()
     product_rows(tiles % 2, rest, tiles * 256)
 
+    kept(*late)
+    grad_far("gate")
+    grad_near("down", 2)
     rows_near(0, out_terms, acc_o)
+    grad_near("down", 1)
     ffn_terms = [(dg, wg_f, ff), (du, wu_f, ff)]
     rows_far(1, ffn_terms)
-    kept(*late)
-    grad_far("gate")
+    grad_far("up")
+    grad_near("down", 3)
     rows_near(1, ffn_terms, acc_m)
-    grad_far("up")
-    grad_near("down", 2)
-    grad_near("down", 1)
+    grad_near("down", 0)
+    make_mask(links, seg, keys, mask_t, True)
     rows_final(0)
 
     def output_rows(m, rows):
@@ -648,8 +773,9 @@
         obuf[m, rows, :] = total.astype(BF)
 
     chunks(output_rows)
-    keep(obuf, out_o)
-    grad_near("down", 3)
+    for b in range(8):
+        keep(obuf.at[:, :, pl.ds(b * 256, 256)], out_o.at[:, :, links.lanes(b)])
+    grad_on("down")
     rows_final(1)
 
     def middle(m, rows):
@@ -663,7 +789,8 @@
     ds = [put(own, dr.at[:, pl.ds(ROWS, ROWS)], links.y), put(own, dr.at[:, pl.ds(2 * ROWS, ROWS)], links.core)]
     na_in = keep(na_h, cot)
     wo_in = [keep(wo_f.at[:, :, :, pl.ds(k * 256, 256)], wcol.at[k]) for k in range(2)]
-    grad_near("down", 0)
+    grad_near("gate", 2)
+    grad_near("gate", 1)
     arrived(ds[0])
     ds.append(put(dr.at[:, pl.ds(ROWS, ROWS)], dr.at[:, pl.ds(3 * ROWS, ROWS)], links.core))
     kept(*wo_in)
@@ -714,22 +841,25 @@
         dqkv[m, :, 512:640] = jnp.where(lane < 64, dk, dv).astype(BF)
 
     attend_back(0)
-    grad_near("gate", 2)
-    grad_near("gate", 1)
+    grad_near("gate", 3)
+    grad_near("gate", 0)
+    grad_on("gate")
     attend_back(1)
     na_terms = [(dqkv, wqkv_f, 640)]
     rows_far(2, na_terms)
     grad_final("down")
+    far_sent("down")
     sent(*zid["down"].values())
     kept(na_in)
     grad_far("out")
     grad_far("qkv")
     rows_near(2, na_terms, acc_o)
-    grad_near("gate", 3)
-    grad_near("gate", 0)
+    grad_near("up", 2)
+    grad_near("up", 1)
+    grad_near("up", 3)
     rows_final(2)
     own_x = far_st.at[:, pl.ds(ROWS, ROWS)]
-    kept(keep(x_ref, own_x))
+    kept(*[keep(x_ref.at[:, :, links.lanes(b)], own_x.at[:, :, pl.ds(b * 256, 256)]) for b in range(8)])
 
     def last_rows(m, rows):
         e = acc_o[m, rows, :] + far_st[m, rows, :].astype(F32)
@@ -737,32 +867,34 @@
         acc_m[m, rows, :] += norm_back(v, e, 0)
 
     chunks(last_rows)
-    keep(acc_m, din_o)
+    for b in range(8):
+        keep(acc_m.at[:, :, pl.ds(b * 256, 256)], din_o.at[:, :, links.lanes(b)])
     gx = put(gacc.at[:, pl.ds(1024, 1024)], gxin, links.x)
     arrived(gx)
     gnear[...] = gacc[:, 0:1024] + gxin[...]
     gz = [put(gnear.at[:, pl.ds(r * 256, 256)], gzin.at[r - 1], links.z[r]) for r in (1, 2, 3)]
-    grad_near("up", 2)
+    grad_near("up", 0)
+    grad_on("up")
     arrived(*gz)
     gown[...] = gnear[:, 0:256] + gzin[0] + gzin[1] + gzin[2]
     gs = [put(gown, gsin.at[k], p) for k, p in enumerate((links.core, links.y, links.both))]
-    grad_near("up", 1)
+    grad_final("gate")
     arrived(*gs)
     gain_o[...] = gown[...] + gsin[0] + gsin[1] + gsin[2]
-    grad_near("up", 3)
-    grad_final("gate")
-    grad_near("up", 0)
     for name in ("out", "qkv"):
         for r in ORDER:
             grad_near(name, r)
+        grad_on(name)
     for name in ("up", "out", "qkv"):
         grad_final(name)
     for c in writing:
         c.wait()
+    for name in ("gate", "up", "out", "qkv"):
+        far_sent(name)
     links.finish()
 
 
-def backward(table, mask_t, gain, x, arrays):
+def backward(seg, gain, table, x, arrays):
     micro, rows, d = x.shape
     sd = jax.ShapeDtypeStruct
     ff = arrays[-4].shape[2]
@@ -770,7 +902,7 @@
     out_shape = [
         sd(x.shape, BF), sd(x.shape, F32), sd((8, 256), F32), sd((256, 640), F32), sd((256, 512), F32),
         sd((256, ff), F32), sd((256, ff), F32), sd((256, ff), F32), sd((3, 4, 256, ff), BF), sd((4, 256, 512), BF),
-        sd((4, 256, 640), BF), sd((3, 3, 256, ff), BF), sd((3, 256, 512), BF), sd((3, 256, 640), BF),
+        sd((4, 256, 640), BF), sd((3, 4, 256, ff), BF), sd((4, 256, 512), BF), sd((4, 256, 640), BF),
         sd((3, 2, 256, d), BF), sd((3, 2, 128, d), BF),
     ]
     toks = (2, 512, d)
@@ -781,72 +913,52 @@
         v((2, 128, d), F32), v((2, 512, 640), BF), v((2, 512, 512), BF), v((2, 512, 512), BF), v((2, 512, 640), BF),
         v((2, 128, d), BF), v((512, 128), F32), v((512, 128), F32), v((8, d), F32), v((8, 1024), F32),
         v((8, 1024), F32), v((3, 8, 256), F32), v((8, 256), F32), v((3, 8, 256), F32),
-        pltpu.SemaphoreType.DMA((64,)), pltpu.SemaphoreType.DMA((64,)), pltpu.SemaphoreType.DMA((32,)),
+        v((4, 512, 128), F32), v((2, 512, 512), BF), v((8, 512), F32),
+        pltpu.SemaphoreType.DMA((80,)), pltpu.SemaphoreType.DMA((80,)), pltpu.SemaphoreType.DMA((64,)),
         pltpu.SemaphoreType.DMA((2,)), pltpu.SemaphoreType.DMA((2, 2)), pltpu.SemaphoreType.DMA((3,)),
         pltpu.SemaphoreType.DMA((1,)),
     ]
     return pl.pallas_call(
         backward_kernel,
         out_shape=out_shape,
-        in_specs=[VMEM] * 3 + [HBM] * (1 + len(arrays)),
+        in_specs=[VMEM] * 2 + [HBM] * (2 + len(arrays)),
         out_specs=[HBM] * 2 + [VMEM] + [HBM] * 13,
         scratch_shapes=scratch,
         compiler_params=pltpu.CompilerParams(collective_id=1, has_side_effects=True, vmem_limit_bytes=LIMIT_B),
-    )(table, mask_t, gain, x, *arrays)
-
-
-def to_relative(a):
-    dp = lax.axis_index("dp")
-    z, x = dp // 2, dp % 2
-    lead = a.shape[:-1]
-    a = a.reshape(lead + (4, 2, -1))
-    a = jnp.where(x == 0, a, jnp.flip(a, -2))
-    a = lax.dynamic_slice_in_dim(jnp.concatenate([a, a], -3), z, 4, len(lead))
-    return jnp.swapaxes(a, -2, -3).reshape(lead + (-1,))
-
-def from_relative(a):
-    dp = lax.axis_index("dp")
-    z, x = dp // 2, dp % 2
-    lead = a.shape[:-1]
-    a = jnp.swapaxes(a.reshape(lead + (2, 4, -1)), -2, -3)
-    a = jnp.where(x == 0, a, jnp.flip(a, -2))
-    a = lax.dynamic_slice_in_dim(jnp.concatenate([a, a], -3), 4 - z, 4, len(lead))
-    return a.reshape(lead + (-1,))
+    )(seg, gain, table, x, *arrays)
+
+
+def rope_table():
+    frequency = THETA ** (-(np.arange(HD // 2) * (2.0 / HD)))
+    angles = np.arange(LEN4)[:, None] * frequency[None, :]
+    cosine, sine = np.cos(angles), np.sin(angles)
+    c4 = np.tile(cosine, (1, 4))
+    s4 = np.concatenate([-sine, sine, -sine, sine], axis=1)
+    one, zero = np.ones((LEN4, HD)), np.zeros((LEN4, HD))
+    ck, sk = np.concatenate([c4[:, :HD], one], axis=1), np.concatenate([s4[:, :HD], zero], axis=1)
+    return np.stack([c4, s4, ck, sk]).astype(np.float32)
 
 
 def per_device_grid(
     inputs, segments, cotangent, attn_gain, w_query, w_key, w_value, w_out, mlp_gain, w_gate, w_up, w_down,
 ):
-    rows = inputs.shape[1]
     nq, nk = w_query.shape[1], w_key.shape[1]
     w_qkv = jnp.concatenate([w_query, w_key, w_value], axis=1)
-    x = to_relative(inputs)
-    c = to_relative(cotangent)
     me = lax.axis_index("seq")
-    order = [me, me ^ 2, me ^ 1, me ^ 3]
-    pos = jnp.concatenate([j * rows + jnp.arange(rows, dtype=jnp.int32) for j in order])
-    segs = jnp.concatenate([lax.dynamic_slice_in_dim(segments, j * rows, rows, 1) for j in order], axis=1)
-    cosine, sine = rope_tables(pos)
-    c4 = jnp.tile(cosine, (1, 4))
-    s4 = jnp.concatenate([-sine, sine, -sine, sine], axis=1)
-    one, zero = jnp.ones_like(c4[:, :64]), jnp.zeros_like(c4[:, :64])
-    table = jnp.stack(
-        [c4, s4, jnp.concatenate([c4[:, :64], one], axis=1), jnp.concatenate([s4[:, :64], zero], axis=1)]
-    )
-    same = segs[:, :, None] == segs[:, None, :]
-    mask = jnp.where((pos[None, :] <= pos[:, None])[None] & same, 0.0, NEGATIVE).astype(BF)
-    mask_t = jnp.where((pos[None, :] >= pos[:, None])[None] & same, 0.0, NEGATIVE).astype(BF)
     size = attn_gain.shape[0]
-    g = jnp.zeros((8, 4, size), F32).at[:2, me].set(jnp.stack([attn_gain, mlp_gain]).astype(F32))
-    made = forward(x, c, g.reshape(8, 4 * size), table, mask, [w_qkv, w_out, w_gate, w_up, w_down])
+    row = lax.broadcasted_iota(jnp.int32, (8, 4 * size), 0)
+    lane = lax.broadcasted_iota(jnp.int32, (8, 4 * size), 1)
+    g = jnp.where(row == 0, jnp.tile(attn_gain, 4)[None].astype(F32), jnp.tile(mlp_gain, 4)[None].astype(F32))
+    g = jnp.where(jnp.logical_and(row < 2, lane // size == me), g, 0.0)
+    table = jnp.asarray(rope_table())
+    made = forward(inputs, cotangent, g, segments, table, [w_qkv, w_out, w_gate, w_up, w_down])
     c_full, wqkv, wo, wg, wu, wd, na, qkv, att, res, nm, gain, prod, fa, fb, down = made
     arrays = [c_full, wqkv, wo, wg, wu, wd, na, qkv, att, res, nm, prod, fa, fb, down]
-    back = backward(table, mask_t, gain, x, arrays)
+    back = backward(segments, gain, table, inputs, arrays)
     output, d_input, gains, gq, go, gg, gu, gd = back[:8]
     gains = lax.dynamic_slice_in_dim(gains, me * size, size, 1)
     return (
-        from_relative(output), from_relative(d_input), gains[0], gq[:, :nq], gq[:, nq : nq + nk], gq[:, nq + nk :],
-        go, gains[1], gg, gu, gd,
+        output, d_input, gains[0], gq[:, :nq], gq[:, nq : nq + nk], gq[:, nq + nk :], go, gains[1], gg, gu, gd,
     )
 
 

time: 723 us -> 611 us (0.85)
  Pallas kernels: 663 us -> 579 us
  other arithmetic: 19.6 us -> 2.46 us
  local copies, waits for them, and re-layouts: 30.1 us -> 16.8 us
    pallas_call x1, Pallas kernels: 366 us -> 318 us  [backward(): pl.pallas_call(backward_kernel, out_shape=out_shape, in_specs=[VMEM] * 2...]
    pallas_call x1, Pallas kernels: 297 us -> 261 us  [forward(): pl.pallas_call(forward_kernel, out_shape=out_shape, in_specs=[HBM, HBM, V...]
    reshape x11 -> x0, local copies, waits for them, and re-layouts: 16 us -> none  [the longest x2 4.69 us: from_relative(): a = jnp.swapaxes(a.reshape(lead + (2, 4, -1)), -2, -3)]
where the time goes in v4:
time: 611 us; the launch traced here: 599 us
  Pallas kernels  579 us (95%)
  local copies, waits for them, and re-layouts  16.8 us (3%)
    pallas_call x1, Pallas kernels, backward(): pl.pallas_call(backward_kernel, out_shape=out_shape, in_specs=[VMEM] * 2...  318 us
    pallas_call x1, Pallas kernels, forward(): pl.pallas_call(forward_kernel, out_shape=out_shape, in_specs=[HBM, HBM, V...  261 us

profile of v4, /device:TPU:0, one launch (start us, length us, event | category | flops | bytes accessed | tf_op | source)
XLA Modules:
  0.0 599.0 jit_solution(2899802642569277321)
XLA Ops:
  0.7 0.7 tile.4
  1.3 0.1 convert_element_type.25
  1.4 0.7 tile.5
  2.1 0.1 convert_element_type.27
  2.2 0.7 select_select_fusion.g_ref
  2.8 0.9 copy.24
  3.7 0.9 copy.25
  4.6 1.8 pad_maximum_fusion.wqkv_s
  6.4 260.7 %shard_map.212 = (bf16[2,512,2048]{2,1,0:T(8,128)(2,1)}, bf16[2,4,256,640]{3,2,1,0:T(8,128)(2,1)}, bf16[2,4,256,512]{3,2,1,0:T(8,128)(2,1)}, bf16[2,4,256,1408]{...) custom-call(bf16[2,128,2048]{2,1,0:T(8,128)(2,1)} %x_ref.3, ...), custom_call_target="tpu_custom_call" | custom-call | tf_op jit(solution)/shard_map/pallas_call | solution.py:518
  267.1 318.1 %shard_map.213 = (bf16[2,128,2048]{2,1,0:T(8,128)(2,1)}, f32[2,128,2048]{2,1,0:T(8,128)}, f32[8,256]{1,0:T(8,128)}, f32[256,640]{1,0:T(8,128)}, f32[256,512]{1,0...) custom-call(s32[2,512]{1,0:T(2,128)} %seg.3, ...), custom_call_target="tpu_custom_call" | custom-call | tf_op jit(solution)/shard_map/pallas_call | solution.py:921
  585.2 0.0 copy-start
  585.2 0.9 constant_dynamic-slice_fusion
  586.1 0.5 slice_bitcast_fusion
  586.6 1.1 fusion.1
  587.7 1.9 slice.16
  589.6 0.7 copy.27
  590.3 0.7 copy.26
  591.0 0.0 copy-start.4
  591.0 2.4 copy.34
  593.3 0.0 copy-done
  593.4 0.0 copy-start.3
  593.4 1.3 copy.35
  594.7 0.0 copy-done.4
  594.7 0.0 copy-start.2
  594.7 0.8 copy.36
  595.5 0.0 copy-done.3
  595.5 0.0 copy-start.1
  595.5 1.1 copy.37
  596.6 0.0 copy-done.2
  596.6 1.1 copy.38
  597.7 0.0 copy-done.1
  597.7 1.1 copy.39
  (3 shorter events, 0.0 us)
Async XLA Ops:
  585.2 8.2 %copy-start = (f32[2,128,2048]{2,1,0:T(8,128)S(1)}, f32[2,128,2048]{2,1,0:T(8,128)}, u32[]{:S(2)}) copy-start(f32[2,128,2048]{2,1,0:T(8,128)} %get-tuple-element.90) | copy-start | bytes 6291460
  591.0 3.7 copy-start.4
  593.4 2.1 copy-start.3
  594.7 1.9 copy-start.2
  595.5 2.2 copy-start.1
